TPU v7x, 32 devices: a whole 2x2x4 slice. The times are simulated.
32 devices in a mesh: job: 2 (over x), tok: 16 (over z, y, core).
Axes of the slice: x: 2, y: 2, z: 4, core: 2. Of those that a mesh axis runs over, the one named last changes fastest.
Arguments:
- pair_states: bfloat16 [1024, 512, 128], P(('job', 'tok')), parts along dimension 0, may hold values from -6 to 6
- weight_in: bfloat16 [128, 1024], replicated, may hold values from -0.5 to 0.5
- weight_out: bfloat16 [512, 128], replicated, may hold values from -0.25 to 0.25
- weight_bias: bfloat16 [2, 128, 16], replicated, may hold values from -0.5 to 0.5
- key_mask: int32 [1024], P('job'), parts along dimension 0, may hold values 0 or 1
- noise_level: int32 [4], P('job'), parts along dimension 0, may hold values from 0 to 199
- query_states: bfloat16 [2, 16, 4, 48, 512], P(None, 'tok', 'job'), parts along dimension 2, may hold values from -16 to 16
- key_states: bfloat16 [2, 16, 4, 48, 512], P(None, 'tok', 'job'), parts along dimension 2, may hold values from -16 to 16
- value_states: bfloat16 [2, 16, 4, 48, 512], P(None, 'tok', 'job'), parts along dimension 2, may hold values from -6 to 6
- output_grad: bfloat16 [2, 16, 4, 48, 512], P(None, 'tok', 'job'), parts along dimension 2, may hold values from -6 to 6
Outputs:
- pair_grad: bfloat16 [1024, 512, 128], P(('job', 'tok')), parts along dimension 0
- query_grad: bfloat16 [2, 16, 4, 48, 512], P(None, 'tok', 'job'), parts along dimension 2
- key_grad: bfloat16 [2, 16, 4, 48, 512], P(None, 'tok', 'job'), parts along dimension 2
- value_grad: bfloat16 [2, 16, 4, 48, 512], P(None, 'tok', 'job'), parts along dimension 2
- weight_in_grad: float32 [256, 1024], P('job'), parts along dimension 0
- weight_out_grad: float32 [1024, 128], P('job'), parts along dimension 0
- weight_bias_grad: float32 [4, 128, 16], P('job'), parts along dimension 0
There are 2 independent parts, one for each index of `job`. A program takes and returns all parts, laid end to end along the dimension named above; an argument that names none is the same for every part. Nothing has to cross between parts.
All inputs are finite; a program needn't handle non-finite values.
Results may differ from a plain program's by a relative error of at most 0.015.
Values may be sent and summed in bfloat16 or wider, within the bound.
No kernel may reach another device: no remote copies, remote signals or barrier semaphores. Data moves between devices by JAX's collectives and lax.ppermute only.
A program may use at most 192 MiB of HBM per device.

v0:
```python
import functools
import math

import jax
import jax.numpy as jnp
from jax import lax
from jax.experimental import pallas as pl
from jax.experimental.pallas import tpu as pltpu
from jax.sharding import PartitionSpec as P

LEVELS = 200
CHUNKS = 1


sigma_high = 160.0
sigma_low = 0.0004
sigma_data = 16.0
rho_power = 7.0
epsilon = 1e-05
masked_score = -1000000000.0

F32 = jnp.float32
BF16 = jnp.bfloat16


def sample_weight(levels):
    level = levels.astype(jnp.float32)
    top_root = sigma_high ** (1.0 / rho_power)
    low_root = sigma_low ** (1.0 / rho_power)
    sigma_level = (top_root + level / (LEVELS - 1) * (low_root - top_root)) ** rho_power
    return (sigma_level * sigma_level + sigma_data * sigma_data) / (sigma_level + sigma_data) ** 2


def mm(left, right, left_dim=1, right_dim=0):
    return lax.dot_general(
        left, right, (((left_dim,), (right_dim,)), ((), ())), preferred_element_type=F32
    )


def normalize(inputs):
    centered = inputs - jnp.mean(inputs, -1, keepdims=True)
    inv_std = lax.rsqrt(jnp.mean(centered * centered, -1, keepdims=True) + epsilon)
    return centered * inv_std, inv_std


def norm_back(normed, inv_std, upstream):
    return inv_std * (
        upstream
        - jnp.mean(upstream, -1, keepdims=True)
        - normed * jnp.mean(upstream * normed, -1, keepdims=True)
    )


def split_width(width):
    return 256 if width % 256 == 0 else width


def forward_kernel(pair_ref, w_in_ref, w_out_ref, w_bias_ref, bias_ref):
    width = w_out_ref.shape[0]
    piece = split_width(width)

    def one_row(row, carry):
        pair_float = pair_ref[row].astype(F32)
        normed_in = normalize(pair_float)[0].astype(BF16)
        lifted = pair_float
        for at in range(0, width, piece):
            half_gate = mm(normed_in, w_in_ref[:, at : at + piece])
            up_in = mm(normed_in, w_in_ref[:, width + at : width + at + piece])
            hidden = (half_gate * (1.0 + jnp.tanh(half_gate)) * up_in).astype(BF16)
            lifted = lifted + mm(hidden, w_out_ref[at : at + piece, :])
        normed_out = normalize(lifted)[0].astype(BF16)
        bias_ref[row] = mm(w_bias_ref[...], normed_out, 1, 1).astype(BF16)
        return carry

    lax.fori_loop(0, pair_ref.shape[0], one_row, 0)


def forward_rows(chunk, rows, pair, w_in_half, w_out, w_bias):
    crop, channels = pair.shape[1:]
    lanes = w_bias.shape[0]
    step = math.gcd(rows, 4)
    steps = rows // step
    positions = rows * crop
    width = w_out.shape[0]
    whole = lambda i: (0, 0)
    return pl.pallas_call(
        forward_kernel,
        grid=(steps,),
        in_specs=[
            pl.BlockSpec((step, crop, channels), lambda i: (chunk * steps + i, 0, 0)),
            pl.BlockSpec(w_in_half.shape, whole),
            pl.BlockSpec(w_out.shape, whole),
            pl.BlockSpec(w_bias.shape, whole),
        ],
        out_specs=pl.BlockSpec((step, lanes, crop), lambda i: (i, 0, 0)),
        out_shape=jax.ShapeDtypeStruct((rows, lanes, crop), BF16),
        compiler_params=pltpu.CompilerParams(vmem_limit_bytes=40 * 2**20),
        cost_estimate=pl.CostEstimate(
            flops=2 * positions * channels * (3 * width + lanes),
            bytes_accessed=positions * (channels + lanes) * 2,
            transcendentals=positions * width,
        ),
        name="pair_forward",
    )(pair, w_in_half, w_out, w_bias)


def backward_kernel(
    first,
    last,
    pair_ref,
    d_bias_ref,
    w_in_ref,
    w_out_ref,
    w_bias_ref,
    w_in_t_ref,
    w_out_t_ref,
    *refs,
):
    if first:
        pair_grad_ref, sums_ref, bias_sums_ref = refs[:3]
    else:
        before_ref, bias_before_ref, _, pair_grad_ref, sums_ref, bias_sums_ref = refs[:6]
    width = w_out_ref.shape[0]
    channels = w_out_ref.shape[1]
    piece = split_width(width)

    @pl.when(pl.program_id(0) == 0)
    def _():
        if first:
            sums_ref[...] = jnp.zeros_like(sums_ref)
            bias_sums_ref[...] = jnp.zeros_like(bias_sums_ref)
        else:
            sums_ref[...] = before_ref[...]
            bias_sums_ref[...] = bias_before_ref[...]

    def one_row(row, carry):
        pair_float = pair_ref[row].astype(F32)
        normed_float, inv_in = normalize(pair_float)
        normed_in = normed_float.astype(BF16)
        lifted = pair_float
        kept = []
        for at in range(0, width, piece):
            half_gate = mm(normed_in, w_in_ref[:, at : at + piece])
            up_in = mm(normed_in, w_in_ref[:, width + at : width + at + piece])
            one_plus = 1.0 + jnp.tanh(half_gate)
            silu = half_gate * one_plus
            hidden = (silu * up_in).astype(BF16)
            slope = one_plus * (1.0 + half_gate * (2.0 - one_plus)) * up_in
            kept.append((silu, slope, hidden))
            lifted = lifted + mm(hidden, w_out_ref[at : at + piece, :])
        out_float, inv_out = normalize(lifted)
        normed_out = out_float.astype(BF16)
        d_bias = d_bias_ref[row]
        bias_sums_ref[...] += mm(d_bias, normed_out)
        d_normed = mm(d_bias, w_bias_ref[...], 0, 0)
        d_lifted = norm_back(out_float, inv_out, d_normed)
        lifted_half = d_lifted.astype(BF16)
        lifted_t = lifted_half.T
        normed_t = normed_in.T
        d_normed_in = jnp.zeros_like(pair_float)
        for index, (silu, slope, hidden) in enumerate(kept):
            at = index * piece
            cols = slice(at, at + piece)
            up_cols = slice(width + at, width + at + piece)
            out_cols = slice(2 * width + at, 2 * width + at + piece)
            sums_ref[:, out_cols] += mm(lifted_t, hidden)
            d_hidden = mm(lifted_half, w_out_t_ref[:, cols])
            d_gate = (0.5 * d_hidden * slope).astype(BF16)
            d_up = (d_hidden * silu).astype(BF16)
            sums_ref[:, cols] += mm(normed_t, d_gate)
            sums_ref[:, up_cols] += mm(normed_t, d_up)
            d_normed_in = d_normed_in + mm(d_gate, w_in_t_ref[cols, :])
            d_normed_in = d_normed_in + mm(d_up, w_in_t_ref[up_cols, :])
        pair_grad_ref[row] = (
            d_lifted + norm_back(normed_float, inv_in, d_normed_in)
        ).astype(BF16)
        return carry

    lax.fori_loop(0, pair_ref.shape[0], one_row, 0)

    if last:
        packed_ref = refs[-1]

        @pl.when(pl.program_id(0) == pl.num_programs(0) - 1)
        def _():
            done = 3 * width
            lanes = bias_sums_ref.shape[0]
            packed_ref[:, :done] = sums_ref[...].astype(BF16)
            padded = jnp.concatenate(
                [bias_sums_ref[...], jnp.zeros((channels - lanes, channels), F32)], 0
            )
            packed_ref[:, done:] = padded.T.astype(BF16)


def backward_rows(chunk, chunks, rows, pair, d_bias, weights, state):
    w_in_half, w_out, w_bias, w_in_t, w_out_t = weights
    crop, channels = pair.shape[1:]
    lanes = w_bias.shape[0]
    width = w_out.shape[0]
    step = math.gcd(rows, 4)
    steps = rows // step
    positions = rows * crop
    first, last = chunk == 0, chunk == chunks - 1
    whole = lambda i: (0, 0)
    pair_spec = pl.BlockSpec((step, crop, channels), lambda i: (chunk * steps + i, 0, 0))
    in_specs = [pair_spec, pl.BlockSpec((step, lanes, crop), lambda i: (i, 0, 0))]
    in_specs += [pl.BlockSpec(w.shape, whole) for w in weights]
    operands = [pair, d_bias, *weights]
    aliases = {}
    if not first:
        pair_grad, sums, bias_sums = state
        operands += [sums, bias_sums, pair_grad]
        in_specs += [pl.BlockSpec(sums.shape, whole), pl.BlockSpec(bias_sums.shape, whole)]
        in_specs += [pl.BlockSpec(memory_space=pl.ANY)]
        aliases = {len(operands) - 1: 0}
    shapes = [
        jax.ShapeDtypeStruct(pair.shape, BF16),
        jax.ShapeDtypeStruct((channels, 3 * width), F32),
        jax.ShapeDtypeStruct((lanes, channels), F32),
    ]
    out_specs = [pair_spec, pl.BlockSpec(shapes[1].shape, whole), pl.BlockSpec(shapes[2].shape, whole)]
    if last:
        shapes.append(jax.ShapeDtypeStruct((channels, 3 * width + channels), BF16))
        out_specs.append(pl.BlockSpec(shapes[3].shape, whole))
    return pl.pallas_call(
        functools.partial(backward_kernel, first, last),
        grid=(steps,),
        in_specs=in_specs,
        out_specs=out_specs,
        out_shape=shapes,
        input_output_aliases=aliases,
        compiler_params=pltpu.CompilerParams(vmem_limit_bytes=48 * 2**20),
        cost_estimate=pl.CostEstimate(
            flops=2 * positions * channels * (9 * width + 2 * lanes),
            bytes_accessed=positions * (2 * channels + lanes) * 2,
            transcendentals=positions * width,
        ),
        name="pair_backward",
    )(*operands)


def attend_kernel(
    first, last, weight_ref, bias_ref, valid_ref, q_ref, k_ref, v_ref, g_ref, *refs
):
    if first:
        dq_ref, dk_ref, dv_ref, d_bias_ref = refs
    else:
        dk_before_ref, dv_before_ref, dq_ref, dk_ref, dv_ref, d_bias_ref = refs
    samples, depth = q_ref.shape[1:3]
    sources, _, rows, crop = bias_ref.shape
    scaling = 1.0 / math.sqrt(depth)
    bias = bias_ref[:, 0].astype(F32).reshape(sources * rows, crop)
    valid = valid_ref[...] > 0
    total = jnp.zeros_like(bias)
    for s in range(samples):
        query, key, value = q_ref[0, s], k_ref[0, s], v_ref[0, s]
        grad_half = (weight_ref[s] * g_ref[0, s].astype(F32)).astype(BF16)
        scores = mm(query, key, 0, 0) * scaling + bias
        scores = jnp.where(valid, scores, masked_score)
        exp_scores = jnp.exp(scores - jnp.max(scores, -1, keepdims=True))
        attention = exp_scores / jnp.sum(exp_scores, -1, keepdims=True)
        d_attention = mm(grad_half, value, 0, 0)
        d_scores = attention * (
            d_attention - jnp.sum(attention * d_attention, -1, keepdims=True)
        )
        total = total + d_scores
        scores_half = d_scores.astype(BF16)
        d_value = mm(grad_half, attention.astype(BF16))
        d_key = mm(query, scores_half)
        dq_ref[0, s] = (mm(key, scores_half, 1, 1) * scaling).astype(BF16)
        if not first:
            d_value = d_value + dv_before_ref[0, s]
            d_key = d_key + dk_before_ref[0, s]
        if last:
            d_key = d_key * scaling
        dv_ref[0, s] = d_value.astype(dv_ref.dtype)
        dk_ref[0, s] = d_key.astype(dk_ref.dtype)
    d_bias_ref[:, 0] = total.astype(BF16).reshape(sources, rows, crop)


def attend_rows(chunk, chunks, weights, bias, valid, query, key, value, grad, state):
    sources, layers, rows, crop = bias.shape
    samples, depth, row_count = query.shape[1:]
    first, last = chunk == 0, chunk == chunks - 1
    vec = lambda shape: pl.BlockSpec((1,) + shape[1:], lambda l: (l, 0, 0, 0))
    plane = pl.BlockSpec((sources, 1, rows, crop), lambda l: (0, l, 0, 0))
    in_specs = [
        pl.BlockSpec(memory_space=pltpu.SMEM),
        plane,
        pl.BlockSpec(valid.shape, lambda l: (0, 0)),
        vec(query.shape),
        vec(key.shape),
        vec(value.shape),
        vec(grad.shape),
    ]
    operands = [weights, bias, valid, query, key, value, grad]
    if not first:
        operands += list(state)
        in_specs += [vec(key.shape), vec(value.shape)]
    kind = BF16 if last else F32
    return pl.pallas_call(
        functools.partial(attend_kernel, first, last),
        grid=(layers,),
        in_specs=in_specs,
        out_specs=[vec(query.shape), vec(key.shape), vec(value.shape), plane],
        out_shape=[
            jax.ShapeDtypeStruct(query.shape, BF16),
            jax.ShapeDtypeStruct(key.shape, kind),
            jax.ShapeDtypeStruct(value.shape, kind),
            jax.ShapeDtypeStruct(bias.shape, BF16),
        ],
        compiler_params=pltpu.CompilerParams(vmem_limit_bytes=48 * 2**20),
        cost_estimate=pl.CostEstimate(
            flops=10 * layers * samples * depth * row_count * crop,
            bytes_accessed=layers * crop * (4 * row_count + 12 * samples * depth),
            transcendentals=layers * samples * row_count * crop,
        ),
        name="attention_backward",
    )(*operands)


def swap(array):
    return lax.all_to_all(array, "tok", split_axis=0, concat_axis=0, tiled=True)


def body(
    pair_states,
    weight_in,
    weight_out,
    weight_bias,
    key_mask,
    noise_level,
    query_states,
    key_states,
    value_states,
    output_grad,
):
    row_count, crop, channels = pair_states.shape
    layers, _, heads = weight_bias.shape
    width = weight_out.shape[0]
    devices = lax.axis_size("tok")
    groups = devices // heads
    samples, depth = query_states.shape[2:4]
    chunks = CHUNKS
    rows = row_count // chunks
    lanes = heads * layers

    halves = jnp.concatenate([jnp.full((width,), 0.5, BF16), jnp.ones((width,), BF16)])
    w_in_half = weight_in * halves[None, :]
    w_bias = jnp.transpose(weight_bias, (2, 0, 1)).reshape(lanes, channels)
    pair_weights = (w_in_half, weight_out, w_bias, weight_in.T, weight_out.T)

    group = lax.axis_index("tok") // heads
    weights = sample_weight(lax.dynamic_slice_in_dim(noise_level, group * samples, samples))
    valid = key_mask[None, :]

    def by_chunk(array):
        cut = array[:, 0].reshape(layers, samples, depth, devices, chunks, rows)
        cut = jnp.transpose(cut, (4, 0, 1, 2, 3, 5))
        return cut.reshape(chunks, layers, samples, depth, devices * rows)

    queries, grads = by_chunk(query_states), by_chunk(output_grad)

    arrived = []
    for chunk in range(chunks):
        bias = forward_rows(chunk, rows, pair_states, w_in_half, weight_out, w_bias)
        bias = jnp.transpose(bias, (1, 0, 2)).reshape(heads, layers, rows, crop)
        arrived.append(swap(jnp.tile(bias, (groups, 1, 1, 1))))

    returned = []
    d_queries = []
    state = None
    for chunk in range(chunks):
        bias = arrived[chunk]
        flat = rows % 16 != 0
        if flat:
            bias = jnp.transpose(bias, (1, 0, 2, 3)).reshape(1, layers, devices * rows, crop)
        d_query, d_key, d_value, d_bias = attend_rows(
            chunk,
            chunks,
            weights,
            bias,
            valid,
            queries[chunk],
            key_states[:, 0],
            value_states[:, 0],
            grads[chunk],
            state,
        )
        state = (d_key, d_value)
        d_queries.append(d_query)
        if flat:
            d_bias = jnp.transpose(d_bias.reshape(layers, devices, rows, crop), (1, 0, 2, 3))
        returned.append(swap(d_bias))

    pair_state = None
    for chunk in range(chunks):
        d_bias = returned[chunk]
        if groups > 1:
            d_bias = d_bias.reshape(groups, heads, layers, rows, crop).astype(F32)
            d_bias = jnp.sum(d_bias, 0).astype(BF16)
        d_bias = jnp.transpose(d_bias.reshape(lanes, rows, crop), (1, 0, 2))
        pair_state = backward_rows(
            chunk, chunks, rows, pair_states, d_bias, pair_weights, pair_state and pair_state[:3]
        )
    pair_grad, _, _, packed = pair_state

    share = channels // devices
    parts = swap(packed.reshape(devices, share, packed.shape[1]))
    summed = jnp.sum(parts.astype(F32), 0).astype(BF16)
    summed = lax.all_gather(summed, "tok", axis=0, tiled=True).astype(F32)
    grad_in = summed[:, : 2 * width]
    grad_out = summed[:, 2 * width : 3 * width].T
    grad_bias = summed[:, 3 * width : 3 * width + lanes].reshape(channels, heads, layers)
    grad_bias = jnp.transpose(grad_bias, (2, 0, 1))

    d_query = jnp.stack(d_queries, 0).reshape(chunks, layers, samples, depth, devices, rows)
    d_query = jnp.transpose(d_query, (1, 2, 3, 4, 0, 5)).reshape(query_states.shape)
    return (
        pair_grad,
        d_query,
        d_key[:, None],
        d_value[:, None],
        grad_in,
        grad_out,
        grad_bias,
    )


def solution(mesh):
    in_specs = (
        P(("job", "tok"), None, None),
        P(),
        P(),
        P(),
        P("job"),
        P("job"),
        P(None, "tok", "job", None, None),
        P(None, "tok", "job", None, None),
        P(None, "tok", "job", None, None),
        P(None, "tok", "job", None, None),
    )
    out_specs = (
        P(("job", "tok"), None, None),
        P(None, "tok", "job", None, None),
        P(None, "tok", "job", None, None),
        P(None, "tok", "job", None, None),
        P("job", None),
        P("job", None),
        P("job", None, None),
    )
    return jax.shard_map(body, mesh=mesh, in_specs=in_specs, out_specs=out_specs, check_vma=False)
```

profile of v0, /device:TPU:0, one launch (start us, length us, event | category | flops | bytes accessed | tf_op | source)
XLA Modules:
  0.0 249.7 jit_solution(16276103391869938381)
XLA Ops:
  0.6 0.7 copy.36
  1.3 1.0 broadcast_multiply_fusion.w_in_ref
  2.3 0.0 copy-start
  2.3 0.9 copy-done
  3.2 2.2 copy-done.2
  5.4 41.2 %pair_forward.1 = bf16[32,32,512]{2,1,0:T(8,128)(2,1)S(1)} custom-call(bf16[32,512,128]{2,1,0:T(8,128)(2,1)S(1)} %copy-done.2, bf16[128,1024]{1,0:T(8,128)(2,1)S(1)} %broadcast_multiply_fusion.w_in_ref, bf16[512,128]{1,0:T(8,128)(2,1)S(1)} %copy-done, bf16[32,128]{1,0:T(8,128)(2,1)S(1)} %bitcast.35), custom_call_target="tpu_custom_call" | custom-call | flops 6576668672 | bytes 5242880 | tf_op jit(solution)/shard_map/pair_forward/pallas_call | solution.py:86
  46.6 0.0 copy-start.3
  46.6 0.0 copy-start.4
  46.7 0.0 copy-start.5
  46.7 0.0 copy-start.6
  46.7 0.0 copy-start.7
  46.7 0.0 copy-start.1
  46.7 0.0 copy-start.8
  46.7 1.5 copy.37
  48.3 7.4 %all-to-all-start = ((bf16[16,2,32,512]{3,2,1,0:T(8,128)(2,1)}), bf16[16,2,32,512]{3,2,1,0:T(8,128)(2,1)S(1)}, u32[]{:S(2)}, u32[]{:S(2)}) async-start(bf16[16,2,32,512]{3,2,1,0:T(8,128)(2,1)} %bitcast.3), calls=%async_computation | async-start | bytes 2097152 | tf_op jit(solution)/shard_map/all_to_all | solution.py:323
  55.7 0.0 copy-done.9
  55.7 22.9 %all-to-all-done.bias_ref = bf16[16,2,32,512]{3,2,1,0:T(8,128)(2,1)S(1)} async-done(((bf16[16,2,32,512]{3,2,1,0:T(8,128)(2,1)}), bf16[16,2,32,512]{3,2,1,0:T(8,128)(2,1)S(1)}, u32[]{:S(2)}, u32[]{:S(2)}) %all-to-all-start) | async-done | bytes 1048608 | tf_op jit(solution)/shard_map/all_to_all | solution.py:323
  78.6 5.7 %attention_backward.1 = (bf16[2,2,48,512]{3,2,1,0:T(8,128)(2,1)}, bf16[2,2,48,512]{3,2,1,0:T(8,128)(2,1)}, bf16[2,2,48,512]{3,2,1,0:T(8,128)(2,1)}, bf16[16,2,32,512]{3,2,1,0:T(8,128)(2,1)}) custom-call(f32[2]{0:T(128)S(1)} %multiply_divide_fusion.weight_ref, bf16[16,2,32,512]{3,2,1,0:T(8,128)(2,1)S(1)} %all-to-all-done.bias_ref, s32[1,512]{1,0:T(1,128)S(1)} %bitcast.41, ...), custom_call_target="tpu_custom_call" | custom-call | flops 503316480 | bytes 3276800 | tf_op jit(solution)/shard_map/attention_backward/pallas_call | solution.py:301
  84.3 6.9 %all-to-all-start.1 = ((bf16[16,2,32,512]{3,2,1,0:T(8,128)(2,1)}), bf16[16,2,32,512]{3,2,1,0:T(8,128)(2,1)S(1)}, u32[]{:S(2)}, u32[]{:S(2)}) async-start(bf16[16,2,32,512]{3,2,1,0:T(8,128)(2,1)} %get-tuple-element.13), calls=%async_computation.1 | async-start | bytes 2097152 | tf_op jit(solution)/shard_map/all_to_all | solution.py:323
  91.2 0.1 copy.40
  91.3 0.2 copy.39
  91.5 22.6 %all-to-all-done.1 = bf16[16,2,32,512]{3,2,1,0:T(8,128)(2,1)S(1)} async-done(((bf16[16,2,32,512]{3,2,1,0:T(8,128)(2,1)}), bf16[16,2,32,512]{3,2,1,0:T(8,128)(2,1)S(1)}, u32[]{:S(2)}, u32[]{:S(2)}) %all-to-all-start.1) | async-done | bytes 1048608 | tf_op jit(solution)/shard_map/all_to_all | solution.py:323
  114.1 0.6 copy.49
  114.7 92.3 %pair_backward.1 = (bf16[32,512,128]{2,1,0:T(8,128)(2,1)}, f32[128,1536]{1,0:T(8,128)}, f32[32,128]{1,0:T(8,128)}, bf16[128,1664]{1,0:T(8,128)(2,1)S(1)}) custom-call(bf16[32,512,128]{2,1,0:T(8,128)(2,1)} %pair_ref.3, bf16[32,32,512]{2,1,0:T(8,128)(2,1)S(1)} %bitcast.30, bf16[128,1024]{1,0:T(8,128)(2,1)S(1)} %broadcast_multiply_fusion.w_in_ref, ...), custom_call_target="tpu_custom_call" | custom-call | flops 19595788288 | bytes 9437184 | tf_op jit(solution)/shard_map/pair_backward/pallas_call | solution.py:225
  207.0 19.4 %all_to_all.15 = bf16[16,8,1664]{2,1,0:T(8,128)(2,1)S(1)} all-to-all(bf16[16,8,1664]{2,1,0:T(8,128)(2,1)S(1)} %bitcast.32), channel_id=1, replica_groups=mesh['job'=2,'tok'=16] {'tok'}, dimensions={0} | all-to-all | bytes 851968 | tf_op jit(solution)/shard_map/all_to_all | solution.py:323
  226.3 0.1 reduce_sum.12
  226.4 20.6 %all_gather.3 = bf16[128,1664]{1,0:T(8,128)(2,1)S(1)} all-gather(bf16[8,1664]{1,0:T(8,128)(2,1)S(1)} %reduce_sum.12), channel_id=1, replica_groups=mesh['job'=2,'tok'=16] {'tok'}, dimensions={0}, use_global_device_ids=true | all-gather | bytes 452608 | tf_op jit(solution)/shard_map/all_gather | solution.py:411
  247.0 0.3 copy.41
  247.3 0.1 convert_element_type.9
  247.4 0.6 copy.46
  248.0 1.0 copy.45
  249.0 0.7 slice_bitcast_fusion
  (12 shorter events, 0.1 us)
Async XLA Ops:
  2.3 0.9 copy-start
  3.2 2.2 copy-start.2
  46.6 9.0 %copy-start.9 = (s32[2]{0:T(128)S(1)}, s32[2]{0:T(128)}, u32[]{:S(2)}) copy-start(s32[2]{0:T(128)} %param.15) | copy-start | bytes 28
  46.6 32.0 %copy-start.3 = (bf16[2,1,2,48,512]{4,3,2,1,0:T(8,128)(2,1)S(1)}, bf16[2,1,2,48,512]{4,3,2,1,0:T(8,128)(2,1)}, u32[]{:S(2)}) copy-start(bf16[2,1,2,48,512]{4,3,2,1,0:T(8,128)(2,1)} %param.16) | copy-start | bytes 589828
  46.6 32.0 %copy-start.4 = (bf16[2,1,2,48,512]{4,3,2,1,0:T(8,128)(2,1)S(1)}, bf16[2,1,2,48,512]{4,3,2,1,0:T(8,128)(2,1)}, u32[]{:S(2)}) copy-start(bf16[2,1,2,48,512]{4,3,2,1,0:T(8,128)(2,1)} %param.17) | copy-start | bytes 589828
  46.7 31.9 %copy-start.5 = (bf16[2,1,2,48,512]{4,3,2,1,0:T(8,128)(2,1)S(1)}, bf16[2,1,2,48,512]{4,3,2,1,0:T(8,128)(2,1)}, u32[]{:S(2)}) copy-start(bf16[2,1,2,48,512]{4,3,2,1,0:T(8,128)(2,1)} %param.18) | copy-start | bytes 589828
  46.7 31.9 %copy-start.6 = (bf16[2,1,2,48,512]{4,3,2,1,0:T(8,128)(2,1)S(1)}, bf16[2,1,2,48,512]{4,3,2,1,0:T(8,128)(2,1)}, u32[]{:S(2)}) copy-start(bf16[2,1,2,48,512]{4,3,2,1,0:T(8,128)(2,1)} %param.19) | copy-start | bytes 589828
  46.7 31.9 %copy-start.7 = (s32[512]{0:T(512)S(1)}, s32[512]{0:T(512)}, u32[]{:S(2)}) copy-start(s32[512]{0:T(512)} %param.14) | copy-start | bytes 6148
  46.7 44.5 %copy-start.1 = (bf16[512,128]{1,0:T(8,128)(2,1)S(1)}, bf16[512,128]{1,0:T(8,128)(2,1)}, u32[]{:S(2)}) copy-start(bf16[512,128]{1,0:T(8,128)(2,1)} %w_out_ref.3) | copy-start | bytes 393220
  46.7 44.6 %copy-start.8 = (bf16[128,1024]{1,0:T(8,128)(2,1)S(1)}, bf16[128,1024]{1,0:T(8,128)(2,1)}, u32[]{:S(2)}) copy-start(bf16[128,1024]{1,0:T(8,128)(2,1)} %param.11) | copy-start | bytes 786436
  48.3 30.3 %all-to-all-start = ((bf16[16,2,32,512]{3,2,1,0:T(8,128)(2,1)}), bf16[16,2,32,512]{3,2,1,0:T(8,128)(2,1)S(1)}, u32[]{:S(2)}, u32[]{:S(2)}) async-start(bf16[16,2,32,512]{3,2,1,0:T(8,128)(2,1)} %bitcast.3), calls=%async_computation | async-start | bytes 2097152 | tf_op jit(solution)/shard_map/all_to_all | solution.py:323
  84.3 29.8 %all-to-all-start.1 = ((bf16[16,2,32,512]{3,2,1,0:T(8,128)(2,1)}), bf16[16,2,32,512]{3,2,1,0:T(8,128)(2,1)S(1)}, u32[]{:S(2)}, u32[]{:S(2)}) async-start(bf16[16,2,32,512]{3,2,1,0:T(8,128)(2,1)} %get-tuple-element.13), calls=%async_computation.1 | async-start | bytes 2097152 | tf_op jit(solution)/shard_map/all_to_all | solution.py:323
where the time goes:
time: 250 us
  Pallas kernels  139 us (56%)
  waiting for transfers between devices  45.5 us (18%)
  blocking collectives  39.9 us (16%)
  starting transfers between devices  14.2 us (6%)
  local copies, waits for them, and re-layouts  8.87 us (4%)
    pallas_call x1, Pallas kernels, backward_rows(): pl.pallas_call(functools.partial(backward_kernel, first, last), grid=(ste...  92.3 us
    all_to_all x2, waiting for transfers between devices, swap(): return lax.all_to_all(array, 'tok', split_axis=0, concat_axis=0, tiled=True)  45.5 us
    pallas_call x1, Pallas kernels, forward_rows(): pl.pallas_call(forward_kernel, grid=(steps,), in_specs=[pl.BlockSpec((ste...  41.2 us
    all_gather x1, blocking collectives, body(): summed = lax.all_gather(summed, 'tok', axis=0, tiled=True).astype(F32)  20.6 us
    all_to_all x1, blocking collectives, swap(): return lax.all_to_all(array, 'tok', split_axis=0, concat_axis=0, tiled=True)  19.4 us
    all_to_all x2, starting transfers between devices, swap(): return lax.all_to_all(array, 'tok', split_axis=0, concat_axis=0, tiled=True)  14.2 us
    pallas_call x1, Pallas kernels, attend_rows(): pl.pallas_call(functools.partial(attend_kernel, first, last), grid=(layer...  5.68 us
    unnamed x24, local copies, waits for them, and re-layouts  5.02 us
  transfers between devices with their start and end apart: 2, of which 2 were waited for; matrix products, arithmetic and copies ran while one was open for 0% of the time, Pallas kernels for 0%

commit v1 on v0

--- a/solution.py
+++ b/solution.py
@@ -9,7 +9,7 @@
 from jax.sharding import PartitionSpec as P
 
 LEVELS = 200
-CHUNKS = 1
+CHUNKS = 2
 
 
 sigma_high = 160.0
@@ -38,16 +38,16 @@
 
 
 def normalize(inputs):
-    centered = inputs - jnp.mean(inputs, -1, keepdims=True)
-    inv_std = lax.rsqrt(jnp.mean(centered * centered, -1, keepdims=True) + epsilon)
+    centered = inputs - jnp.mean(inputs, 0, keepdims=True)
+    inv_std = lax.rsqrt(jnp.mean(centered * centered, 0, keepdims=True) + epsilon)
     return centered * inv_std, inv_std
 
 
 def norm_back(normed, inv_std, upstream):
     return inv_std * (
         upstream
-        - jnp.mean(upstream, -1, keepdims=True)
-        - normed * jnp.mean(upstream * normed, -1, keepdims=True)
+        - jnp.mean(upstream, 0, keepdims=True)
+        - normed * jnp.mean(upstream * normed, 0, keepdims=True)
     )
 
 
@@ -55,53 +55,80 @@
     return 256 if width % 256 == 0 else width
 
 
-def forward_kernel(pair_ref, w_in_ref, w_out_ref, w_bias_ref, bias_ref):
-    width = w_out_ref.shape[0]
+def interleave(make_stages, count, lag):
+    rows = [make_stages(index) for index in range(count)]
+    running = []
+    clock = 0
+    while rows or running:
+        if rows and clock % lag == 0:
+            running.append(rows.pop(0))
+        running = [row for row in running if next(row, None) is not None]
+        clock += 1
+
+
+def for_rows(count, group, make_stages, lag):
+    group = math.gcd(count, group)
+
+    def step(at, carry):
+        interleave(lambda index: make_stages(at * group + index), group, lag)
+        return carry
+
+    if count == group:
+        step(0, 0)
+    else:
+        lax.fori_loop(0, count // group, step, 0)
+
+
+def forward_kernel(pair_ref, w_in_t_ref, w_out_t_ref, w_bias_ref, bias_ref):
+    width = w_out_t_ref.shape[1]
     piece = split_width(width)
 
-    def one_row(row, carry):
-        pair_float = pair_ref[row].astype(F32)
+    def stages(row):
+        pair_float = pair_ref[row].T.astype(F32)
         normed_in = normalize(pair_float)[0].astype(BF16)
+        yield True
         lifted = pair_float
         for at in range(0, width, piece):
-            half_gate = mm(normed_in, w_in_ref[:, at : at + piece])
-            up_in = mm(normed_in, w_in_ref[:, width + at : width + at + piece])
+            half_gate = mm(w_in_t_ref[at : at + piece, :], normed_in)
+            up_in = mm(w_in_t_ref[width + at : width + at + piece, :], normed_in)
+            yield True
             hidden = (half_gate * (1.0 + jnp.tanh(half_gate)) * up_in).astype(BF16)
-            lifted = lifted + mm(hidden, w_out_ref[at : at + piece, :])
+            lifted = lifted + mm(w_out_t_ref[:, at : at + piece], hidden)
+            yield True
         normed_out = normalize(lifted)[0].astype(BF16)
-        bias_ref[row] = mm(w_bias_ref[...], normed_out, 1, 1).astype(BF16)
-        return carry
-
-    lax.fori_loop(0, pair_ref.shape[0], one_row, 0)
-
-
-def forward_rows(chunk, rows, pair, w_in_half, w_out, w_bias):
+        yield True
+        bias_ref[row] = mm(w_bias_ref[...], normed_out).astype(BF16)
+
+    for_rows(pair_ref.shape[0], 4, stages, 2)
+
+
+def forward_rows(chunk, rows, pair, w_in_half_t, w_out_t, w_bias):
     crop, channels = pair.shape[1:]
     lanes = w_bias.shape[0]
-    step = math.gcd(rows, 4)
+    step = math.gcd(rows, 8)
     steps = rows // step
     positions = rows * crop
-    width = w_out.shape[0]
+    width = w_out_t.shape[1]
     whole = lambda i: (0, 0)
     return pl.pallas_call(
         forward_kernel,
         grid=(steps,),
         in_specs=[
             pl.BlockSpec((step, crop, channels), lambda i: (chunk * steps + i, 0, 0)),
-            pl.BlockSpec(w_in_half.shape, whole),
-            pl.BlockSpec(w_out.shape, whole),
+            pl.BlockSpec(w_in_half_t.shape, whole),
+            pl.BlockSpec(w_out_t.shape, whole),
             pl.BlockSpec(w_bias.shape, whole),
         ],
         out_specs=pl.BlockSpec((step, lanes, crop), lambda i: (i, 0, 0)),
         out_shape=jax.ShapeDtypeStruct((rows, lanes, crop), BF16),
-        compiler_params=pltpu.CompilerParams(vmem_limit_bytes=40 * 2**20),
+        compiler_params=pltpu.CompilerParams(vmem_limit_bytes=48 * 2**20),
         cost_estimate=pl.CostEstimate(
             flops=2 * positions * channels * (3 * width + lanes),
             bytes_accessed=positions * (channels + lanes) * 2,
             transcendentals=positions * width,
         ),
         name="pair_forward",
-    )(pair, w_in_half, w_out, w_bias)
+    )(pair, w_in_half_t, w_out_t, w_bias)
 
 
 def backward_kernel(
@@ -109,95 +136,92 @@
     last,
     pair_ref,
     d_bias_ref,
+    w_in_t_ref,
+    w_out_t_ref,
+    w_bias_t_ref,
     w_in_ref,
     w_out_ref,
-    w_bias_ref,
-    w_in_t_ref,
-    w_out_t_ref,
     *refs,
 ):
     if first:
-        pair_grad_ref, sums_ref, bias_sums_ref = refs[:3]
+        pair_grad_ref, sums_ref = refs[:2]
     else:
-        before_ref, bias_before_ref, _, pair_grad_ref, sums_ref, bias_sums_ref = refs[:6]
+        before_ref, _, pair_grad_ref, sums_ref = refs[:4]
     width = w_out_ref.shape[0]
-    channels = w_out_ref.shape[1]
     piece = split_width(width)
+    lanes = w_bias_t_ref.shape[1]
 
     @pl.when(pl.program_id(0) == 0)
     def _():
         if first:
             sums_ref[...] = jnp.zeros_like(sums_ref)
-            bias_sums_ref[...] = jnp.zeros_like(bias_sums_ref)
         else:
             sums_ref[...] = before_ref[...]
-            bias_sums_ref[...] = bias_before_ref[...]
-
-    def one_row(row, carry):
-        pair_float = pair_ref[row].astype(F32)
+
+    def stages(row):
+        pair_float = pair_ref[row].T.astype(F32)
         normed_float, inv_in = normalize(pair_float)
         normed_in = normed_float.astype(BF16)
+        yield True
         lifted = pair_float
         kept = []
         for at in range(0, width, piece):
-            half_gate = mm(normed_in, w_in_ref[:, at : at + piece])
-            up_in = mm(normed_in, w_in_ref[:, width + at : width + at + piece])
+            half_gate = mm(w_in_t_ref[at : at + piece, :], normed_in)
+            up_in = mm(w_in_t_ref[width + at : width + at + piece, :], normed_in)
+            yield True
             one_plus = 1.0 + jnp.tanh(half_gate)
             silu = half_gate * one_plus
             hidden = (silu * up_in).astype(BF16)
             slope = one_plus * (1.0 + half_gate * (2.0 - one_plus)) * up_in
             kept.append((silu, slope, hidden))
-            lifted = lifted + mm(hidden, w_out_ref[at : at + piece, :])
+            lifted = lifted + mm(w_out_t_ref[:, at : at + piece], hidden)
+            yield True
         out_float, inv_out = normalize(lifted)
         normed_out = out_float.astype(BF16)
+        yield True
         d_bias = d_bias_ref[row]
-        bias_sums_ref[...] += mm(d_bias, normed_out)
-        d_normed = mm(d_bias, w_bias_ref[...], 0, 0)
+        d_normed = mm(w_bias_t_ref[...], d_bias)
+        sums_ref[3 * width : 3 * width + lanes, :] += mm(d_bias, normed_out, 1, 1)
         d_lifted = norm_back(out_float, inv_out, d_normed)
         lifted_half = d_lifted.astype(BF16)
-        lifted_t = lifted_half.T
-        normed_t = normed_in.T
+        yield True
         d_normed_in = jnp.zeros_like(pair_float)
         for index, (silu, slope, hidden) in enumerate(kept):
             at = index * piece
             cols = slice(at, at + piece)
             up_cols = slice(width + at, width + at + piece)
             out_cols = slice(2 * width + at, 2 * width + at + piece)
-            sums_ref[:, out_cols] += mm(lifted_t, hidden)
-            d_hidden = mm(lifted_half, w_out_t_ref[:, cols])
+            d_hidden = mm(w_out_ref[cols, :], lifted_half)
+            sums_ref[out_cols, :] += mm(hidden, lifted_half, 1, 1)
+            yield True
             d_gate = (0.5 * d_hidden * slope).astype(BF16)
             d_up = (d_hidden * silu).astype(BF16)
-            sums_ref[:, cols] += mm(normed_t, d_gate)
-            sums_ref[:, up_cols] += mm(normed_t, d_up)
-            d_normed_in = d_normed_in + mm(d_gate, w_in_t_ref[cols, :])
-            d_normed_in = d_normed_in + mm(d_up, w_in_t_ref[up_cols, :])
-        pair_grad_ref[row] = (
-            d_lifted + norm_back(normed_float, inv_in, d_normed_in)
-        ).astype(BF16)
-        return carry
-
-    lax.fori_loop(0, pair_ref.shape[0], one_row, 0)
+            d_normed_in = d_normed_in + mm(w_in_ref[:, cols], d_gate)
+            sums_ref[cols, :] += mm(d_gate, normed_in, 1, 1)
+            d_normed_in = d_normed_in + mm(w_in_ref[:, up_cols], d_up)
+            sums_ref[up_cols, :] += mm(d_up, normed_in, 1, 1)
+            yield True
+        pair_grad = d_lifted + norm_back(normed_float, inv_in, d_normed_in)
+        pair_grad_ref[row] = pair_grad.astype(BF16).T
+
+    for_rows(pair_ref.shape[0], 4, stages, 3)
 
     if last:
         packed_ref = refs[-1]
 
         @pl.when(pl.program_id(0) == pl.num_programs(0) - 1)
         def _():
-            done = 3 * width
-            lanes = bias_sums_ref.shape[0]
-            packed_ref[:, :done] = sums_ref[...].astype(BF16)
-            padded = jnp.concatenate(
-                [bias_sums_ref[...], jnp.zeros((channels - lanes, channels), F32)], 0
-            )
-            packed_ref[:, done:] = padded.T.astype(BF16)
-
-
-def backward_rows(chunk, chunks, rows, pair, d_bias, weights, state):
-    w_in_half, w_out, w_bias, w_in_t, w_out_t = weights
+            done = sums_ref.shape[0]
+            packed_ref[:done, :] = sums_ref[...].astype(BF16)
+            packed_ref[done:, :] = jnp.zeros((packed_ref.shape[0] - done, packed_ref.shape[1]), BF16)
+
+
+def backward_rows(chunk, chunks, rows, packed_rows, pair, d_bias, weights, state):
+    w_in_half_t, w_out_t, w_bias_t, w_in, w_out = weights
     crop, channels = pair.shape[1:]
-    lanes = w_bias.shape[0]
+    lanes = w_bias_t.shape[1]
     width = w_out.shape[0]
-    step = math.gcd(rows, 4)
+    step = math.gcd(rows, 8)
     steps = rows // step
     positions = rows * crop
     first, last = chunk == 0, chunk == chunks - 1
@@ -208,20 +232,18 @@
     operands = [pair, d_bias, *weights]
     aliases = {}
     if not first:
-        pair_grad, sums, bias_sums = state
-        operands += [sums, bias_sums, pair_grad]
-        in_specs += [pl.BlockSpec(sums.shape, whole), pl.BlockSpec(bias_sums.shape, whole)]
-        in_specs += [pl.BlockSpec(memory_space=pl.ANY)]
+        pair_grad, sums = state
+        operands += [sums, pair_grad]
+        in_specs += [pl.BlockSpec(sums.shape, whole), pl.BlockSpec(memory_space=pl.ANY)]
         aliases = {len(operands) - 1: 0}
     shapes = [
         jax.ShapeDtypeStruct(pair.shape, BF16),
-        jax.ShapeDtypeStruct((channels, 3 * width), F32),
-        jax.ShapeDtypeStruct((lanes, channels), F32),
+        jax.ShapeDtypeStruct((3 * width + lanes, channels), F32),
     ]
-    out_specs = [pair_spec, pl.BlockSpec(shapes[1].shape, whole), pl.BlockSpec(shapes[2].shape, whole)]
+    out_specs = [pair_spec, pl.BlockSpec(shapes[1].shape, whole)]
     if last:
-        shapes.append(jax.ShapeDtypeStruct((channels, 3 * width + channels), BF16))
-        out_specs.append(pl.BlockSpec(shapes[3].shape, whole))
+        shapes.append(jax.ShapeDtypeStruct((packed_rows, channels), BF16))
+        out_specs.append(pl.BlockSpec(shapes[2].shape, whole))
     return pl.pallas_call(
         functools.partial(backward_kernel, first, last),
         grid=(steps,),
@@ -229,7 +251,7 @@
         out_specs=out_specs,
         out_shape=shapes,
         input_output_aliases=aliases,
-        compiler_params=pltpu.CompilerParams(vmem_limit_bytes=48 * 2**20),
+        compiler_params=pltpu.CompilerParams(vmem_limit_bytes=56 * 2**20),
         cost_estimate=pl.CostEstimate(
             flops=2 * positions * channels * (9 * width + 2 * lanes),
             bytes_accessed=positions * (2 * channels + lanes) * 2,
@@ -346,9 +368,10 @@
     lanes = heads * layers
 
     halves = jnp.concatenate([jnp.full((width,), 0.5, BF16), jnp.ones((width,), BF16)])
-    w_in_half = weight_in * halves[None, :]
+    w_in_half_t = (weight_in * halves[None, :]).T
+    w_out_t = weight_out.T
     w_bias = jnp.transpose(weight_bias, (2, 0, 1)).reshape(lanes, channels)
-    pair_weights = (w_in_half, weight_out, w_bias, weight_in.T, weight_out.T)
+    pair_weights = (w_in_half_t, w_out_t, w_bias.T, weight_in, weight_out)
 
     group = lax.axis_index("tok") // heads
     weights = sample_weight(lax.dynamic_slice_in_dim(noise_level, group * samples, samples))
@@ -363,7 +386,7 @@
 
     arrived = []
     for chunk in range(chunks):
-        bias = forward_rows(chunk, rows, pair_states, w_in_half, weight_out, w_bias)
+        bias = forward_rows(chunk, rows, pair_states, w_in_half_t, w_out_t, w_bias)
         bias = jnp.transpose(bias, (1, 0, 2)).reshape(heads, layers, rows, crop)
         arrived.append(swap(jnp.tile(bias, (groups, 1, 1, 1))))
 
@@ -393,6 +416,8 @@
             d_bias = jnp.transpose(d_bias.reshape(layers, devices, rows, crop), (1, 0, 2, 3))
         returned.append(swap(d_bias))
 
+    sum_rows = 3 * width + lanes
+    share = 16 * -(-sum_rows // (16 * devices))
     pair_state = None
     for chunk in range(chunks):
         d_bias = returned[chunk]
@@ -401,18 +426,24 @@
             d_bias = jnp.sum(d_bias, 0).astype(BF16)
         d_bias = jnp.transpose(d_bias.reshape(lanes, rows, crop), (1, 0, 2))
         pair_state = backward_rows(
-            chunk, chunks, rows, pair_states, d_bias, pair_weights, pair_state and pair_state[:3]
+            chunk,
+            chunks,
+            rows,
+            share * devices,
+            pair_states,
+            d_bias,
+            pair_weights,
+            pair_state and pair_state[:2],
         )
-    pair_grad, _, _, packed = pair_state
-
-    share = channels // devices
-    parts = swap(packed.reshape(devices, share, packed.shape[1]))
+    pair_grad, _, packed = pair_state
+
+    parts = swap(packed.reshape(devices, share, channels))
     summed = jnp.sum(parts.astype(F32), 0).astype(BF16)
     summed = lax.all_gather(summed, "tok", axis=0, tiled=True).astype(F32)
-    grad_in = summed[:, : 2 * width]
-    grad_out = summed[:, 2 * width : 3 * width].T
-    grad_bias = summed[:, 3 * width : 3 * width + lanes].reshape(channels, heads, layers)
-    grad_bias = jnp.transpose(grad_bias, (2, 0, 1))
+    grad_in = summed[: 2 * width].T
+    grad_out = summed[2 * width : 3 * width]
+    grad_bias = summed[3 * width : sum_rows].reshape(heads, layers, channels)
+    grad_bias = jnp.transpose(grad_bias, (1, 2, 0))
 
     d_query = jnp.stack(d_queries, 0).reshape(chunks, layers, samples, depth, devices, rows)
     d_query = jnp.transpose(d_query, (1, 2, 3, 4, 0, 5)).reshape(query_states.shape)

time: 250 us -> 199 us (0.80)
  Pallas kernels: 139 us -> 84.9 us
  waiting for transfers between devices: 45.5 us -> 34.4 us
  local copies, waits for them, and re-layouts: 8.87 us -> 17.2 us
  starting transfers between devices: 14.2 us -> 20.6 us
    pallas_call x1 -> x2, Pallas kernels: 92.3 us -> 56.2 us  [backward_rows(): pl.pallas_call(functools.partial(backward_kernel, first, last), grid=(ste...]
    pallas_call x1 -> x2, Pallas kernels: 41.2 us -> 20.2 us  [forward_rows(): pl.pallas_call(forward_kernel, grid=(steps,), in_specs=[pl.BlockSpec((ste...]
    all_to_all x2 -> x4, waiting for transfers between devices: 45.5 us -> 34.4 us  [swap(): return lax.all_to_all(array, 'tok', split_axis=0, concat_axis=0, tiled=True)]
    all_to_all x2 -> x4, starting transfers between devices: 14.2 us -> 20.6 us  [swap(): return lax.all_to_all(array, 'tok', split_axis=0, concat_axis=0, tiled=True)]
    unnamed x24 -> x27, local copies, waits for them, and re-layouts: 5.02 us -> 9.7 us
    pallas_call x1 -> x2, Pallas kernels: 5.68 us -> 8.45 us  [attend_rows(): pl.pallas_call(functools.partial(attend_kernel, first, last), grid=(layer...]
  transfers between devices with their start and end apart: 2 -> 4, of which waited for: 2 -> 4; matrix products, arithmetic and copies ran while one was open for 0% -> 3% of each run, Pallas kernels for 0% -> 7%
where the time goes in v1:
time: 199 us; the launch traced here: 198 us
  Pallas kernels  84.9 us (43%)
  blocking collectives  39.2 us (20%)
  waiting for transfers between devices  34.4 us (17%)
  starting transfers between devices  20.6 us (10%)
  local copies, waits for them, and re-layouts  17.2 us (9%)
    pallas_call x2, Pallas kernels, backward_rows(): pl.pallas_call(functools.partial(backward_kernel, first, last), grid=(ste...  56.2 us
    all_to_all x4, waiting for transfers between devices, swap(): return lax.all_to_all(array, 'tok', split_axis=0, concat_axis=0, tiled=True)  34.4 us
    all_gather x1, blocking collectives, body(): summed = lax.all_gather(summed, 'tok', axis=0, tiled=True).astype(F32)  20.9 us
    all_to_all x4, starting transfers between devices, swap(): return lax.all_to_all(array, 'tok', split_axis=0, concat_axis=0, tiled=True)  20.6 us
    pallas_call x2, Pallas kernels, forward_rows(): pl.pallas_call(forward_kernel, grid=(steps,), in_specs=[pl.BlockSpec((ste...  20.2 us
    all_to_all x1, blocking collectives, swap(): return lax.all_to_all(array, 'tok', split_axis=0, concat_axis=0, tiled=True)  18.4 us
    unnamed x27, local copies, waits for them, and re-layouts  9.7 us
    pallas_call x2, Pallas kernels, attend_rows(): pl.pallas_call(functools.partial(attend_kernel, first, last), grid=(layer...  8.45 us
  transfers between devices with their start and end apart: 4, of which 4 were waited for; matrix products, arithmetic and copies ran while one was open for 3% of the time, Pallas kernels for 7%

profile of v1, /device:TPU:0, one launch (start us, length us, event | category | flops | bytes accessed | tf_op | source)
XLA Modules:
  0.0 198.4 jit_solution(16328905010086251214)
XLA Ops:
  0.6 0.7 copy.35
  1.3 1.0 copy.34
  2.4 1.2 copy.33
  3.5 0.9 multiply_bitcast_fusion.w_in_t_ref
  4.4 2.3 %copy-done.5 = bf16[32,512,128]{2,1,0:T(8,128)(2,1)S(1)} copy-done((bf16[32,512,128]{2,1,0:T(8,128)(2,1)S(1)}, bf16[32,512,128]{2,1,0:T(8,128)(2,1)}, u32[]{:S(2)}) %copy-start.5) | copy-done | bytes 4194328
  6.7 10.1 %pair_forward.3 = bf16[16,32,512]{2,1,0:T(8,128)(2,1)S(1)} custom-call(bf16[32,512,128]{2,1,0:T(8,128)(2,1)S(1)} %copy-done.5, bf16[1024,128]{1,0:T(8,128)(2,1)S(1)} %multiply_bitcast_fusion.w_in_t_ref, bf16[128,512]{1,0:T(8,128)(2,1)S(1)} %bitcast.54, bf16[32,128]{1,0:T(8,128)(2,1)S(1)} %bitcast.58), custom_call_target="tpu_custom_call" | custom-call | flops 3288334336 | bytes 2621440 | tf_op jit(solution)/shard_map/pair_forward/pallas_call | solution.py:113
  16.8 1.1 copy.39
  17.9 7.4 %all-to-all-start.1 = ((bf16[16,2,16,512]{3,2,1,0:T(8,128)(2,1)}), bf16[16,2,16,512]{3,2,1,0:T(8,128)(2,1)S(1)}, u32[]{:S(2)}, u32[]{:S(2)}) async-start(bf16[16,2,16,512]{3,2,1,0:T(8,128)(2,1)} %bitcast.16), calls=%async_computation.1 | async-start | bytes 1048576 | tf_op jit(solution)/shard_map/all_to_all | solution.py:345
  25.3 2.2 %copy-done.6 = bf16[32,512,128]{2,1,0:T(8,128)(2,1)S(1)} copy-done((bf16[32,512,128]{2,1,0:T(8,128)(2,1)S(1)}, bf16[32,512,128]{2,1,0:T(8,128)(2,1)}, u32[]{:S(2)}) %copy-start.6) | copy-done | bytes 4194328
  27.5 10.1 %pair_forward.2 = bf16[16,32,512]{2,1,0:T(8,128)(2,1)S(1)} custom-call(bf16[32,512,128]{2,1,0:T(8,128)(2,1)S(1)} %copy-done.6, bf16[1024,128]{1,0:T(8,128)(2,1)S(1)} %multiply_bitcast_fusion.w_in_t_ref, bf16[128,512]{1,0:T(8,128)(2,1)S(1)} %bitcast.55, bf16[32,128]{1,0:T(8,128)(2,1)S(1)} %bitcast.59), custom_call_target="tpu_custom_call" | custom-call | flops 3288334336 | bytes 2621440 | tf_op jit(solution)/shard_map/pair_forward/pallas_call | solution.py:113
  37.7 1.1 copy.36
  38.8 1.0 all-to-all-done.1.bias_ref
  39.8 5.0 %all-to-all-start = ((bf16[16,2,16,512]{3,2,1,0:T(8,128)(2,1)}), bf16[16,2,16,512]{3,2,1,0:T(8,128)(2,1)S(1)}, u32[]{:S(2)}, u32[]{:S(2)}) async-start(bf16[16,2,16,512]{3,2,1,0:T(8,128)(2,1)} %bitcast.5), calls=%async_computation | async-start | bytes 1048576 | tf_op jit(solution)/shard_map/all_to_all | solution.py:345
  44.8 0.3 copy.37
  46.1 4.3 %attention_backward.2 = (bf16[2,2,48,256]{3,2,1,0:T(8,128)(2,1)S(1)}, f32[2,2,48,512]{3,2,1,0:T(8,128)S(1)}, f32[2,2,48,512]{3,2,1,0:T(8,128)S(1)}, bf16[16,2,16,512]{3,2,1,0:T(8,128)(2,1)}) custom-call(f32[2]{0:T(128)S(1)} %multiply_divide_fusion.weight_ref, bf16[16,2,16,512]{3,2,1,0:T(8,128)(2,1)S(1)} %all-to-all-done.1.bias_ref, s32[1,512]{1,0:T(1,128)S(1)} %bitcast.61, ...), custom_call_target="tpu_custom_call" | custom-call | flops 251658240 | bytes 2228224 | tf_op jit(solution)/shard_map/attention_backward/pallas_call | solution.py:323
  50.3 8.9 %all-to-all-done.bias_ref = bf16[16,2,16,512]{3,2,1,0:T(8,128)(2,1)S(1)} async-done(((bf16[16,2,16,512]{3,2,1,0:T(8,128)(2,1)}), bf16[16,2,16,512]{3,2,1,0:T(8,128)(2,1)S(1)}, u32[]{:S(2)}, u32[]{:S(2)}) %all-to-all-start) | async-done | bytes 524320 | tf_op jit(solution)/shard_map/all_to_all | solution.py:345
  59.3 4.2 %attention_backward.3 = (bf16[2,2,48,256]{3,2,1,0:T(8,128)(2,1)S(1)}, bf16[2,2,48,512]{3,2,1,0:T(8,128)(2,1)}, bf16[2,2,48,512]{3,2,1,0:T(8,128)(2,1)}, bf16[16,2,16,512]{3,2,1,0:T(8,128)(2,1)S(1)}) custom-call(f32[2]{0:T(128)S(1)} %multiply_divide_fusion.weight_ref, bf16[16,2,16,512]{3,2,1,0:T(8,128)(2,1)S(1)} %all-to-all-done.bias_ref, ...), custom_call_target="tpu_custom_call" | custom-call | flops 251658240 | bytes 2228224 | tf_op jit(solution)/shard_map/attention_backward/pallas_call | solution.py:323
  63.4 18.4 %all_to_all.25 = bf16[16,2,16,512]{3,2,1,0:T(8,128)(2,1)S(1)} all-to-all(bf16[16,2,16,512]{3,2,1,0:T(8,128)(2,1)S(1)} %get-tuple-element.21), channel_id=1, replica_groups=mesh['job'=2,'tok'=16] {'tok'}, dimensions={0} | all-to-all | bytes 1048576 | tf_op jit(solution)/shard_map/all_to_all | solution.py:345
  81.8 4.1 %all-to-all-start.3 = ((bf16[16,2,16,512]{3,2,1,0:T(8,128)(2,1)}), bf16[16,2,16,512]{3,2,1,0:T(8,128)(2,1)S(1)}, u32[]{:S(2)}, u32[]{:S(2)}) async-start(bf16[16,2,16,512]{3,2,1,0:T(8,128)(2,1)} %get-tuple-element.22), calls=%async_computation.3 | async-start | bytes 1048576 | tf_op jit(solution)/shard_map/all_to_all | solution.py:345
  85.9 0.7 copy.45
  86.6 1.1 copy.60
  87.7 12.7 %all-to-all-done.3 = bf16[16,2,16,512]{3,2,1,0:T(8,128)(2,1)S(1)} async-done(((bf16[16,2,16,512]{3,2,1,0:T(8,128)(2,1)}), bf16[16,2,16,512]{3,2,1,0:T(8,128)(2,1)S(1)}, u32[]{:S(2)}, u32[]{:S(2)}) %all-to-all-start.3) | async-done | bytes 524320 | tf_op jit(solution)/shard_map/all_to_all | solution.py:345
  100.4 1.1 copy.59
  101.5 27.7 %pair_backward.2 = (bf16[32,512,128]{2,1,0:T(8,128)(2,1)}, f32[1568,128]{1,0:T(8,128)}) custom-call(bf16[32,512,128]{2,1,0:T(8,128)(2,1)} %pair_ref.7, bf16[16,32,512]{2,1,0:T(8,128)(2,1)} %bitcast.75, bf16[1024,128]{1,0:T(8,128)(2,1)} %copy-done.2, bf16[128,512]{1,0:T(8,128)(2,1)} %bitcast.56, bf16[128,32]{1,0:T(8,128)(2,1)} %bitcast.78, ...), custom_call_target="tpu_custom_call" | custom-call | flops 9797894144 | bytes 4718592 | tf_op jit(solution)/shard_map/pair_backward/pallas_call | solution.py:247
  129.2 28.5 %pair_backward.3 = (bf16[32,512,128]{2,1,0:T(8,128)(2,1)}, f32[1568,128]{1,0:T(8,128)}, bf16[1792,128]{1,0:T(8,128)(2,1)}) custom-call(bf16[32,512,128]{2,1,0:T(8,128)(2,1)} %pair_ref.7, bf16[16,32,512]{2,1,0:T(8,128)(2,1)} %bitcast.74, bf16[1024,128]{1,0:T(8,128)(2,1)} %copy-done.2, bf16[128,512]{1,0:T(8,128)(2,1)} %bitcast.57, ...), custom_call_target="tpu_custom_call", output_to_operand_aliasing={{0}: (8, {})} | custom-call | flops 9797894144 | bytes 4718592 | tf_op jit(solution)/shard_map/pair_backward/pallas_call | solution.py:247
  157.7 4.1 %all-to-all-start.4 = ((bf16[16,112,128]{2,1,0:T(8,128)(2,1)}), bf16[16,112,128]{2,1,0:T(8,128)(2,1)S(1)}, u32[]{:S(2)}, u32[]{:S(2)}) async-start(bf16[16,112,128]{2,1,0:T(8,128)(2,1)} %bitcast.76), calls=%async_computation.4 | async-start | bytes 917504 | tf_op jit(solution)/shard_map/all_to_all | solution.py:345
  162.3 0.9 copy.50
  163.2 11.8 %all-to-all-done.4 = bf16[16,112,128]{2,1,0:T(8,128)(2,1)S(1)} async-done(((bf16[16,112,128]{2,1,0:T(8,128)(2,1)}), bf16[16,112,128]{2,1,0:T(8,128)(2,1)S(1)}, u32[]{:S(2)}, u32[]{:S(2)}) %all-to-all-start.4) | async-done | bytes 458784 | tf_op jit(solution)/shard_map/all_to_all | solution.py:345
  175.1 20.9 %all_gather.3 = bf16[1792,128]{1,0:T(8,128)(2,1)S(1)} all-gather(bf16[112,128]{1,0:T(8,128)(2,1)S(1)} %reduce_sum.12), channel_id=1, replica_groups=mesh['job'=2,'tok'=16] {'tok'}, dimensions={0}, use_global_device_ids=true | all-gather | bytes 487424 | tf_op jit(solution)/shard_map/all_gather | solution.py:442
  196.0 0.7 slice.37
  196.7 0.6 copy.54
  197.4 1.0 copy.53
  (34 shorter events, 1.6 us)
Async XLA Ops:
  2.3 23.0 %copy-start.3 = (bf16[512,128]{0,1:T(8,128)(2,1)}, bf16[512,128]{0,1:T(8,128)(2,1)S(1)}, u32[]{:S(2)}) copy-start(bf16[512,128]{0,1:T(8,128)(2,1)S(1)} %copy.34) | copy-start | bytes 393220
  4.4 20.9 %copy-start.2 = (bf16[1024,128]{1,0:T(8,128)(2,1)}, bf16[1024,128]{1,0:T(8,128)(2,1)S(1)}, u32[]{:S(2)}) copy-start(bf16[1024,128]{1,0:T(8,128)(2,1)S(1)} %multiply_bitcast_fusion.w_in_t_ref) | copy-start | bytes 786436
  4.4 2.3 %copy-start.5 = (bf16[32,512,128]{2,1,0:T(8,128)(2,1)S(1)}, bf16[32,512,128]{2,1,0:T(8,128)(2,1)}, u32[]{:S(2)}) copy-start(bf16[32,512,128]{2,1,0:T(8,128)(2,1)} %pair_ref.7) | copy-start | bytes 12582916
  17.9 21.9 %all-to-all-start.1 = ((bf16[16,2,16,512]{3,2,1,0:T(8,128)(2,1)}), bf16[16,2,16,512]{3,2,1,0:T(8,128)(2,1)S(1)}, u32[]{:S(2)}, u32[]{:S(2)}) async-start(bf16[16,2,16,512]{3,2,1,0:T(8,128)(2,1)} %bitcast.16), calls=%async_computation.1 | async-start | bytes 1048576 | tf_op jit(solution)/shard_map/all_to_all | solution.py:345
  25.3 2.2 %copy-start.6 = (bf16[32,512,128]{2,1,0:T(8,128)(2,1)S(1)}, bf16[32,512,128]{2,1,0:T(8,128)(2,1)}, u32[]{:S(2)}) copy-start(bf16[32,512,128]{2,1,0:T(8,128)(2,1)} %pair_ref.7) | copy-start | bytes 12582916
  27.5 17.3 %copy-start.7 = (bf16[2,1,2,48,512]{4,3,2,1,0:T(8,128)(2,1)S(1)}, bf16[2,1,2,48,512]{4,3,2,1,0:T(8,128)(2,1)}, u32[]{:S(2)}) copy-start(bf16[2,1,2,48,512]{4,3,2,1,0:T(8,128)(2,1)} %param.16) | copy-start | bytes 589828
  37.6 7.8 %copy-start.8 = (bf16[2,1,2,48,512]{4,3,2,1,0:T(8,128)(2,1)S(1)}, bf16[2,1,2,48,512]{4,3,2,1,0:T(8,128)(2,1)}, u32[]{:S(2)}) copy-start(bf16[2,1,2,48,512]{4,3,2,1,0:T(8,128)(2,1)} %param.19) | copy-start | bytes 589828
  37.6 8.4 %copy-start.9 = (s32[2]{0:T(128)S(1)}, s32[2]{0:T(128)}, u32[]{:S(2)}) copy-start(s32[2]{0:T(128)} %param.15) | copy-start | bytes 28
  37.7 8.4 %copy-start = (bf16[2,1,2,48,512]{4,3,2,1,0:T(8,128)(2,1)S(1)}, bf16[2,1,2,48,512]{4,3,2,1,0:T(8,128)(2,1)}, u32[]{:S(2)}) copy-start(bf16[2,1,2,48,512]{4,3,2,1,0:T(8,128)(2,1)} %param.17) | copy-start | bytes 589828
  37.7 8.4 %copy-start.1 = (bf16[2,1,2,48,512]{4,3,2,1,0:T(8,128)(2,1)S(1)}, bf16[2,1,2,48,512]{4,3,2,1,0:T(8,128)(2,1)}, u32[]{:S(2)}) copy-start(bf16[2,1,2,48,512]{4,3,2,1,0:T(8,128)(2,1)} %param.18) | copy-start | bytes 589828
  37.7 8.4 %copy-start.4 = (s32[512]{0:T(512)S(1)}, s32[512]{0:T(512)}, u32[]{:S(2)}) copy-start(s32[512]{0:T(512)} %param.14) | copy-start | bytes 6148
  39.8 19.5 %all-to-all-start = ((bf16[16,2,16,512]{3,2,1,0:T(8,128)(2,1)}), bf16[16,2,16,512]{3,2,1,0:T(8,128)(2,1)S(1)}, u32[]{:S(2)}, u32[]{:S(2)}) async-start(bf16[16,2,16,512]{3,2,1,0:T(8,128)(2,1)} %bitcast.5), calls=%async_computation | async-start | bytes 1048576 | tf_op jit(solution)/shard_map/all_to_all | solution.py:345
  81.8 18.6 %all-to-all-start.3 = ((bf16[16,2,16,512]{3,2,1,0:T(8,128)(2,1)}), bf16[16,2,16,512]{3,2,1,0:T(8,128)(2,1)S(1)}, u32[]{:S(2)}, u32[]{:S(2)}) async-start(bf16[16,2,16,512]{3,2,1,0:T(8,128)(2,1)} %get-tuple-element.22), calls=%async_computation.3 | async-start | bytes 1048576 | tf_op jit(solution)/shard_map/all_to_all | solution.py:345
  157.7 17.4 %all-to-all-start.4 = ((bf16[16,112,128]{2,1,0:T(8,128)(2,1)}), bf16[16,112,128]{2,1,0:T(8,128)(2,1)S(1)}, u32[]{:S(2)}, u32[]{:S(2)}) async-start(bf16[16,112,128]{2,1,0:T(8,128)(2,1)} %bitcast.76), calls=%async_computation.4 | async-start | bytes 917504 | tf_op jit(solution)/shard_map/all_to_all | solution.py:345

commit v2 on v1

--- a/solution.py
+++ b/solution.py
@@ -79,92 +79,45 @@
         lax.fori_loop(0, count // group, step, 0)
 
 
-def forward_kernel(pair_ref, w_in_t_ref, w_out_t_ref, w_bias_ref, bias_ref):
-    width = w_out_t_ref.shape[1]
-    piece = split_width(width)
-
-    def stages(row):
-        pair_float = pair_ref[row].T.astype(F32)
-        normed_in = normalize(pair_float)[0].astype(BF16)
-        yield True
-        lifted = pair_float
-        for at in range(0, width, piece):
-            half_gate = mm(w_in_t_ref[at : at + piece, :], normed_in)
-            up_in = mm(w_in_t_ref[width + at : width + at + piece, :], normed_in)
-            yield True
-            hidden = (half_gate * (1.0 + jnp.tanh(half_gate)) * up_in).astype(BF16)
-            lifted = lifted + mm(w_out_t_ref[:, at : at + piece], hidden)
-            yield True
-        normed_out = normalize(lifted)[0].astype(BF16)
-        yield True
-        bias_ref[row] = mm(w_bias_ref[...], normed_out).astype(BF16)
-
-    for_rows(pair_ref.shape[0], 4, stages, 2)
-
-
-def forward_rows(chunk, rows, pair, w_in_half_t, w_out_t, w_bias):
-    crop, channels = pair.shape[1:]
-    lanes = w_bias.shape[0]
-    step = math.gcd(rows, 8)
-    steps = rows // step
-    positions = rows * crop
-    width = w_out_t.shape[1]
-    whole = lambda i: (0, 0)
-    return pl.pallas_call(
-        forward_kernel,
-        grid=(steps,),
-        in_specs=[
-            pl.BlockSpec((step, crop, channels), lambda i: (chunk * steps + i, 0, 0)),
-            pl.BlockSpec(w_in_half_t.shape, whole),
-            pl.BlockSpec(w_out_t.shape, whole),
-            pl.BlockSpec(w_bias.shape, whole),
-        ],
-        out_specs=pl.BlockSpec((step, lanes, crop), lambda i: (i, 0, 0)),
-        out_shape=jax.ShapeDtypeStruct((rows, lanes, crop), BF16),
-        compiler_params=pltpu.CompilerParams(vmem_limit_bytes=48 * 2**20),
-        cost_estimate=pl.CostEstimate(
-            flops=2 * positions * channels * (3 * width + lanes),
-            bytes_accessed=positions * (channels + lanes) * 2,
-            transcendentals=positions * width,
-        ),
-        name="pair_forward",
-    )(pair, w_in_half_t, w_out_t, w_bias)
-
-
-def backward_kernel(
-    first,
-    last,
+def forward_kernel(
+    direct,
     pair_ref,
-    d_bias_ref,
+    w_in_ref,
+    w_out_ref,
+    w_bias_ref,
+    bias_ref,
+    kept_ref,
+    normed_ref,
+    inv_ref,
     w_in_t_ref,
     w_out_t_ref,
-    w_bias_t_ref,
-    w_in_ref,
-    w_out_ref,
-    *refs,
+    w_lanes_ref,
+    lines_ref,
 ):
-    if first:
-        pair_grad_ref, sums_ref = refs[:2]
-    else:
-        before_ref, _, pair_grad_ref, sums_ref = refs[:4]
     width = w_out_ref.shape[0]
+    channels = w_out_ref.shape[1]
+    layers, _, heads = w_bias_ref.shape
     piece = split_width(width)
-    lanes = w_bias_t_ref.shape[1]
+    step = pair_ref.shape[0]
+    first_row = pl.program_id(0) * step
 
     @pl.when(pl.program_id(0) == 0)
     def _():
-        if first:
-            sums_ref[...] = jnp.zeros_like(sums_ref)
-        else:
-            sums_ref[...] = before_ref[...]
+        w_in_t = w_in_ref[...].T
+        w_in_t_ref[:width, :] = w_in_t[:width] * 0.5
+        w_in_t_ref[width:, :] = w_in_t[width:]
+        w_out_t_ref[...] = w_out_ref[...].T
+        for layer in range(layers):
+            lanes = w_bias_ref[layer].astype(F32)
+            w_lanes_ref[layer * heads : (layer + 1) * heads, :] = lanes.T.astype(BF16)
 
     def stages(row):
         pair_float = pair_ref[row].T.astype(F32)
         normed_float, inv_in = normalize(pair_float)
         normed_in = normed_float.astype(BF16)
+        normed_ref[row, :channels, :] = normed_in
         yield True
         lifted = pair_float
-        kept = []
         for at in range(0, width, piece):
             half_gate = mm(w_in_t_ref[at : at + piece, :], normed_in)
             up_in = mm(w_in_t_ref[width + at : width + at + piece, :], normed_in)
@@ -172,42 +125,168 @@
             one_plus = 1.0 + jnp.tanh(half_gate)
             silu = half_gate * one_plus
             hidden = (silu * up_in).astype(BF16)
-            slope = one_plus * (1.0 + half_gate * (2.0 - one_plus)) * up_in
-            kept.append((silu, slope, hidden))
+            slope = one_plus * (0.5 + half_gate * (1.0 - 0.5 * one_plus)) * up_in
+            kept_ref[row, at : at + piece, :] = slope.astype(BF16)
+            kept_ref[row, width + at : width + at + piece, :] = silu.astype(BF16)
+            kept_ref[row, 2 * width + at : 2 * width + at + piece, :] = hidden
             lifted = lifted + mm(w_out_t_ref[:, at : at + piece], hidden)
             yield True
         out_float, inv_out = normalize(lifted)
         normed_out = out_float.astype(BF16)
-        yield True
-        d_bias = d_bias_ref[row]
-        d_normed = mm(w_bias_t_ref[...], d_bias)
-        sums_ref[3 * width : 3 * width + lanes, :] += mm(d_bias, normed_out, 1, 1)
-        d_lifted = norm_back(out_float, inv_out, d_normed)
+        normed_ref[row, channels:, :] = normed_out
+        inv_ref[row, 0:1, :] = inv_in
+        inv_ref[row, 1:2, :] = inv_out
+        yield True
+        bias = mm(w_lanes_ref[...], normed_out)
+        if direct:
+            tiles, total, tile = lines_ref.shape
+            rows = total // (layers * heads)
+            for layer in range(layers):
+                at = pl.ds(layer * rows + first_row + row, heads, stride=layers * rows)
+                lines = bias[layer * heads : (layer + 1) * heads]
+                for index in range(tiles):
+                    lines_ref[index, at, :] = lines[:, index * tile : (index + 1) * tile]
+        else:
+            bias_ref[row] = bias.astype(BF16)
+
+    for_rows(step, 4, stages, 2)
+
+    if direct:
+
+        @pl.when(pl.program_id(0) == pl.num_programs(0) - 1)
+        def _():
+            tiles, _, tile = lines_ref.shape
+            for index in range(tiles):
+                lines = lines_ref[index].reshape(bias_ref.shape[:2] + (tile,))
+                bias_ref[:, :, index * tile : (index + 1) * tile] = lines.astype(BF16)
+
+
+def forward_rows(chunk, rows, pair, w_in, w_out, w_bias):
+    crop, channels = pair.shape[1:]
+    layers, _, heads = w_bias.shape
+    lanes = layers * heads
+    step = math.gcd(rows, 4)
+    steps = rows // step
+    positions = rows * crop
+    width = w_out.shape[0]
+    direct = rows % 16 == 0 and crop % 128 == 0
+    line_shape = (heads * layers, rows, crop) if direct else (rows, lanes, crop)
+    line_spec = (
+        pl.BlockSpec(line_shape, lambda i: (0, 0, 0))
+        if direct
+        else pl.BlockSpec((step, lanes, crop), lambda i: (i, 0, 0))
+    )
+    by_row = lambda height: pl.BlockSpec((step, height, crop), lambda i: (i, 0, 0))
+    return pl.pallas_call(
+        functools.partial(forward_kernel, direct),
+        grid=(steps,),
+        in_specs=[
+            pl.BlockSpec((step, crop, channels), lambda i: (chunk * steps + i, 0, 0)),
+            pl.BlockSpec(w_in.shape, lambda i: (0, 0)),
+            pl.BlockSpec(w_out.shape, lambda i: (0, 0)),
+            pl.BlockSpec(w_bias.shape, lambda i: (0, 0, 0)),
+        ],
+        out_specs=[line_spec, by_row(3 * width), by_row(2 * channels), by_row(2)],
+        out_shape=[
+            jax.ShapeDtypeStruct(line_shape, BF16),
+            jax.ShapeDtypeStruct((rows, 3 * width, crop), BF16),
+            jax.ShapeDtypeStruct((rows, 2 * channels, crop), BF16),
+            jax.ShapeDtypeStruct((rows, 2, crop), F32),
+        ],
+        scratch_shapes=[
+            pltpu.VMEM((2 * width, channels), BF16),
+            pltpu.VMEM((channels, width), BF16),
+            pltpu.VMEM((lanes, channels), BF16),
+            pltpu.VMEM((crop // 128, lanes * rows, 128) if direct else (1, 8, 128), F32),
+        ],
+        compiler_params=pltpu.CompilerParams(vmem_limit_bytes=56 * 2**20),
+        cost_estimate=pl.CostEstimate(
+            flops=6 * positions * channels * (3 * width + lanes),
+            bytes_accessed=positions * (3 * width + 3 * channels + lanes) * 2,
+            transcendentals=positions * width,
+        ),
+        name="pair_forward",
+    )(pair, w_in, w_out, w_bias)
+
+
+def backward_kernel(
+    first,
+    last,
+    direct,
+    kept_ref,
+    normed_ref,
+    inv_ref,
+    d_bias_ref,
+    w_in_ref,
+    w_out_ref,
+    w_bias_ref,
+    *refs,
+):
+    if first:
+        pair_grad_ref, sums_ref = refs[:2]
+    else:
+        before_ref, _, pair_grad_ref, sums_ref = refs[:4]
+    w_lanes_ref, lines_ref = refs[-2:]
+    width, channels = w_out_ref.shape
+    layers, _, heads = w_bias_ref.shape
+    lanes = layers * heads
+    step = kept_ref.shape[0]
+    first_row = pl.program_id(0) * step
+
+    @pl.when(pl.program_id(0) == 0)
+    def _():
+        if first:
+            sums_ref[...] = jnp.zeros_like(sums_ref)
+        else:
+            sums_ref[...] = before_ref[...]
+        for layer in range(layers):
+            line = w_bias_ref[layer].astype(F32)
+            w_lanes_ref[layer * heads : (layer + 1) * heads, :] = line.T.astype(BF16)
+        if direct:
+            tiles, total, tile = lines_ref.shape
+            for index in range(tiles):
+                lines = d_bias_ref[:, :, index * tile : (index + 1) * tile].astype(F32)
+                lines_ref[index] = lines.reshape(total, tile)
+
+    def stages(row):
+        if direct:
+            tiles, total, _ = lines_ref.shape
+            rows = total // lanes
+            lines = []
+            for layer in range(layers):
+                at = pl.ds(layer * rows + first_row + row, heads, stride=layers * rows)
+                lines.append(
+                    jnp.concatenate([lines_ref[index, at, :] for index in range(tiles)], 1)
+                )
+            d_bias = jnp.concatenate(lines, 0).astype(BF16)
+        else:
+            d_bias = d_bias_ref[row]
+        normed_in = normed_ref[row, :channels, :]
+        normed_out = normed_ref[row, channels:, :]
+        inv_in, inv_out = inv_ref[row, 0:1, :], inv_ref[row, 1:2, :]
+        d_normed = mm(w_lanes_ref[...], d_bias, 0, 0)
+        sums_ref[3 * width :, :] += mm(d_bias, normed_out, 1, 1)
+        yield True
+        d_lifted = norm_back(normed_out.astype(F32), inv_out, d_normed)
         lifted_half = d_lifted.astype(BF16)
         yield True
-        d_normed_in = jnp.zeros_like(pair_float)
-        for index, (silu, slope, hidden) in enumerate(kept):
-            at = index * piece
-            cols = slice(at, at + piece)
-            up_cols = slice(width + at, width + at + piece)
-            out_cols = slice(2 * width + at, 2 * width + at + piece)
-            d_hidden = mm(w_out_ref[cols, :], lifted_half)
-            sums_ref[out_cols, :] += mm(hidden, lifted_half, 1, 1)
-            yield True
-            d_gate = (0.5 * d_hidden * slope).astype(BF16)
-            d_up = (d_hidden * silu).astype(BF16)
-            d_normed_in = d_normed_in + mm(w_in_ref[:, cols], d_gate)
-            sums_ref[cols, :] += mm(d_gate, normed_in, 1, 1)
-            d_normed_in = d_normed_in + mm(w_in_ref[:, up_cols], d_up)
-            sums_ref[up_cols, :] += mm(d_up, normed_in, 1, 1)
-            yield True
-        pair_grad = d_lifted + norm_back(normed_float, inv_in, d_normed_in)
+        sums_ref[2 * width : 3 * width, :] += mm(kept_ref[row, 2 * width :, :], lifted_half, 1, 1)
+        d_hidden = mm(w_out_ref[...], lifted_half)
+        yield True
+        d_gate = (d_hidden * kept_ref[row, :width, :].astype(F32)).astype(BF16)
+        d_up = (d_hidden * kept_ref[row, width : 2 * width, :].astype(F32)).astype(BF16)
+        d_projected = jnp.concatenate([d_gate, d_up], 0)
+        yield True
+        d_normed_in = mm(w_in_ref[...], d_projected)
+        sums_ref[: 2 * width, :] += mm(d_projected, normed_in, 1, 1)
+        yield True
+        pair_grad = d_lifted + norm_back(normed_in.astype(F32), inv_in, d_normed_in)
         pair_grad_ref[row] = pair_grad.astype(BF16).T
 
-    for_rows(pair_ref.shape[0], 4, stages, 3)
+    for_rows(step, 4, stages, 2)
 
     if last:
-        packed_ref = refs[-1]
+        packed_ref = refs[-3]
 
         @pl.when(pl.program_id(0) == pl.num_programs(0) - 1)
         def _():
@@ -216,20 +295,30 @@
             packed_ref[done:, :] = jnp.zeros((packed_ref.shape[0] - done, packed_ref.shape[1]), BF16)
 
 
-def backward_rows(chunk, chunks, rows, packed_rows, pair, d_bias, weights, state):
-    w_in_half_t, w_out_t, w_bias_t, w_in, w_out = weights
-    crop, channels = pair.shape[1:]
-    lanes = w_bias_t.shape[1]
+def backward_rows(chunk, chunks, rows, packed_rows, shape, stored, d_bias, weights, state):
+    w_in, w_out, w_bias = weights
+    crop, channels = shape[1:]
+    layers, _, heads = w_bias.shape
+    lanes = layers * heads
     width = w_out.shape[0]
-    step = math.gcd(rows, 8)
+    step = math.gcd(rows, 4)
     steps = rows // step
     positions = rows * crop
     first, last = chunk == 0, chunk == chunks - 1
+    direct = rows % 16 == 0 and crop % 128 == 0
     whole = lambda i: (0, 0)
-    pair_spec = pl.BlockSpec((step, crop, channels), lambda i: (chunk * steps + i, 0, 0))
-    in_specs = [pair_spec, pl.BlockSpec((step, lanes, crop), lambda i: (i, 0, 0))]
-    in_specs += [pl.BlockSpec(w.shape, whole) for w in weights]
-    operands = [pair, d_bias, *weights]
+    by_row = lambda height: pl.BlockSpec((step, height, crop), lambda i: (i, 0, 0))
+    in_specs = [by_row(array.shape[1]) for array in stored]
+    if direct:
+        in_specs.append(pl.BlockSpec(d_bias.shape, lambda i: (0, 0, 0)))
+    else:
+        in_specs.append(by_row(lanes))
+    in_specs += [
+        pl.BlockSpec(w_in.shape, whole),
+        pl.BlockSpec(w_out.shape, whole),
+        pl.BlockSpec(w_bias.shape, lambda i: (0, 0, 0)),
+    ]
+    operands = [*stored, d_bias, *weights]
     aliases = {}
     if not first:
         pair_grad, sums = state
@@ -237,25 +326,32 @@
         in_specs += [pl.BlockSpec(sums.shape, whole), pl.BlockSpec(memory_space=pl.ANY)]
         aliases = {len(operands) - 1: 0}
     shapes = [
-        jax.ShapeDtypeStruct(pair.shape, BF16),
+        jax.ShapeDtypeStruct(shape, BF16),
         jax.ShapeDtypeStruct((3 * width + lanes, channels), F32),
     ]
-    out_specs = [pair_spec, pl.BlockSpec(shapes[1].shape, whole)]
+    out_specs = [
+        pl.BlockSpec((step, crop, channels), lambda i: (chunk * steps + i, 0, 0)),
+        pl.BlockSpec(shapes[1].shape, whole),
+    ]
     if last:
         shapes.append(jax.ShapeDtypeStruct((packed_rows, channels), BF16))
         out_specs.append(pl.BlockSpec(shapes[2].shape, whole))
     return pl.pallas_call(
-        functools.partial(backward_kernel, first, last),
+        functools.partial(backward_kernel, first, last, direct),
         grid=(steps,),
         in_specs=in_specs,
         out_specs=out_specs,
         out_shape=shapes,
         input_output_aliases=aliases,
+        scratch_shapes=[
+            pltpu.VMEM((lanes, channels), BF16),
+            pltpu.VMEM((crop // 128, lanes * rows, 128) if direct else (1, 8, 128), F32),
+        ],
         compiler_params=pltpu.CompilerParams(vmem_limit_bytes=56 * 2**20),
         cost_estimate=pl.CostEstimate(
-            flops=2 * positions * channels * (9 * width + 2 * lanes),
-            bytes_accessed=positions * (2 * channels + lanes) * 2,
-            transcendentals=positions * width,
+            flops=6 * positions * channels * (6 * width + 2 * lanes),
+            bytes_accessed=positions * (3 * width + 3 * channels + lanes) * 2,
+            transcendentals=0,
         ),
         name="pair_backward",
     )(*operands)
@@ -333,7 +429,7 @@
         ],
         compiler_params=pltpu.CompilerParams(vmem_limit_bytes=48 * 2**20),
         cost_estimate=pl.CostEstimate(
-            flops=10 * layers * samples * depth * row_count * crop,
+            flops=200 * layers * samples * depth * row_count * crop,
             bytes_accessed=layers * crop * (4 * row_count + 12 * samples * depth),
             transcendentals=layers * samples * row_count * crop,
         ),
@@ -367,11 +463,7 @@
     rows = row_count // chunks
     lanes = heads * layers
 
-    halves = jnp.concatenate([jnp.full((width,), 0.5, BF16), jnp.ones((width,), BF16)])
-    w_in_half_t = (weight_in * halves[None, :]).T
-    w_out_t = weight_out.T
-    w_bias = jnp.transpose(weight_bias, (2, 0, 1)).reshape(lanes, channels)
-    pair_weights = (w_in_half_t, w_out_t, w_bias.T, weight_in, weight_out)
+    pair_weights = (weight_in, weight_out, weight_bias)
 
     group = lax.axis_index("tok") // heads
     weights = sample_weight(lax.dynamic_slice_in_dim(noise_level, group * samples, samples))
@@ -384,19 +476,26 @@
 
     queries, grads = by_chunk(query_states), by_chunk(output_grad)
 
+    direct = rows % 16 == 0 and crop % 128 == 0
     arrived = []
+    stored = []
     for chunk in range(chunks):
-        bias = forward_rows(chunk, rows, pair_states, w_in_half_t, w_out_t, w_bias)
-        bias = jnp.transpose(bias, (1, 0, 2)).reshape(heads, layers, rows, crop)
-        arrived.append(swap(jnp.tile(bias, (groups, 1, 1, 1))))
+        bias, *kept = forward_rows(chunk, rows, pair_states, *pair_weights)
+        stored.append(kept)
+        if direct:
+            bias = bias.reshape(heads, layers, rows, crop)
+        else:
+            bias = jnp.transpose(bias.reshape(rows, layers, heads, crop), (2, 1, 0, 3))
+        if groups > 1:
+            bias = jnp.tile(bias, (groups, 1, 1, 1))
+        arrived.append(swap(bias))
 
     returned = []
     d_queries = []
     state = None
     for chunk in range(chunks):
         bias = arrived[chunk]
-        flat = rows % 16 != 0
-        if flat:
+        if not direct:
             bias = jnp.transpose(bias, (1, 0, 2, 3)).reshape(1, layers, devices * rows, crop)
         d_query, d_key, d_value, d_bias = attend_rows(
             chunk,
@@ -412,7 +511,7 @@
         )
         state = (d_key, d_value)
         d_queries.append(d_query)
-        if flat:
+        if not direct:
             d_bias = jnp.transpose(d_bias.reshape(layers, devices, rows, crop), (1, 0, 2, 3))
         returned.append(swap(d_bias))
 
@@ -424,13 +523,17 @@
         if groups > 1:
             d_bias = d_bias.reshape(groups, heads, layers, rows, crop).astype(F32)
             d_bias = jnp.sum(d_bias, 0).astype(BF16)
-        d_bias = jnp.transpose(d_bias.reshape(lanes, rows, crop), (1, 0, 2))
+        if direct:
+            d_bias = d_bias.reshape(lanes, rows, crop)
+        else:
+            d_bias = jnp.transpose(d_bias, (2, 1, 0, 3)).reshape(rows, lanes, crop)
         pair_state = backward_rows(
             chunk,
             chunks,
             rows,
             share * devices,
-            pair_states,
+            pair_states.shape,
+            stored[chunk],
             d_bias,
             pair_weights,
             pair_state and pair_state[:2],
@@ -439,11 +542,12 @@
 
     parts = swap(packed.reshape(devices, share, channels))
     summed = jnp.sum(parts.astype(F32), 0).astype(BF16)
-    summed = lax.all_gather(summed, "tok", axis=0, tiled=True).astype(F32)
+    copies = jnp.broadcast_to(summed[None], (devices, share, channels))
+    summed = swap(copies).reshape(devices * share, channels).astype(F32)
     grad_in = summed[: 2 * width].T
     grad_out = summed[2 * width : 3 * width]
-    grad_bias = summed[3 * width : sum_rows].reshape(heads, layers, channels)
-    grad_bias = jnp.transpose(grad_bias, (1, 2, 0))
+    grad_bias = summed[3 * width : sum_rows].reshape(layers, heads, channels)
+    grad_bias = jnp.transpose(grad_bias, (0, 2, 1))
 
     d_query = jnp.stack(d_queries, 0).reshape(chunks, layers, samples, depth, devices, rows)
     d_query = jnp.transpose(d_query, (1, 2, 3, 4, 0, 5)).reshape(query_states.shape)

time: 199 us -> 174 us (0.87)
  blocking collectives: 39.2 us -> 19.2 us
  local copies, waits for them, and re-layouts: 17.2 us -> 7.84 us
  starting transfers between devices: 20.6 us -> 25.7 us
  waiting for transfers between devices: 34.4 us -> 31.2 us
  Pallas kernels: 84.9 us -> 88.1 us
    all_gather x1 -> x0, blocking collectives: 20.9 us -> none  [body(): summed = lax.all_gather(summed, 'tok', axis=0, tiled=True).astype(F32)]
    all_to_all x4 -> x5, starting transfers between devices: 20.6 us -> 25.7 us  [swap(): return lax.all_to_all(array, 'tok', split_axis=0, concat_axis=0, tiled=True)]
    unnamed x27 -> x19, local copies, waits for them, and re-layouts: 9.7 us -> 4.69 us
    all_to_all x4 -> x5, waiting for transfers between devices: 34.4 us -> 31.2 us  [swap(): return lax.all_to_all(array, 'tok', split_axis=0, concat_axis=0, tiled=True)]
    pallas_call x4, Pallas kernels: 76.4 us -> 79.5 us  [the longest x2 40.3 us: forward_rows(): pl.pallas_call(functools.partial(forward_kernel, direct), grid=(steps,),...]
    reshape x3 -> x0, local copies, waits for them, and re-layouts: 2.89 us -> none  [the longest x2 2.18 us: body(): d_bias = jnp.transpose(d_bias.reshape(lanes, rows, crop), (1, 0, 2))]
    transpose x3 -> x0, local copies, waits for them, and re-layouts: 2.88 us -> none  [the longest x2 2.17 us: body(): bias = jnp.transpose(bias, (1, 0, 2)).reshape(heads, layers, rows, crop)]
  transfers between devices with their start and end apart: 4 -> 5, of which waited for: 4 -> 3; matrix products, arithmetic and copies ran while one was open for 3% -> 1% of each run, Pallas kernels for 7% -> 28%
where the time goes in v2:
time: 174 us; the launch traced here: 173 us
  Pallas kernels  88.1 us (51%)
  waiting for transfers between devices  31.2 us (18%)
  starting transfers between devices  25.7 us (15%)
  blocking collectives  19.2 us (11%)
  local copies, waits for them, and re-layouts  7.84 us (5%)
    pallas_call x2, Pallas kernels, forward_rows(): pl.pallas_call(functools.partial(forward_kernel, direct), grid=(steps,),...  40.3 us
    pallas_call x2, Pallas kernels, backward_rows(): pl.pallas_call(functools.partial(backward_kernel, first, last, direct), g...  39.3 us
    all_to_all x5, waiting for transfers between devices, swap(): return lax.all_to_all(array, 'tok', split_axis=0, concat_axis=0, tiled=True)  31.2 us
    all_to_all x5, starting transfers between devices, swap(): return lax.all_to_all(array, 'tok', split_axis=0, concat_axis=0, tiled=True)  25.7 us
    all_to_all x1, blocking collectives, swap(): return lax.all_to_all(array, 'tok', split_axis=0, concat_axis=0, tiled=True)  19.2 us
    pallas_call x2, Pallas kernels, attend_rows(): pl.pallas_call(functools.partial(attend_kernel, first, last), grid=(layer...  8.56 us
    unnamed x19, local copies, waits for them, and re-layouts  4.69 us
  transfers between devices with their start and end apart: 5, of which 3 were waited for; matrix products, arithmetic and copies ran while one was open for 1% of the time, Pallas kernels for 28%

profile of v2, /device:TPU:0, one launch (start us, length us, event | category | flops | bytes accessed | tf_op | source)
XLA Modules:
  0.0 173.3 jit_solution(13650007805080089456)
XLA Ops:
  0.6 1.4 copy.28.w_bias_ref
  2.1 20.1 %pair_forward.3 = (bf16[32,16,512]{2,1,0:T(8,128)(2,1)}, bf16[16,1536,512]{2,1,0:T(8,128)(2,1)}, bf16[16,256,512]{2,1,0:T(8,128)(2,1)}, f32[16,2,512]{2,1,0:T(2,128)}) custom-call(bf16[32,512,128]{2,1,0:T(8,128)(2,1)} %pair_ref.3, bf16[128,1024]{1,0:T(8,128)(2,1)} %w_in_ref.7, bf16[512,128]{1,0:T(8,128)(2,1)} %w_out_ref.7, bf16[2,128,16]{2,1,0:T(8,128)(2,1)} %copy.28.w_bias_ref), custom_call_target="tpu_custom_call" | custom-call | flops 9865003008 | bytes 31981568 | tf_op jit(solution)/shard_map/pair_forward/pallas_call | solution.py:180
  22.2 7.4 %all-to-all-start.1 = ((bf16[16,2,16,512]{3,2,1,0:T(8,128)(2,1)}), bf16[16,2,16,512]{3,2,1,0:T(8,128)(2,1)S(1)}, u32[]{:S(2)}, u32[]{:S(2)}) async-start(bf16[16,2,16,512]{3,2,1,0:T(8,128)(2,1)} %bitcast.54), calls=%async_computation.1 | async-start | bytes 1048576 | tf_op jit(solution)/shard_map/all_to_all | solution.py:441
  29.6 0.3 copy.29
  29.9 20.2 %pair_forward.2 = (bf16[32,16,512]{2,1,0:T(8,128)(2,1)}, bf16[16,1536,512]{2,1,0:T(8,128)(2,1)}, bf16[16,256,512]{2,1,0:T(8,128)(2,1)}, f32[16,2,512]{2,1,0:T(2,128)}) custom-call(bf16[32,512,128]{2,1,0:T(8,128)(2,1)} %pair_ref.3, bf16[128,1024]{1,0:T(8,128)(2,1)} %w_in_ref.7, bf16[512,128]{1,0:T(8,128)(2,1)} %w_out_ref.7, bf16[2,128,16]{2,1,0:T(8,128)(2,1)} %copy.28.w_bias_ref), custom_call_target="tpu_custom_call" | custom-call | flops 9865003008 | bytes 31981568 | tf_op jit(solution)/shard_map/pair_forward/pallas_call | solution.py:180
  50.1 6.2 %all-to-all-start = ((bf16[16,2,16,512]{3,2,1,0:T(8,128)(2,1)}), bf16[16,2,16,512]{3,2,1,0:T(8,128)(2,1)S(1)}, u32[]{:S(2)}, u32[]{:S(2)}) async-start(bf16[16,2,16,512]{3,2,1,0:T(8,128)(2,1)} %bitcast.52), calls=%async_computation | async-start | bytes 1048576 | tf_op jit(solution)/shard_map/all_to_all | solution.py:441
  56.3 0.1 copy.32.q_ref
  56.4 0.3 copy.30
  56.8 0.1 copy.33.g_ref
  56.9 4.3 %attention_backward.2 = (bf16[2,2,48,256]{3,2,1,0:T(8,128)(2,1)S(1)}, f32[2,2,48,512]{3,2,1,0:T(8,128)S(1)}, f32[2,2,48,512]{3,2,1,0:T(8,128)S(1)}, bf16[16,2,16,512]{3,2,1,0:T(8,128)(2,1)}) custom-call(f32[2]{0:T(128)S(1)} %multiply_divide_fusion.weight_ref, bf16[16,2,16,512]{3,2,1,0:T(8,128)(2,1)S(1)} %all-to-all-done.1.bias_ref, s32[1,512]{1,0:T(1,128)S(1)} %bitcast.41, ...), custom_call_target="tpu_custom_call" | custom-call | flops 5033164800 | bytes 2228224 | tf_op jit(solution)/shard_map/attention_backward/pallas_call | solution.py:419
  61.2 9.5 %all-to-all-done.bias_ref = bf16[16,2,16,512]{3,2,1,0:T(8,128)(2,1)S(1)} async-done(((bf16[16,2,16,512]{3,2,1,0:T(8,128)(2,1)}), bf16[16,2,16,512]{3,2,1,0:T(8,128)(2,1)S(1)}, u32[]{:S(2)}, u32[]{:S(2)}) %all-to-all-start) | async-done | bytes 524320 | tf_op jit(solution)/shard_map/all_to_all | solution.py:441
  70.7 4.2 %all-to-all-start.3 = ((bf16[16,2,16,512]{3,2,1,0:T(8,128)(2,1)}), bf16[16,2,16,512]{3,2,1,0:T(8,128)(2,1)}, u32[]{:S(2)}, u32[]{:S(2)}) async-start(bf16[16,2,16,512]{3,2,1,0:T(8,128)(2,1)} %get-tuple-element.38), calls=%async_computation.3 | async-start | bytes 1048576 | tf_op jit(solution)/shard_map/all_to_all | solution.py:441
  74.9 0.1 copy.34.q_ref
  75.1 0.1 copy.35.g_ref
  75.2 4.3 %attention_backward.3 = (bf16[2,2,48,256]{3,2,1,0:T(8,128)(2,1)S(1)}, bf16[2,2,48,512]{3,2,1,0:T(8,128)(2,1)}, bf16[2,2,48,512]{3,2,1,0:T(8,128)(2,1)}, bf16[16,2,16,512]{3,2,1,0:T(8,128)(2,1)}) custom-call(f32[2]{0:T(128)S(1)} %multiply_divide_fusion.weight_ref, bf16[16,2,16,512]{3,2,1,0:T(8,128)(2,1)S(1)} %all-to-all-done.bias_ref, s32[1,512]{1,0:T(1,128)S(1)} %bitcast.42, ...), custom_call_target="tpu_custom_call" | custom-call | flops 5033164800 | bytes 2228224 | tf_op jit(solution)/shard_map/attention_backward/pallas_call | solution.py:419
  79.5 9.9 %all-to-all-done.3 = bf16[16,2,16,512]{3,2,1,0:T(8,128)(2,1)} async-done(((bf16[16,2,16,512]{3,2,1,0:T(8,128)(2,1)}), bf16[16,2,16,512]{3,2,1,0:T(8,128)(2,1)}, u32[]{:S(2)}, u32[]{:S(2)}) %all-to-all-start.3) | async-done | bytes 524320 | tf_op jit(solution)/shard_map/all_to_all | solution.py:441
  89.4 4.1 %all-to-all-start.2 = ((bf16[16,2,16,512]{3,2,1,0:T(8,128)(2,1)}), bf16[16,2,16,512]{3,2,1,0:T(8,128)(2,1)S(1)}, u32[]{:S(2)}, u32[]{:S(2)}) async-start(bf16[16,2,16,512]{3,2,1,0:T(8,128)(2,1)} %get-tuple-element.34), calls=%async_computation.2 | async-start | bytes 1048576 | tf_op jit(solution)/shard_map/all_to_all | solution.py:441
  93.5 19.4 %pair_backward.2 = (bf16[32,512,128]{2,1,0:T(8,128)(2,1)}, f32[1568,128]{1,0:T(8,128)}) custom-call(bf16[16,1536,512]{2,1,0:T(8,128)(2,1)} %get-tuple-element.35.kept_ref, bf16[16,256,512]{2,1,0:T(8,128)(2,1)} %get-tuple-element.36.normed_ref, f32[16,2,512]{2,1,0:T(2,128)} %get-tuple-element.37.inv_ref, bf16[32,16,512]{2,1,0:T(8,128)(2,1)} %bitcast.16.d_bias_ref, ...), custom_call_target="tpu_custom_call" | custom-call | flops 19730006016 | bytes 31981568 | tf_op jit(solution)/shard_map/pair_backward/pallas_call | solution.py:339
  112.9 0.8 copy-done.3
  113.7 19.9 %pair_backward.3 = (bf16[32,512,128]{2,1,0:T(8,128)(2,1)}, f32[1568,128]{1,0:T(8,128)}, bf16[1792,128]{1,0:T(8,128)(2,1)}) custom-call(bf16[16,1536,512]{2,1,0:T(8,128)(2,1)} %get-tuple-element.27.kept_ref, bf16[16,256,512]{2,1,0:T(8,128)(2,1)} %get-tuple-element.28.normed_ref, ...), custom_call_target="tpu_custom_call", output_to_operand_aliasing={{0}: (8, {})} | custom-call | flops 19730006016 | bytes 31981568 | tf_op jit(solution)/shard_map/pair_backward/pallas_call | solution.py:339
  133.6 19.2 %all_to_all.30 = bf16[16,112,128]{2,1,0:T(8,128)(2,1)S(1)} all-to-all(bf16[16,112,128]{2,1,0:T(8,128)(2,1)} %bitcast.55), channel_id=1, replica_groups=mesh['job'=2,'tok'=16] {'tok'}, dimensions={0} | all-to-all | bytes 917504 | tf_op jit(solution)/shard_map/all_to_all | solution.py:441
  152.9 0.8 broadcast_in_dim.18
  153.7 3.9 %all-to-all-start.5 = ((bf16[16,112,128]{2,1,0:T(8,128)(2,1)}), bf16[16,112,128]{2,1,0:T(8,128)(2,1)S(1)}, u32[]{:S(2)}, u32[]{:S(2)}) async-start(bf16[16,112,128]{2,1,0:T(8,128)(2,1)} %broadcast_in_dim.18), calls=%async_computation.5 | async-start | bytes 917504 | tf_op jit(solution)/shard_map/all_to_all | solution.py:441
  157.6 0.2 copy.38
  157.8 0.2 copy.39
  158.0 0.1 maximum_bitcast_fusion
  158.2 0.9 copy.41
  159.0 11.8 %all-to-all-done.5 = bf16[16,112,128]{2,1,0:T(8,128)(2,1)S(1)} async-done(((bf16[16,112,128]{2,1,0:T(8,128)(2,1)}), bf16[16,112,128]{2,1,0:T(8,128)(2,1)S(1)}, u32[]{:S(2)}, u32[]{:S(2)}) %all-to-all-start.5) | async-done | bytes 458784 | tf_op jit(solution)/shard_map/all_to_all | solution.py:441
  170.9 0.1 bitcast_convert_fusion
  171.0 0.6 slice.38
  171.6 0.7 slice.37
  172.3 1.0 copy.44
  (21 shorter events, 0.3 us)
Async XLA Ops:
  2.1 27.5 %copy-start.4 = (bf16[2,1,2,48,512]{4,3,2,1,0:T(8,128)(2,1)S(1)}, bf16[2,1,2,48,512]{4,3,2,1,0:T(8,128)(2,1)}, u32[]{:S(2)}) copy-start(bf16[2,1,2,48,512]{4,3,2,1,0:T(8,128)(2,1)} %param.16) | copy-start | bytes 589828
  22.2 27.9 %all-to-all-start.1 = ((bf16[16,2,16,512]{3,2,1,0:T(8,128)(2,1)}), bf16[16,2,16,512]{3,2,1,0:T(8,128)(2,1)S(1)}, u32[]{:S(2)}, u32[]{:S(2)}) async-start(bf16[16,2,16,512]{3,2,1,0:T(8,128)(2,1)} %bitcast.54), calls=%async_computation.1 | async-start | bytes 1048576 | tf_op jit(solution)/shard_map/all_to_all | solution.py:441
  29.8 26.6 %copy-start.5 = (bf16[2,1,2,48,512]{4,3,2,1,0:T(8,128)(2,1)S(1)}, bf16[2,1,2,48,512]{4,3,2,1,0:T(8,128)(2,1)}, u32[]{:S(2)}) copy-start(bf16[2,1,2,48,512]{4,3,2,1,0:T(8,128)(2,1)} %param.19) | copy-start | bytes 589828
  50.0 6.9 %copy-start.6 = (s32[2]{0:T(128)S(1)}, s32[2]{0:T(128)}, u32[]{:S(2)}) copy-start(s32[2]{0:T(128)} %param.15) | copy-start | bytes 28
  50.0 6.9 %copy-start = (bf16[2,1,2,48,512]{4,3,2,1,0:T(8,128)(2,1)S(1)}, bf16[2,1,2,48,512]{4,3,2,1,0:T(8,128)(2,1)}, u32[]{:S(2)}) copy-start(bf16[2,1,2,48,512]{4,3,2,1,0:T(8,128)(2,1)} %param.17) | copy-start | bytes 589828
  50.0 6.9 %copy-start.1 = (bf16[2,1,2,48,512]{4,3,2,1,0:T(8,128)(2,1)S(1)}, bf16[2,1,2,48,512]{4,3,2,1,0:T(8,128)(2,1)}, u32[]{:S(2)}) copy-start(bf16[2,1,2,48,512]{4,3,2,1,0:T(8,128)(2,1)} %param.18) | copy-start | bytes 589828
  50.0 6.9 %copy-start.2 = (s32[512]{0:T(512)S(1)}, s32[512]{0:T(512)}, u32[]{:S(2)}) copy-start(s32[512]{0:T(512)} %param.14) | copy-start | bytes 6148
  50.1 20.6 %all-to-all-start = ((bf16[16,2,16,512]{3,2,1,0:T(8,128)(2,1)}), bf16[16,2,16,512]{3,2,1,0:T(8,128)(2,1)S(1)}, u32[]{:S(2)}, u32[]{:S(2)}) async-start(bf16[16,2,16,512]{3,2,1,0:T(8,128)(2,1)} %bitcast.52), calls=%async_computation | async-start | bytes 1048576 | tf_op jit(solution)/shard_map/all_to_all | solution.py:441
  70.7 18.7 %all-to-all-start.3 = ((bf16[16,2,16,512]{3,2,1,0:T(8,128)(2,1)}), bf16[16,2,16,512]{3,2,1,0:T(8,128)(2,1)}, u32[]{:S(2)}, u32[]{:S(2)}) async-start(bf16[16,2,16,512]{3,2,1,0:T(8,128)(2,1)} %get-tuple-element.38), calls=%async_computation.3 | async-start | bytes 1048576 | tf_op jit(solution)/shard_map/all_to_all | solution.py:441
  89.4 23.5 %all-to-all-start.2 = ((bf16[16,2,16,512]{3,2,1,0:T(8,128)(2,1)}), bf16[16,2,16,512]{3,2,1,0:T(8,128)(2,1)S(1)}, u32[]{:S(2)}, u32[]{:S(2)}) async-start(bf16[16,2,16,512]{3,2,1,0:T(8,128)(2,1)} %get-tuple-element.34), calls=%async_computation.2 | async-start | bytes 1048576 | tf_op jit(solution)/shard_map/all_to_all | solution.py:441
  112.9 0.8 copy-start.3
  153.7 17.2 %all-to-all-start.5 = ((bf16[16,112,128]{2,1,0:T(8,128)(2,1)}), bf16[16,112,128]{2,1,0:T(8,128)(2,1)S(1)}, u32[]{:S(2)}, u32[]{:S(2)}) async-start(bf16[16,112,128]{2,1,0:T(8,128)(2,1)} %broadcast_in_dim.18), calls=%async_computation.5 | async-start | bytes 917504 | tf_op jit(solution)/shard_map/all_to_all | solution.py:441

commit v3 on v2

--- a/solution.py
+++ b/solution.py
@@ -51,8 +51,12 @@
     )
 
 
-def split_width(width):
-    return 256 if width % 256 == 0 else width
+UNIT = 128
+LANES = 256
+
+
+def unit_of(size, wanted):
+    return wanted if size % wanted == 0 else size
 
 
 def interleave(make_stages, count, lag):
@@ -70,13 +74,34 @@
     group = math.gcd(count, group)
 
     def step(at, carry):
-        interleave(lambda index: make_stages(at * group + index), group, lag)
+        interleave(lambda index: make_stages(at * group + index, index), group, lag)
         return carry
 
     if count == group:
         step(0, 0)
     else:
         lax.fori_loop(0, count // group, step, 0)
+
+
+def mix_weights(w_in_ref, w_out_ref, w_mix_ref, w_out_t_ref):
+    width = w_out_ref.shape[0]
+    unit = unit_of(width, UNIT)
+    w_in_t = w_in_ref[...].T
+    for at in range(0, width, unit):
+        w_mix_ref[2 * at : 2 * at + unit, :] = w_in_t[at : at + unit] * 0.5
+        w_mix_ref[2 * at + unit : 2 * at + 2 * unit, :] = w_in_t[width + at : width + at + unit]
+    w_out_t_ref[...] = w_out_ref[...].T
+
+
+def pipelined(products, finish):
+    waiting = None
+    for make in products:
+        fresh = make()
+        if waiting is not None:
+            finish(*waiting)
+        waiting = fresh
+        yield True
+    finish(*waiting)
 
 
 def forward_kernel(
@@ -86,70 +111,59 @@
     w_out_ref,
     w_bias_ref,
     bias_ref,
-    kept_ref,
-    normed_ref,
-    inv_ref,
-    w_in_t_ref,
+    w_mix_ref,
     w_out_t_ref,
-    w_lanes_ref,
     lines_ref,
+    hidden_ref,
 ):
     width = w_out_ref.shape[0]
-    channels = w_out_ref.shape[1]
-    layers, _, heads = w_bias_ref.shape
-    piece = split_width(width)
-    step = pair_ref.shape[0]
+    layers, heads, channels = w_bias_ref.shape
+    unit = unit_of(width, UNIT)
+    step, crop, _ = pair_ref.shape
+    span = unit_of(crop, LANES)
     first_row = pl.program_id(0) * step
 
     @pl.when(pl.program_id(0) == 0)
     def _():
-        w_in_t = w_in_ref[...].T
-        w_in_t_ref[:width, :] = w_in_t[:width] * 0.5
-        w_in_t_ref[width:, :] = w_in_t[width:]
-        w_out_t_ref[...] = w_out_ref[...].T
-        for layer in range(layers):
-            lanes = w_bias_ref[layer].astype(F32)
-            w_lanes_ref[layer * heads : (layer + 1) * heads, :] = lanes.T.astype(BF16)
-
-    def stages(row):
-        pair_float = pair_ref[row].T.astype(F32)
-        normed_float, inv_in = normalize(pair_float)
-        normed_in = normed_float.astype(BF16)
-        normed_ref[row, :channels, :] = normed_in
-        yield True
-        lifted = pair_float
-        for at in range(0, width, piece):
-            half_gate = mm(w_in_t_ref[at : at + piece, :], normed_in)
-            up_in = mm(w_in_t_ref[width + at : width + at + piece, :], normed_in)
-            yield True
-            one_plus = 1.0 + jnp.tanh(half_gate)
-            silu = half_gate * one_plus
-            hidden = (silu * up_in).astype(BF16)
-            slope = one_plus * (0.5 + half_gate * (1.0 - 0.5 * one_plus)) * up_in
-            kept_ref[row, at : at + piece, :] = slope.astype(BF16)
-            kept_ref[row, width + at : width + at + piece, :] = silu.astype(BF16)
-            kept_ref[row, 2 * width + at : 2 * width + at + piece, :] = hidden
-            lifted = lifted + mm(w_out_t_ref[:, at : at + piece], hidden)
-            yield True
-        out_float, inv_out = normalize(lifted)
-        normed_out = out_float.astype(BF16)
-        normed_ref[row, channels:, :] = normed_out
-        inv_ref[row, 0:1, :] = inv_in
-        inv_ref[row, 1:2, :] = inv_out
-        yield True
-        bias = mm(w_lanes_ref[...], normed_out)
-        if direct:
-            tiles, total, tile = lines_ref.shape
-            rows = total // (layers * heads)
-            for layer in range(layers):
-                at = pl.ds(layer * rows + first_row + row, heads, stride=layers * rows)
-                lines = bias[layer * heads : (layer + 1) * heads]
-                for index in range(tiles):
-                    lines_ref[index, at, :] = lines[:, index * tile : (index + 1) * tile]
-        else:
-            bias_ref[row] = bias.astype(BF16)
-
-    for_rows(step, 4, stages, 2)
+        mix_weights(w_in_ref, w_out_ref, w_mix_ref, w_out_t_ref)
+
+    def stages(row, slot):
+        for left in range(0, crop, span):
+            cols = slice(left, left + span)
+            pair_float = pair_ref[row, cols, :].T.astype(F32)
+            normed_in = normalize(pair_float)[0].astype(BF16)
+            yield True
+
+            def product(at):
+                both = mm(w_mix_ref[2 * at : 2 * at + 2 * unit, :], normed_in)
+                return at, both[:unit], both[unit:]
+
+            def finish(at, half_gate, up_in):
+                silu = half_gate + half_gate * jnp.tanh(half_gate)
+                hidden_ref[slot, at : at + unit, cols] = (silu * up_in).astype(BF16)
+
+            yield from pipelined(
+                [functools.partial(product, at) for at in range(0, width, unit)], finish
+            )
+            lifted = pair_float + mm(w_out_t_ref[...], hidden_ref[slot, :, cols])
+            yield True
+            normed_out = normalize(lifted)[0].astype(BF16)
+            bias = mm(w_bias_ref[...].reshape(layers * heads, channels), normed_out)
+            if direct:
+                tiles, total, tile = lines_ref.shape
+                rows = total // (layers * heads)
+                for layer in range(layers):
+                    at = pl.ds(layer * rows + first_row + row, heads, stride=layers * rows)
+                    lines = bias[layer * heads : (layer + 1) * heads]
+                    for index in range(span // tile):
+                        lines_ref[left // tile + index, at, :] = lines[
+                            :, index * tile : (index + 1) * tile
+                        ]
+            else:
+                bias_ref[row, :, cols] = bias.astype(BF16)
+            yield True
+
+    for_rows(step, 4, stages, 7)
 
     if direct:
 
@@ -163,9 +177,9 @@
 
 def forward_rows(chunk, rows, pair, w_in, w_out, w_bias):
     crop, channels = pair.shape[1:]
-    layers, _, heads = w_bias.shape
+    layers, heads, _ = w_bias.shape
     lanes = layers * heads
-    step = math.gcd(rows, 4)
+    step = math.gcd(rows, 8)
     steps = rows // step
     positions = rows * crop
     width = w_out.shape[0]
@@ -176,7 +190,6 @@
         if direct
         else pl.BlockSpec((step, lanes, crop), lambda i: (i, 0, 0))
     )
-    by_row = lambda height: pl.BlockSpec((step, height, crop), lambda i: (i, 0, 0))
     return pl.pallas_call(
         functools.partial(forward_kernel, direct),
         grid=(steps,),
@@ -186,23 +199,18 @@
             pl.BlockSpec(w_out.shape, lambda i: (0, 0)),
             pl.BlockSpec(w_bias.shape, lambda i: (0, 0, 0)),
         ],
-        out_specs=[line_spec, by_row(3 * width), by_row(2 * channels), by_row(2)],
-        out_shape=[
-            jax.ShapeDtypeStruct(line_shape, BF16),
-            jax.ShapeDtypeStruct((rows, 3 * width, crop), BF16),
-            jax.ShapeDtypeStruct((rows, 2 * channels, crop), BF16),
-            jax.ShapeDtypeStruct((rows, 2, crop), F32),
-        ],
+        out_specs=line_spec,
+        out_shape=jax.ShapeDtypeStruct(line_shape, BF16),
         scratch_shapes=[
             pltpu.VMEM((2 * width, channels), BF16),
             pltpu.VMEM((channels, width), BF16),
-            pltpu.VMEM((lanes, channels), BF16),
             pltpu.VMEM((crop // 128, lanes * rows, 128) if direct else (1, 8, 128), F32),
+            pltpu.VMEM((4, width, crop), BF16),
         ],
         compiler_params=pltpu.CompilerParams(vmem_limit_bytes=56 * 2**20),
         cost_estimate=pl.CostEstimate(
             flops=6 * positions * channels * (3 * width + lanes),
-            bytes_accessed=positions * (3 * width + 3 * channels + lanes) * 2,
+            bytes_accessed=positions * (channels + lanes) * 2,
             transcendentals=positions * width,
         ),
         name="pair_forward",
@@ -213,9 +221,7 @@
     first,
     last,
     direct,
-    kept_ref,
-    normed_ref,
-    inv_ref,
+    pair_ref,
     d_bias_ref,
     w_in_ref,
     w_out_ref,
@@ -226,67 +232,107 @@
         pair_grad_ref, sums_ref = refs[:2]
     else:
         before_ref, _, pair_grad_ref, sums_ref = refs[:4]
-    w_lanes_ref, lines_ref = refs[-2:]
-    width, channels = w_out_ref.shape
-    layers, _, heads = w_bias_ref.shape
+    w_mix_ref, w_out_t_ref, lines_ref = refs[-8:-5]
+    hidden_ref, slope_ref, silu_ref, d_projected_ref, flipped_ref = refs[-5:]
+    width = w_out_ref.shape[0]
+    layers, heads, channels = w_bias_ref.shape
     lanes = layers * heads
-    step = kept_ref.shape[0]
+    unit = unit_of(width, UNIT)
+    step, crop, _ = pair_ref.shape
+    span = unit_of(crop, LANES)
     first_row = pl.program_id(0) * step
 
     @pl.when(pl.program_id(0) == 0)
     def _():
+        mix_weights(w_in_ref, w_out_ref, w_mix_ref, w_out_t_ref)
         if first:
             sums_ref[...] = jnp.zeros_like(sums_ref)
         else:
             sums_ref[...] = before_ref[...]
-        for layer in range(layers):
-            line = w_bias_ref[layer].astype(F32)
-            w_lanes_ref[layer * heads : (layer + 1) * heads, :] = line.T.astype(BF16)
         if direct:
             tiles, total, tile = lines_ref.shape
             for index in range(tiles):
                 lines = d_bias_ref[:, :, index * tile : (index + 1) * tile].astype(F32)
                 lines_ref[index] = lines.reshape(total, tile)
 
-    def stages(row):
-        if direct:
-            tiles, total, _ = lines_ref.shape
-            rows = total // lanes
-            lines = []
-            for layer in range(layers):
-                at = pl.ds(layer * rows + first_row + row, heads, stride=layers * rows)
-                lines.append(
-                    jnp.concatenate([lines_ref[index, at, :] for index in range(tiles)], 1)
-                )
-            d_bias = jnp.concatenate(lines, 0).astype(BF16)
-        else:
-            d_bias = d_bias_ref[row]
-        normed_in = normed_ref[row, :channels, :]
-        normed_out = normed_ref[row, channels:, :]
-        inv_in, inv_out = inv_ref[row, 0:1, :], inv_ref[row, 1:2, :]
-        d_normed = mm(w_lanes_ref[...], d_bias, 0, 0)
-        sums_ref[3 * width :, :] += mm(d_bias, normed_out, 1, 1)
+    def read_lines(row, left):
+        if not direct:
+            return d_bias_ref[row, :, left : left + span]
+        tiles, total, tile = lines_ref.shape
+        rows = total // lanes
+        found = []
+        for layer in range(layers):
+            at = pl.ds(layer * rows + first_row + row, heads, stride=layers * rows)
+            held = [lines_ref[left // tile + index, at, :] for index in range(span // tile)]
+            found.append(jnp.concatenate(held, 1))
+        return jnp.concatenate(found, 0).astype(BF16)
+
+    def stages(row, slot):
+        bias_sum = jnp.zeros((lanes, channels), F32)
+        for left in range(0, crop, span):
+            cols = slice(left, left + span)
+            pair_float = pair_ref[row, cols, :].T.astype(F32)
+            normed_float, inv_in = normalize(pair_float)
+            normed_in = normed_float.astype(BF16)
+            flipped_ref[slot, 0, cols, :] = normed_in.T
+            yield True
+
+            def product(at):
+                both = mm(w_mix_ref[2 * at : 2 * at + 2 * unit, :], normed_in)
+                return at, both[:unit], both[unit:]
+
+            def finish(at, half_gate, up_in):
+                one_plus = 1.0 + jnp.tanh(half_gate)
+                silu = half_gate * one_plus
+                slope = one_plus * (0.5 + half_gate * (1.0 - 0.5 * one_plus)) * up_in
+                hidden_ref[slot, at : at + unit, cols] = (silu * up_in).astype(BF16)
+                silu_ref[slot, at : at + unit, :] = silu
+                slope_ref[slot, at : at + unit, :] = slope
+
+            yield from pipelined(
+                [functools.partial(product, at) for at in range(0, width, unit)], finish
+            )
+            lifted = pair_float + mm(w_out_t_ref[...], hidden_ref[slot, :, cols])
+            d_bias = read_lines(row, left)
+            d_normed = mm(w_bias_ref[...].reshape(lanes, channels), d_bias, 0, 0)
+            yield True
+            out_float, inv_out = normalize(lifted)
+            bias_sum = bias_sum + mm(d_bias, out_float.astype(BF16), 1, 1)
+            d_lifted = norm_back(out_float, inv_out, d_normed)
+            lifted_half = d_lifted.astype(BF16)
+            flipped_ref[slot, 1, cols, :] = lifted_half.T
+            yield True
+
+            def product_back(at):
+                return at, mm(w_out_ref[at : at + unit, :], lifted_half)
+
+            def finish_back(at, d_hidden):
+                d_gate = d_hidden * slope_ref[slot, at : at + unit, :]
+                d_up = d_hidden * silu_ref[slot, at : at + unit, :]
+                d_projected_ref[slot, at : at + unit, cols] = d_gate.astype(BF16)
+                d_projected_ref[slot, width + at : width + at + unit, cols] = d_up.astype(BF16)
+
+            yield from pipelined(
+                [functools.partial(product_back, at) for at in range(0, width, unit)], finish_back
+            )
+            d_normed_in = mm(w_in_ref[...], d_projected_ref[slot, :, cols])
+            yield True
+            pair_grad = d_lifted + norm_back(normed_float, inv_in, d_normed_in)
+            pair_grad_ref[row, cols, :] = pair_grad.astype(BF16).T
+            yield True
+        sums_ref[3 * width :, :] += bias_sum
+        for at in range(0, 2 * width, width):
+            sums_ref[at : at + width, :] += mm(
+                d_projected_ref[slot, at : at + width, :], flipped_ref[slot, 0]
+            )
+            yield True
+        sums_ref[2 * width : 3 * width, :] += mm(hidden_ref[slot], flipped_ref[slot, 1])
         yield True
-        d_lifted = norm_back(normed_out.astype(F32), inv_out, d_normed)
-        lifted_half = d_lifted.astype(BF16)
-        yield True
-        sums_ref[2 * width : 3 * width, :] += mm(kept_ref[row, 2 * width :, :], lifted_half, 1, 1)
-        d_hidden = mm(w_out_ref[...], lifted_half)
-        yield True
-        d_gate = (d_hidden * kept_ref[row, :width, :].astype(F32)).astype(BF16)
-        d_up = (d_hidden * kept_ref[row, width : 2 * width, :].astype(F32)).astype(BF16)
-        d_projected = jnp.concatenate([d_gate, d_up], 0)
-        yield True
-        d_normed_in = mm(w_in_ref[...], d_projected)
-        sums_ref[: 2 * width, :] += mm(d_projected, normed_in, 1, 1)
-        yield True
-        pair_grad = d_lifted + norm_back(normed_in.astype(F32), inv_in, d_normed_in)
-        pair_grad_ref[row] = pair_grad.astype(BF16).T
-
-    for_rows(step, 4, stages, 2)
+
+    for_rows(step, 4, stages, 14)
 
     if last:
-        packed_ref = refs[-3]
+        packed_ref = refs[-9]
 
         @pl.when(pl.program_id(0) == pl.num_programs(0) - 1)
         def _():
@@ -295,30 +341,30 @@
             packed_ref[done:, :] = jnp.zeros((packed_ref.shape[0] - done, packed_ref.shape[1]), BF16)
 
 
-def backward_rows(chunk, chunks, rows, packed_rows, shape, stored, d_bias, weights, state):
+def backward_rows(chunk, chunks, rows, packed_rows, pair, d_bias, weights, state):
     w_in, w_out, w_bias = weights
-    crop, channels = shape[1:]
-    layers, _, heads = w_bias.shape
+    crop, channels = pair.shape[1:]
+    layers, heads, _ = w_bias.shape
     lanes = layers * heads
     width = w_out.shape[0]
-    step = math.gcd(rows, 4)
+    step = math.gcd(rows, 8)
     steps = rows // step
     positions = rows * crop
     first, last = chunk == 0, chunk == chunks - 1
     direct = rows % 16 == 0 and crop % 128 == 0
     whole = lambda i: (0, 0)
-    by_row = lambda height: pl.BlockSpec((step, height, crop), lambda i: (i, 0, 0))
-    in_specs = [by_row(array.shape[1]) for array in stored]
+    pair_spec = pl.BlockSpec((step, crop, channels), lambda i: (chunk * steps + i, 0, 0))
+    in_specs = [pair_spec]
     if direct:
         in_specs.append(pl.BlockSpec(d_bias.shape, lambda i: (0, 0, 0)))
     else:
-        in_specs.append(by_row(lanes))
+        in_specs.append(pl.BlockSpec((step, lanes, crop), lambda i: (i, 0, 0)))
     in_specs += [
         pl.BlockSpec(w_in.shape, whole),
         pl.BlockSpec(w_out.shape, whole),
         pl.BlockSpec(w_bias.shape, lambda i: (0, 0, 0)),
     ]
-    operands = [*stored, d_bias, *weights]
+    operands = [pair, d_bias, *weights]
     aliases = {}
     if not first:
         pair_grad, sums = state
@@ -326,16 +372,15 @@
         in_specs += [pl.BlockSpec(sums.shape, whole), pl.BlockSpec(memory_space=pl.ANY)]
         aliases = {len(operands) - 1: 0}
     shapes = [
-        jax.ShapeDtypeStruct(shape, BF16),
+        jax.ShapeDtypeStruct(pair.shape, BF16),
         jax.ShapeDtypeStruct((3 * width + lanes, channels), F32),
     ]
-    out_specs = [
-        pl.BlockSpec((step, crop, channels), lambda i: (chunk * steps + i, 0, 0)),
-        pl.BlockSpec(shapes[1].shape, whole),
-    ]
+    out_specs = [pair_spec, pl.BlockSpec(shapes[1].shape, whole)]
     if last:
         shapes.append(jax.ShapeDtypeStruct((packed_rows, channels), BF16))
         out_specs.append(pl.BlockSpec(shapes[2].shape, whole))
+    slots = 4
+    span = unit_of(crop, LANES)
     return pl.pallas_call(
         functools.partial(backward_kernel, first, last, direct),
         grid=(steps,),
@@ -344,14 +389,20 @@
         out_shape=shapes,
         input_output_aliases=aliases,
         scratch_shapes=[
-            pltpu.VMEM((lanes, channels), BF16),
+            pltpu.VMEM((2 * width, channels), BF16),
+            pltpu.VMEM((channels, width), BF16),
             pltpu.VMEM((crop // 128, lanes * rows, 128) if direct else (1, 8, 128), F32),
+            pltpu.VMEM((slots, width, crop), BF16),
+            pltpu.VMEM((slots, width, span), F32),
+            pltpu.VMEM((slots, width, span), F32),
+            pltpu.VMEM((slots, 2 * width, crop), BF16),
+            pltpu.VMEM((slots, 2, crop, channels), BF16),
         ],
         compiler_params=pltpu.CompilerParams(vmem_limit_bytes=56 * 2**20),
         cost_estimate=pl.CostEstimate(
-            flops=6 * positions * channels * (6 * width + 2 * lanes),
-            bytes_accessed=positions * (3 * width + 3 * channels + lanes) * 2,
-            transcendentals=0,
+            flops=6 * positions * channels * (9 * width + 2 * lanes),
+            bytes_accessed=positions * (2 * channels + lanes) * 2,
+            transcendentals=positions * width,
         ),
         name="pair_backward",
     )(*operands)
@@ -437,8 +488,10 @@
     )(*operands)
 
 
-def swap(array):
-    return lax.all_to_all(array, "tok", split_axis=0, concat_axis=0, tiled=True)
+def swap(array, teams=None):
+    return lax.all_to_all(
+        array, "tok", split_axis=0, concat_axis=0, tiled=True, axis_index_groups=teams
+    )
 
 
 def body(
@@ -463,7 +516,7 @@
     rows = row_count // chunks
     lanes = heads * layers
 
-    pair_weights = (weight_in, weight_out, weight_bias)
+    pair_weights = (weight_in, weight_out, jnp.transpose(weight_bias, (0, 2, 1)))
 
     group = lax.axis_index("tok") // heads
     weights = sample_weight(lax.dynamic_slice_in_dim(noise_level, group * samples, samples))
@@ -478,10 +531,8 @@
 
     direct = rows % 16 == 0 and crop % 128 == 0
     arrived = []
-    stored = []
     for chunk in range(chunks):
-        bias, *kept = forward_rows(chunk, rows, pair_states, *pair_weights)
-        stored.append(kept)
+        bias = forward_rows(chunk, rows, pair_states, *pair_weights)
         if direct:
             bias = bias.reshape(heads, layers, rows, crop)
         else:
@@ -532,18 +583,28 @@
             chunks,
             rows,
             share * devices,
-            pair_states.shape,
-            stored[chunk],
+            pair_states,
             d_bias,
             pair_weights,
             pair_state and pair_state[:2],
         )
     pair_grad, _, packed = pair_state
 
-    parts = swap(packed.reshape(devices, share, channels))
+    parity = lax.axis_index("tok") % 2
+    across = [(index, index ^ 1) for index in range(devices)]
+    teams = [list(range(odd, devices, 2)) for odd in range(2)]
+    halves = packed.reshape(2, devices // 2 * share, channels)
+    theirs = lax.ppermute(lax.dynamic_index_in_dim(halves, 1 - parity, 0, False), "tok", across)
+    mine = lax.dynamic_index_in_dim(halves, parity, 0, False)
+    mine = (mine.astype(F32) + theirs.astype(F32)).astype(BF16)
+    parts = swap(mine.reshape(devices // 2, share, channels), teams)
     summed = jnp.sum(parts.astype(F32), 0).astype(BF16)
-    copies = jnp.broadcast_to(summed[None], (devices, share, channels))
-    summed = swap(copies).reshape(devices * share, channels).astype(F32)
+    copies = jnp.broadcast_to(summed[None], (devices // 2, share, channels))
+    mine = swap(copies, teams).reshape(devices // 2 * share, channels)
+    theirs = lax.ppermute(mine, "tok", across)
+    even = parity == 0
+    summed = jnp.concatenate([jnp.where(even, mine, theirs), jnp.where(even, theirs, mine)], 0)
+    summed = summed.astype(F32)
     grad_in = summed[: 2 * width].T
     grad_out = summed[2 * width : 3 * width]
     grad_bias = summed[3 * width : sum_rows].reshape(layers, heads, channels)

time: 174 us -> 186 us (1.069)
  Pallas kernels: 88.1 us -> 108 us
  waiting for transfers between devices: 31.2 us -> 20.6 us
  blocking collectives: 19.2 us -> 25.7 us
  starting transfers between devices: 25.7 us -> 22.3 us
  local copies, waits for them, and re-layouts: 7.84 us -> 5.21 us
  other arithmetic: 0.3 us -> 2.61 us
    pallas_call x2, Pallas kernels: 39.3 us -> 67.4 us  [backward_rows(): pl.pallas_call(functools.partial(backward_kernel, first, last, direct), g...]
    all_to_all x5 -> x4, waiting for transfers between devices: 31.2 us -> 19.4 us  [swap(): lax.all_to_all(array, 'tok', split_axis=0, concat_axis=0, tiled=True, axi...]
    pallas_call x2, Pallas kernels: 40.3 us -> 31.8 us  [forward_rows(): pl.pallas_call(functools.partial(forward_kernel, direct), grid=(steps,),...]
    all_to_all x1 -> x2, blocking collectives: 19.2 us -> 25.7 us  [swap(): lax.all_to_all(array, 'tok', split_axis=0, concat_axis=0, tiled=True, axi...]
    all_to_all x5 -> x4, starting transfers between devices: 25.7 us -> 21.8 us  [swap(): lax.all_to_all(array, 'tok', split_axis=0, concat_axis=0, tiled=True, axi...]
    unnamed x19 -> x18, local copies, waits for them, and re-layouts: 4.69 us -> 3.23 us
  transfers between devices with their start and end apart: 5 -> 6, of which waited for: 3 -> 4; matrix products, arithmetic and copies ran while one was open for 1% -> 1% of each run, Pallas kernels for 28% -> 31%
where the time goes in v3:
time: 186 us; the launch traced here: 185 us
  Pallas kernels  108 us (58%)
  blocking collectives  25.7 us (14%)
  starting transfers between devices  22.3 us (12%)
  waiting for transfers between devices  20.6 us (11%)
  local copies, waits for them, and re-layouts  5.21 us (3%)
  other arithmetic  2.61 us (1%)
    pallas_call x2, Pallas kernels, backward_rows(): pl.pallas_call(functools.partial(backward_kernel, first, last, direct), g...  67.4 us
    pallas_call x2, Pallas kernels, forward_rows(): pl.pallas_call(functools.partial(forward_kernel, direct), grid=(steps,),...  31.8 us
    all_to_all x2, blocking collectives, swap(): lax.all_to_all(array, 'tok', split_axis=0, concat_axis=0, tiled=True, axi...  25.7 us
    all_to_all x4, starting transfers between devices, swap(): lax.all_to_all(array, 'tok', split_axis=0, concat_axis=0, tiled=True, axi...  21.8 us
    all_to_all x4, waiting for transfers between devices, swap(): lax.all_to_all(array, 'tok', split_axis=0, concat_axis=0, tiled=True, axi...  19.4 us
    pallas_call x2, Pallas kernels, attend_rows(): pl.pallas_call(functools.partial(attend_kernel, first, last), grid=(layer...  8.55 us
  transfers between devices with their start and end apart: 6, of which 4 were waited for; matrix products, arithmetic and copies ran while one was open for 1% of the time, Pallas kernels for 31%

profile of v3, /device:TPU:0, one launch (start us, length us, event | category | flops | bytes accessed | tf_op | source)
XLA Modules:
  0.0 185.0 jit_solution(13012916670206467549)
XLA Ops:
  0.6 15.9 %pair_forward.3 = bf16[32,16,512]{2,1,0:T(8,128)(2,1)} custom-call(bf16[32,512,128]{2,1,0:T(8,128)(2,1)} %pair_ref.7, bf16[128,1024]{1,0:T(8,128)(2,1)} %w_in_ref.7, bf16[512,128]{1,0:T(8,128)(2,1)} %w_out_ref.7, bf16[2,16,128]{2,1,0:T(8,128)(2,1)} %bitcast.67), custom_call_target="tpu_custom_call" | custom-call | flops 9865003008 | bytes 2621440 | tf_op jit(solution)/shard_map/pair_forward/pallas_call | solution.py:193
  16.5 7.4 %all-to-all-start.1 = ((bf16[16,2,16,512]{3,2,1,0:T(8,128)(2,1)}), bf16[16,2,16,512]{3,2,1,0:T(8,128)(2,1)S(1)}, u32[]{:S(2)}, u32[]{:S(2)}) async-start(bf16[16,2,16,512]{3,2,1,0:T(8,128)(2,1)} %bitcast.63), calls=%async_computation.1 | async-start | bytes 1048576 | tf_op jit(solution)/shard_map/all_to_all | solution.py:492
  23.9 0.3 copy.24
  24.2 15.9 %pair_forward.2 = bf16[32,16,512]{2,1,0:T(8,128)(2,1)} custom-call(bf16[32,512,128]{2,1,0:T(8,128)(2,1)} %pair_ref.7, bf16[128,1024]{1,0:T(8,128)(2,1)} %w_in_ref.7, bf16[512,128]{1,0:T(8,128)(2,1)} %w_out_ref.7, bf16[2,16,128]{2,1,0:T(8,128)(2,1)} %bitcast.68), custom_call_target="tpu_custom_call" | custom-call | flops 9865003008 | bytes 2621440 | tf_op jit(solution)/shard_map/pair_forward/pallas_call | solution.py:193
  40.1 6.1 %all-to-all-start = ((bf16[16,2,16,512]{3,2,1,0:T(8,128)(2,1)}), bf16[16,2,16,512]{3,2,1,0:T(8,128)(2,1)S(1)}, u32[]{:S(2)}, u32[]{:S(2)}) async-start(bf16[16,2,16,512]{3,2,1,0:T(8,128)(2,1)} %bitcast.61), calls=%async_computation | async-start | bytes 1048576 | tf_op jit(solution)/shard_map/all_to_all | solution.py:492
  46.3 0.3 copy.25
  46.6 0.1 copy.26.q_ref
  46.8 0.1 copy.27.g_ref
  47.0 4.3 %attention_backward.2 = (bf16[2,2,48,256]{3,2,1,0:T(8,128)(2,1)S(1)}, f32[2,2,48,512]{3,2,1,0:T(8,128)S(1)}, f32[2,2,48,512]{3,2,1,0:T(8,128)S(1)}, bf16[16,2,16,512]{3,2,1,0:T(8,128)(2,1)}) custom-call(f32[2]{0:T(128)S(1)} %multiply_divide_fusion.weight_ref, bf16[16,2,16,512]{3,2,1,0:T(8,128)(2,1)S(1)} %all-to-all-done.1.bias_ref, s32[1,512]{1,0:T(1,128)S(1)} %bitcast.48, ...), custom_call_target="tpu_custom_call" | custom-call | flops 5033164800 | bytes 2228224 | tf_op jit(solution)/shard_map/attention_backward/pallas_call | solution.py:470
  51.3 9.5 %all-to-all-done.bias_ref = bf16[16,2,16,512]{3,2,1,0:T(8,128)(2,1)S(1)} async-done(((bf16[16,2,16,512]{3,2,1,0:T(8,128)(2,1)}), bf16[16,2,16,512]{3,2,1,0:T(8,128)(2,1)S(1)}, u32[]{:S(2)}, u32[]{:S(2)}) %all-to-all-start) | async-done | bytes 524320 | tf_op jit(solution)/shard_map/all_to_all | solution.py:492
  60.7 4.3 %all-to-all-start.3 = ((bf16[16,2,16,512]{3,2,1,0:T(8,128)(2,1)}), bf16[16,2,16,512]{3,2,1,0:T(8,128)(2,1)}, u32[]{:S(2)}, u32[]{:S(2)}) async-start(bf16[16,2,16,512]{3,2,1,0:T(8,128)(2,1)} %get-tuple-element.22), calls=%async_computation.3 | async-start | bytes 1048576 | tf_op jit(solution)/shard_map/all_to_all | solution.py:492
  65.0 0.1 copy.28.q_ref
  65.1 0.1 copy.29.g_ref
  65.3 4.3 %attention_backward.3 = (bf16[2,2,48,256]{3,2,1,0:T(8,128)(2,1)S(1)}, bf16[2,2,48,512]{3,2,1,0:T(8,128)(2,1)}, bf16[2,2,48,512]{3,2,1,0:T(8,128)(2,1)}, bf16[16,2,16,512]{3,2,1,0:T(8,128)(2,1)}) custom-call(f32[2]{0:T(128)S(1)} %multiply_divide_fusion.weight_ref, bf16[16,2,16,512]{3,2,1,0:T(8,128)(2,1)S(1)} %all-to-all-done.bias_ref, s32[1,512]{1,0:T(1,128)S(1)} %bitcast.49, ...), custom_call_target="tpu_custom_call" | custom-call | flops 5033164800 | bytes 2228224 | tf_op jit(solution)/shard_map/attention_backward/pallas_call | solution.py:470
  69.6 9.9 %all-to-all-done.3 = bf16[16,2,16,512]{3,2,1,0:T(8,128)(2,1)} async-done(((bf16[16,2,16,512]{3,2,1,0:T(8,128)(2,1)}), bf16[16,2,16,512]{3,2,1,0:T(8,128)(2,1)}, u32[]{:S(2)}, u32[]{:S(2)}) %all-to-all-start.3) | async-done | bytes 524320 | tf_op jit(solution)/shard_map/all_to_all | solution.py:492
  79.5 4.0 %all-to-all-start.2 = ((bf16[16,2,16,512]{3,2,1,0:T(8,128)(2,1)}), bf16[16,2,16,512]{3,2,1,0:T(8,128)(2,1)S(1)}, u32[]{:S(2)}, u32[]{:S(2)}) async-start(bf16[16,2,16,512]{3,2,1,0:T(8,128)(2,1)} %get-tuple-element.21), calls=%async_computation.2 | async-start | bytes 1048576 | tf_op jit(solution)/shard_map/all_to_all | solution.py:492
  83.5 33.5 %pair_backward.2 = (bf16[32,512,128]{2,1,0:T(8,128)(2,1)}, f32[1568,128]{1,0:T(8,128)}) custom-call(bf16[32,512,128]{2,1,0:T(8,128)(2,1)} %pair_ref.7, bf16[32,16,512]{2,1,0:T(8,128)(2,1)} %bitcast.17.d_bias_ref, bf16[128,1024]{1,0:T(8,128)(2,1)} %w_in_ref.7, bf16[512,128]{1,0:T(8,128)(2,1)} %w_out_ref.7, bf16[2,16,128]{2,1,0:T(8,128)(2,1)} %bitcast.69), custom_call_target="tpu_custom_call" | custom-call | flops 29393682432 | bytes 4718592 | tf_op jit(solution)/shard_map/pair_backward/pallas_call | solution.py:384
  117.0 0.8 copy-done.3
  117.8 33.9 %pair_backward.3 = (bf16[32,512,128]{2,1,0:T(8,128)(2,1)}, f32[1568,128]{1,0:T(8,128)}, bf16[1792,128]{1,0:T(8,128)(2,1)}) custom-call(bf16[32,512,128]{2,1,0:T(8,128)(2,1)} %pair_ref.7, bf16[32,16,512]{2,1,0:T(8,128)(2,1)} %bitcast.62, bf16[128,1024]{1,0:T(8,128)(2,1)} %w_in_ref.7, bf16[512,128]{1,0:T(8,128)(2,1)} %w_out_ref.7, ...), custom_call_target="tpu_custom_call", output_to_operand_aliasing={{0}: (6, {})} | custom-call | flops 29393682432 | bytes 4718592 | tf_op jit(solution)/shard_map/pair_backward/pallas_call | solution.py:384
  151.7 1.0 dynamic-slice_bitcast_fusion
  152.7 0.5 collective-permute-start
  153.1 1.1 collective-permute-done
  154.3 1.0 fusion
  155.3 14.4 %all_to_all.30 = bf16[8,112,128]{2,1,0:T(8,128)(2,1)S(1)} all-to-all(bf16[8,112,128]{2,1,0:T(8,128)(2,1)S(1)} %bitcast.60), channel_id=1, replica_groups={{0,2,4,6,8,10,12,14},{1,3,5,7,9,11,13,15},{16,18,20,22,24,26,28,30},{17..., dimensions={0} | all-to-all | bytes 458752 | tf_op jit(solution)/shard_map/all_to_all | solution.py:492
  169.8 11.3 %all_to_all.31 = bf16[8,112,128]{2,1,0:T(8,128)(2,1)S(1)} all-to-all(bf16[8,112,128]{2,1,0:T(8,128)(2,1)S(1)} %broadcast_in_dim.18), channel_id=1, replica_groups={{0,2,4,6,8,10,12,14},{1,3,5,7,9,11,13,15},{16,18,20,22,24,26,28,30},{17..., dimensions={0} | all-to-all | bytes 458752 | tf_op jit(solution)/shard_map/all_to_all | solution.py:492
  181.1 0.2 copy.31
  181.2 0.2 copy.30
  181.4 0.1 maximum_bitcast_fusion
  181.6 0.9 copy.33
  182.7 0.7 maximum_convert_fusion.1
  183.4 0.6 maximum_convert_fusion.2
  184.0 1.0 copy.36
  (26 shorter events, 0.5 us)
Async XLA Ops:
  0.6 23.3 %copy-start.4 = (bf16[2,1,2,48,512]{4,3,2,1,0:T(8,128)(2,1)S(1)}, bf16[2,1,2,48,512]{4,3,2,1,0:T(8,128)(2,1)}, u32[]{:S(2)}) copy-start(bf16[2,1,2,48,512]{4,3,2,1,0:T(8,128)(2,1)} %param.16) | copy-start | bytes 589828
  16.5 23.6 %all-to-all-start.1 = ((bf16[16,2,16,512]{3,2,1,0:T(8,128)(2,1)}), bf16[16,2,16,512]{3,2,1,0:T(8,128)(2,1)S(1)}, u32[]{:S(2)}, u32[]{:S(2)}) async-start(bf16[16,2,16,512]{3,2,1,0:T(8,128)(2,1)} %bitcast.63), calls=%async_computation.1 | async-start | bytes 1048576 | tf_op jit(solution)/shard_map/all_to_all | solution.py:492
  24.2 22.1 %copy-start.5 = (bf16[2,1,2,48,512]{4,3,2,1,0:T(8,128)(2,1)S(1)}, bf16[2,1,2,48,512]{4,3,2,1,0:T(8,128)(2,1)}, u32[]{:S(2)}) copy-start(bf16[2,1,2,48,512]{4,3,2,1,0:T(8,128)(2,1)} %param.19) | copy-start | bytes 589828
  40.1 6.8 %copy-start.6 = (s32[2]{0:T(128)S(1)}, s32[2]{0:T(128)}, u32[]{:S(2)}) copy-start(s32[2]{0:T(128)} %param.15) | copy-start | bytes 28
  40.1 6.9 %copy-start = (bf16[2,1,2,48,512]{4,3,2,1,0:T(8,128)(2,1)S(1)}, bf16[2,1,2,48,512]{4,3,2,1,0:T(8,128)(2,1)}, u32[]{:S(2)}) copy-start(bf16[2,1,2,48,512]{4,3,2,1,0:T(8,128)(2,1)} %param.17) | copy-start | bytes 589828
  40.1 6.9 %copy-start.1 = (bf16[2,1,2,48,512]{4,3,2,1,0:T(8,128)(2,1)S(1)}, bf16[2,1,2,48,512]{4,3,2,1,0:T(8,128)(2,1)}, u32[]{:S(2)}) copy-start(bf16[2,1,2,48,512]{4,3,2,1,0:T(8,128)(2,1)} %param.18) | copy-start | bytes 589828
  40.1 6.9 %copy-start.2 = (s32[512]{0:T(512)S(1)}, s32[512]{0:T(512)}, u32[]{:S(2)}) copy-start(s32[512]{0:T(512)} %param.14) | copy-start | bytes 6148
  40.1 20.6 %all-to-all-start = ((bf16[16,2,16,512]{3,2,1,0:T(8,128)(2,1)}), bf16[16,2,16,512]{3,2,1,0:T(8,128)(2,1)S(1)}, u32[]{:S(2)}, u32[]{:S(2)}) async-start(bf16[16,2,16,512]{3,2,1,0:T(8,128)(2,1)} %bitcast.61), calls=%async_computation | async-start | bytes 1048576 | tf_op jit(solution)/shard_map/all_to_all | solution.py:492
  60.7 18.7 %all-to-all-start.3 = ((bf16[16,2,16,512]{3,2,1,0:T(8,128)(2,1)}), bf16[16,2,16,512]{3,2,1,0:T(8,128)(2,1)}, u32[]{:S(2)}, u32[]{:S(2)}) async-start(bf16[16,2,16,512]{3,2,1,0:T(8,128)(2,1)} %get-tuple-element.22), calls=%async_computation.3 | async-start | bytes 1048576 | tf_op jit(solution)/shard_map/all_to_all | solution.py:492
  79.5 37.5 %all-to-all-start.2 = ((bf16[16,2,16,512]{3,2,1,0:T(8,128)(2,1)}), bf16[16,2,16,512]{3,2,1,0:T(8,128)(2,1)S(1)}, u32[]{:S(2)}, u32[]{:S(2)}) async-start(bf16[16,2,16,512]{3,2,1,0:T(8,128)(2,1)} %get-tuple-element.21), calls=%async_computation.2 | async-start | bytes 1048576 | tf_op jit(solution)/shard_map/all_to_all | solution.py:492
  117.0 0.8 copy-start.3
  152.7 1.6 collective-permute-start
  181.0 1.5 collective-permute-start.1

commit v4 on v2

--- a/solution.py
+++ b/solution.py
@@ -66,11 +66,11 @@
         clock += 1
 
 
-def for_rows(count, group, make_stages, lag):
+def for_groups(count, group, one_group):
     group = math.gcd(count, group)
 
     def step(at, carry):
-        interleave(lambda index: make_stages(at * group + index), group, lag)
+        one_group(at * group, group)
         return carry
 
     if count == group:
@@ -86,17 +86,12 @@
     w_out_ref,
     w_bias_ref,
     bias_ref,
-    kept_ref,
-    normed_ref,
-    inv_ref,
     w_in_t_ref,
     w_out_t_ref,
-    w_lanes_ref,
     lines_ref,
 ):
     width = w_out_ref.shape[0]
-    channels = w_out_ref.shape[1]
-    layers, _, heads = w_bias_ref.shape
+    layers, heads, channels = w_bias_ref.shape
     piece = split_width(width)
     step = pair_ref.shape[0]
     first_row = pl.program_id(0) * step
@@ -107,37 +102,23 @@
         w_in_t_ref[:width, :] = w_in_t[:width] * 0.5
         w_in_t_ref[width:, :] = w_in_t[width:]
         w_out_t_ref[...] = w_out_ref[...].T
-        for layer in range(layers):
-            lanes = w_bias_ref[layer].astype(F32)
-            w_lanes_ref[layer * heads : (layer + 1) * heads, :] = lanes.T.astype(BF16)
 
     def stages(row):
         pair_float = pair_ref[row].T.astype(F32)
-        normed_float, inv_in = normalize(pair_float)
-        normed_in = normed_float.astype(BF16)
-        normed_ref[row, :channels, :] = normed_in
+        normed_in = normalize(pair_float)[0].astype(BF16)
         yield True
-        lifted = pair_float
+        hiddens = []
         for at in range(0, width, piece):
             half_gate = mm(w_in_t_ref[at : at + piece, :], normed_in)
             up_in = mm(w_in_t_ref[width + at : width + at + piece, :], normed_in)
             yield True
-            one_plus = 1.0 + jnp.tanh(half_gate)
-            silu = half_gate * one_plus
-            hidden = (silu * up_in).astype(BF16)
-            slope = one_plus * (0.5 + half_gate * (1.0 - 0.5 * one_plus)) * up_in
-            kept_ref[row, at : at + piece, :] = slope.astype(BF16)
-            kept_ref[row, width + at : width + at + piece, :] = silu.astype(BF16)
-            kept_ref[row, 2 * width + at : 2 * width + at + piece, :] = hidden
-            lifted = lifted + mm(w_out_t_ref[:, at : at + piece], hidden)
+            hidden = half_gate * (1.0 + jnp.tanh(half_gate)) * up_in
+            hiddens.append(hidden.astype(BF16))
             yield True
-        out_float, inv_out = normalize(lifted)
-        normed_out = out_float.astype(BF16)
-        normed_ref[row, channels:, :] = normed_out
-        inv_ref[row, 0:1, :] = inv_in
-        inv_ref[row, 1:2, :] = inv_out
+        lifted = pair_float + mm(w_out_t_ref[...], jnp.concatenate(hiddens, 0))
+        normed_out = normalize(lifted)[0].astype(BF16)
         yield True
-        bias = mm(w_lanes_ref[...], normed_out)
+        bias = mm(w_bias_ref[...].reshape(layers * heads, channels), normed_out)
         if direct:
             tiles, total, tile = lines_ref.shape
             rows = total // (layers * heads)
@@ -149,7 +130,7 @@
         else:
             bias_ref[row] = bias.astype(BF16)
 
-    for_rows(step, 4, stages, 2)
+    for_groups(step, 4, lambda at, count: interleave(lambda i: stages(at + i), count, 2))
 
     if direct:
 
@@ -163,9 +144,9 @@
 
 def forward_rows(chunk, rows, pair, w_in, w_out, w_bias):
     crop, channels = pair.shape[1:]
-    layers, _, heads = w_bias.shape
+    layers, heads, _ = w_bias.shape
     lanes = layers * heads
-    step = math.gcd(rows, 4)
+    step = math.gcd(rows, 8)
     steps = rows // step
     positions = rows * crop
     width = w_out.shape[0]
@@ -176,7 +157,6 @@
         if direct
         else pl.BlockSpec((step, lanes, crop), lambda i: (i, 0, 0))
     )
-    by_row = lambda height: pl.BlockSpec((step, height, crop), lambda i: (i, 0, 0))
     return pl.pallas_call(
         functools.partial(forward_kernel, direct),
         grid=(steps,),
@@ -186,23 +166,17 @@
             pl.BlockSpec(w_out.shape, lambda i: (0, 0)),
             pl.BlockSpec(w_bias.shape, lambda i: (0, 0, 0)),
         ],
-        out_specs=[line_spec, by_row(3 * width), by_row(2 * channels), by_row(2)],
-        out_shape=[
-            jax.ShapeDtypeStruct(line_shape, BF16),
-            jax.ShapeDtypeStruct((rows, 3 * width, crop), BF16),
-            jax.ShapeDtypeStruct((rows, 2 * channels, crop), BF16),
-            jax.ShapeDtypeStruct((rows, 2, crop), F32),
-        ],
+        out_specs=line_spec,
+        out_shape=jax.ShapeDtypeStruct(line_shape, BF16),
         scratch_shapes=[
             pltpu.VMEM((2 * width, channels), BF16),
             pltpu.VMEM((channels, width), BF16),
-            pltpu.VMEM((lanes, channels), BF16),
             pltpu.VMEM((crop // 128, lanes * rows, 128) if direct else (1, 8, 128), F32),
         ],
         compiler_params=pltpu.CompilerParams(vmem_limit_bytes=56 * 2**20),
         cost_estimate=pl.CostEstimate(
             flops=6 * positions * channels * (3 * width + lanes),
-            bytes_accessed=positions * (3 * width + 3 * channels + lanes) * 2,
+            bytes_accessed=positions * (channels + lanes) * 2,
             transcendentals=positions * width,
         ),
         name="pair_forward",
@@ -213,9 +187,7 @@
     first,
     last,
     direct,
-    kept_ref,
-    normed_ref,
-    inv_ref,
+    pair_ref,
     d_bias_ref,
     w_in_ref,
     w_out_ref,
@@ -226,99 +198,132 @@
         pair_grad_ref, sums_ref = refs[:2]
     else:
         before_ref, _, pair_grad_ref, sums_ref = refs[:4]
-    w_lanes_ref, lines_ref = refs[-2:]
-    width, channels = w_out_ref.shape
-    layers, _, heads = w_bias_ref.shape
+    w_in_t_ref, w_out_t_ref, w_back_ref, w_half_ref, lines_ref = refs[-5:]
+    width = w_out_ref.shape[0]
+    layers, heads, channels = w_bias_ref.shape
     lanes = layers * heads
-    step = kept_ref.shape[0]
+    piece = split_width(width)
+    step = pair_ref.shape[0]
     first_row = pl.program_id(0) * step
 
     @pl.when(pl.program_id(0) == 0)
     def _():
+        w_in_t = w_in_ref[...].T
+        w_in_t_ref[:width, :] = w_in_t[:width] * 0.5
+        w_in_t_ref[width:, :] = w_in_t[width:]
+        w_out_t_ref[...] = w_out_ref[...].T
+        w_back_ref[:, :width] = w_in_ref[:, :width]
+        w_back_ref[:, width:] = w_in_ref[:, width:] * 2.0
+        w_half_ref[...] = w_out_ref[...] * 0.5
         if first:
             sums_ref[...] = jnp.zeros_like(sums_ref)
         else:
             sums_ref[...] = before_ref[...]
-        for layer in range(layers):
-            line = w_bias_ref[layer].astype(F32)
-            w_lanes_ref[layer * heads : (layer + 1) * heads, :] = line.T.astype(BF16)
         if direct:
             tiles, total, tile = lines_ref.shape
             for index in range(tiles):
                 lines = d_bias_ref[:, :, index * tile : (index + 1) * tile].astype(F32)
                 lines_ref[index] = lines.reshape(total, tile)
 
-    def stages(row):
-        if direct:
-            tiles, total, _ = lines_ref.shape
-            rows = total // lanes
-            lines = []
-            for layer in range(layers):
-                at = pl.ds(layer * rows + first_row + row, heads, stride=layers * rows)
-                lines.append(
-                    jnp.concatenate([lines_ref[index, at, :] for index in range(tiles)], 1)
-                )
-            d_bias = jnp.concatenate(lines, 0).astype(BF16)
-        else:
-            d_bias = d_bias_ref[row]
-        normed_in = normed_ref[row, :channels, :]
-        normed_out = normed_ref[row, channels:, :]
-        inv_in, inv_out = inv_ref[row, 0:1, :], inv_ref[row, 1:2, :]
-        d_normed = mm(w_lanes_ref[...], d_bias, 0, 0)
-        sums_ref[3 * width :, :] += mm(d_bias, normed_out, 1, 1)
+    def read_lines(row):
+        if not direct:
+            return d_bias_ref[row]
+        tiles, total, _ = lines_ref.shape
+        rows = total // lanes
+        found = []
+        for layer in range(layers):
+            at = pl.ds(layer * rows + first_row + row, heads, stride=layers * rows)
+            found.append(jnp.concatenate([lines_ref[index, at, :] for index in range(tiles)], 1))
+        return jnp.concatenate(found, 0).astype(BF16)
+
+    def stages(row, kept):
+        pair_float = pair_ref[row].T.astype(F32)
+        normed_float, inv_in = normalize(pair_float)
+        normed_in = normed_float.astype(BF16)
         yield True
-        d_lifted = norm_back(normed_out.astype(F32), inv_out, d_normed)
+        pieces = []
+        for at in range(0, width, piece):
+            half_gate = mm(w_in_t_ref[at : at + piece, :], normed_in)
+            up_in = mm(w_in_t_ref[width + at : width + at + piece, :], normed_in)
+            yield True
+            one_plus = 1.0 + jnp.tanh(half_gate)
+            silu = half_gate * one_plus
+            hidden = (silu * up_in).astype(BF16)
+            slope = one_plus * (1.0 + half_gate * (2.0 - one_plus)) * up_in
+            pieces.append((silu, slope, hidden))
+            yield True
+        hidden = jnp.concatenate([hidden for _, _, hidden in pieces], 0)
+        lifted = pair_float + mm(w_out_t_ref[...], hidden)
+        d_bias = read_lines(row)
+        d_normed = mm(w_bias_ref[...].reshape(lanes, channels), d_bias, 0, 0)
+        yield True
+        out_float, inv_out = normalize(lifted)
+        normed_out = out_float.astype(BF16)
+        d_lifted = norm_back(out_float, inv_out, d_normed)
         lifted_half = d_lifted.astype(BF16)
         yield True
-        sums_ref[2 * width : 3 * width, :] += mm(kept_ref[row, 2 * width :, :], lifted_half, 1, 1)
-        d_hidden = mm(w_out_ref[...], lifted_half)
+        d_gates, d_ups = [], []
+        for index, (silu, slope, _) in enumerate(pieces):
+            at = index * piece
+            d_hidden = mm(w_half_ref[at : at + piece, :], lifted_half)
+            yield True
+            d_gates.append((d_hidden * slope).astype(BF16))
+            d_ups.append((d_hidden * silu).astype(BF16))
+            yield True
+        d_projected = jnp.concatenate(d_gates + d_ups, 0)
+        kept.append((d_projected, normed_in, hidden, lifted_half, d_bias, normed_out))
+        d_normed_in = mm(w_back_ref[...], d_projected)
         yield True
-        d_gate = (d_hidden * kept_ref[row, :width, :].astype(F32)).astype(BF16)
-        d_up = (d_hidden * kept_ref[row, width : 2 * width, :].astype(F32)).astype(BF16)
-        d_projected = jnp.concatenate([d_gate, d_up], 0)
-        yield True
-        d_normed_in = mm(w_in_ref[...], d_projected)
+        pair_grad = d_lifted + norm_back(normed_float, inv_in, d_normed_in)
+        pair_grad_ref[row] = pair_grad.astype(BF16).T
+
+    def one_group(at, count):
+        kept = []
+        interleave(lambda index: stages(at + index, kept), count, 3)
+        d_projected, normed_in, hidden, lifted_half, d_bias, normed_out = (
+            jnp.concatenate(parts, 1) for parts in zip(*kept)
+        )
         sums_ref[: 2 * width, :] += mm(d_projected, normed_in, 1, 1)
-        yield True
-        pair_grad = d_lifted + norm_back(normed_in.astype(F32), inv_in, d_normed_in)
-        pair_grad_ref[row] = pair_grad.astype(BF16).T
-
-    for_rows(step, 4, stages, 2)
+        sums_ref[2 * width : 3 * width, :] += mm(hidden, lifted_half, 1, 1)
+        sums_ref[3 * width :, :] += mm(d_bias, normed_out, 1, 1)
+
+    for_groups(step, 4, one_group)
 
     if last:
-        packed_ref = refs[-3]
+        packed_ref = refs[-6]
 
         @pl.when(pl.program_id(0) == pl.num_programs(0) - 1)
         def _():
             done = sums_ref.shape[0]
             packed_ref[:done, :] = sums_ref[...].astype(BF16)
+            packed_ref[width : 2 * width, :] = (2.0 * sums_ref[width : 2 * width, :]).astype(BF16)
             packed_ref[done:, :] = jnp.zeros((packed_ref.shape[0] - done, packed_ref.shape[1]), BF16)
 
 
-def backward_rows(chunk, chunks, rows, packed_rows, shape, stored, d_bias, weights, state):
+def backward_rows(chunk, chunks, rows, packed_rows, pair, d_bias, weights, state):
     w_in, w_out, w_bias = weights
-    crop, channels = shape[1:]
-    layers, _, heads = w_bias.shape
+    crop, channels = pair.shape[1:]
+    layers, heads, _ = w_bias.shape
     lanes = layers * heads
     width = w_out.shape[0]
-    step = math.gcd(rows, 4)
+    step = math.gcd(rows, 8)
     steps = rows // step
     positions = rows * crop
     first, last = chunk == 0, chunk == chunks - 1
     direct = rows % 16 == 0 and crop % 128 == 0
     whole = lambda i: (0, 0)
-    by_row = lambda height: pl.BlockSpec((step, height, crop), lambda i: (i, 0, 0))
-    in_specs = [by_row(array.shape[1]) for array in stored]
+    pair_spec = pl.BlockSpec((step, crop, channels), lambda i: (chunk * steps + i, 0, 0))
+    in_specs = [pair_spec]
     if direct:
         in_specs.append(pl.BlockSpec(d_bias.shape, lambda i: (0, 0, 0)))
     else:
-        in_specs.append(by_row(lanes))
+        in_specs.append(pl.BlockSpec((step, lanes, crop), lambda i: (i, 0, 0)))
     in_specs += [
         pl.BlockSpec(w_in.shape, whole),
         pl.BlockSpec(w_out.shape, whole),
         pl.BlockSpec(w_bias.shape, lambda i: (0, 0, 0)),
     ]
-    operands = [*stored, d_bias, *weights]
+    operands = [pair, d_bias, *weights]
     aliases = {}
     if not first:
         pair_grad, sums = state
@@ -326,13 +331,10 @@
         in_specs += [pl.BlockSpec(sums.shape, whole), pl.BlockSpec(memory_space=pl.ANY)]
         aliases = {len(operands) - 1: 0}
     shapes = [
-        jax.ShapeDtypeStruct(shape, BF16),
+        jax.ShapeDtypeStruct(pair.shape, BF16),
         jax.ShapeDtypeStruct((3 * width + lanes, channels), F32),
     ]
-    out_specs = [
-        pl.BlockSpec((step, crop, channels), lambda i: (chunk * steps + i, 0, 0)),
-        pl.BlockSpec(shapes[1].shape, whole),
-    ]
+    out_specs = [pair_spec, pl.BlockSpec(shapes[1].shape, whole)]
     if last:
         shapes.append(jax.ShapeDtypeStruct((packed_rows, channels), BF16))
         out_specs.append(pl.BlockSpec(shapes[2].shape, whole))
@@ -344,14 +346,17 @@
         out_shape=shapes,
         input_output_aliases=aliases,
         scratch_shapes=[
-            pltpu.VMEM((lanes, channels), BF16),
+            pltpu.VMEM((2 * width, channels), BF16),
+            pltpu.VMEM((channels, width), BF16),
+            pltpu.VMEM((channels, 2 * width), BF16),
+            pltpu.VMEM((width, channels), BF16),
             pltpu.VMEM((crop // 128, lanes * rows, 128) if direct else (1, 8, 128), F32),
         ],
         compiler_params=pltpu.CompilerParams(vmem_limit_bytes=56 * 2**20),
         cost_estimate=pl.CostEstimate(
-            flops=6 * positions * channels * (6 * width + 2 * lanes),
-            bytes_accessed=positions * (3 * width + 3 * channels + lanes) * 2,
-            transcendentals=0,
+            flops=6 * positions * channels * (9 * width + 2 * lanes),
+            bytes_accessed=positions * (2 * channels + lanes) * 2,
+            transcendentals=positions * width,
         ),
         name="pair_backward",
     )(*operands)
@@ -441,6 +446,58 @@
     return lax.all_to_all(array, "tok", split_axis=0, concat_axis=0, tiled=True)
 
 
+def bit_groups(devices):
+    bits = list(range(devices.bit_length() - 1))
+    groups = [[bit] for bit in bits[:2]]
+    return groups + [bits[at : at + 2] for at in range(2, len(bits), 2)]
+
+
+def partner_list(devices, bits, step):
+    mask = sum(((step >> place) & 1) << bit for place, bit in enumerate(bits))
+    return [(index, index ^ mask) for index in range(devices)]
+
+
+def digit_of(index, bits):
+    return sum(((index >> bit) & 1) << place for place, bit in enumerate(bits))
+
+
+def pick(blocks, index):
+    return lax.dynamic_index_in_dim(blocks, index, 0, False)
+
+
+def sum_over_devices(array):
+    devices = lax.axis_size("tok")
+    index = lax.axis_index("tok")
+    groups = bit_groups(devices)
+    held = array
+    for bits in groups:
+        count = 1 << len(bits)
+        digit = digit_of(index, bits)
+        blocks = held.reshape(count, held.shape[0] // count, held.shape[1])
+        total = pick(blocks, digit).astype(F32)
+        received = [
+            lax.ppermute(pick(blocks, digit ^ step), "tok", partner_list(devices, bits, step))
+            for step in range(1, count)
+        ]
+        for block in received:
+            total = total + block.astype(F32)
+        held = total.astype(BF16)
+    for bits in reversed(groups):
+        count = 1 << len(bits)
+        digit = digit_of(index, bits)
+        received = [held] + [
+            lax.ppermute(held, "tok", partner_list(devices, bits, step)) for step in range(1, count)
+        ]
+        if count == 2:
+            even = digit == 0
+            ordered = [jnp.where(even, *received), jnp.where(even, *received[::-1])]
+        else:
+            stacked = jnp.stack(received, 0)
+            ordered = [pick(stacked, digit ^ place) for place in range(count)]
+        held = jnp.concatenate(ordered, 0)
+    return held.astype(F32)
+
+
 def body(
     pair_states,
     weight_in,
@@ -463,7 +520,7 @@
     rows = row_count // chunks
     lanes = heads * layers
 
-    pair_weights = (weight_in, weight_out, weight_bias)
+    pair_weights = (weight_in, weight_out, jnp.transpose(weight_bias, (0, 2, 1)))
 
     group = lax.axis_index("tok") // heads
     weights = sample_weight(lax.dynamic_slice_in_dim(noise_level, group * samples, samples))
@@ -478,10 +535,8 @@
 
     direct = rows % 16 == 0 and crop % 128 == 0
     arrived = []
-    stored = []
     for chunk in range(chunks):
-        bias, *kept = forward_rows(chunk, rows, pair_states, *pair_weights)
-        stored.append(kept)
+        bias = forward_rows(chunk, rows, pair_states, *pair_weights)
         if direct:
             bias = bias.reshape(heads, layers, rows, crop)
         else:
@@ -532,18 +587,14 @@
             chunks,
             rows,
             share * devices,
-            pair_states.shape,
-            stored[chunk],
+            pair_states,
             d_bias,
             pair_weights,
             pair_state and pair_state[:2],
         )
     pair_grad, _, packed = pair_state
 
-    parts = swap(packed.reshape(devices, share, channels))
-    summed = jnp.sum(parts.astype(F32), 0).astype(BF16)
-    copies = jnp.broadcast_to(summed[None], (devices, share, channels))
-    summed = swap(copies).reshape(devices * share, channels).astype(F32)
+    summed = sum_over_devices(packed)
     grad_in = summed[: 2 * width].T
     grad_out = summed[2 * width : 3 * width]
     grad_bias = summed[3 * width : sum_rows].reshape(layers, heads, channels)

time: 174 us -> 176 us (1.011)
  blocking collectives: 19.2 us -> 0 us
  Pallas kernels: 88.1 us -> 96.4 us
  starting transfers between devices: 25.7 us -> 32.9 us
  waiting for transfers between devices: 31.2 us -> 36.9 us
  local copies, waits for them, and re-layouts: 7.84 us -> 5.26 us
  other arithmetic: 0.3 us -> 2.77 us
    pallas_call x2, Pallas kernels: 39.3 us -> 63.9 us  [backward_rows(): pl.pallas_call(functools.partial(backward_kernel, first, last, direct), g...]
    all_to_all x1 -> x0, blocking collectives: 19.2 us -> none  [swap(): return lax.all_to_all(array, 'tok', split_axis=0, concat_axis=0, tiled=True)]
    pallas_call x2, Pallas kernels: 40.3 us -> 23.9 us  [forward_rows(): pl.pallas_call(functools.partial(forward_kernel, direct), grid=(steps,),...]
    ppermute x0 -> x10, waiting for transfers between devices: none -> 15.4 us  [the longest x5 9.97 us: sum_over_devices(): lax.ppermute(pick(blocks, digit ^ step), 'tok', partner_list(devices, bit...]
    ppermute x0 -> x10, starting transfers between devices: none -> 13.1 us  [the longest x5 6.87 us: sum_over_devices(): lax.ppermute(pick(blocks, digit ^ step), 'tok', partner_list(devices, bit...]
    all_to_all x5 -> x4, waiting for transfers between devices: 31.2 us -> 21.6 us  [swap(): return lax.all_to_all(array, 'tok', split_axis=0, concat_axis=0, tiled=True)]
    all_to_all x5 -> x4, starting transfers between devices: 25.7 us -> 19.8 us  [swap(): return lax.all_to_all(array, 'tok', split_axis=0, concat_axis=0, tiled=True)]
    unnamed x19 -> x18, local copies, waits for them, and re-layouts: 4.69 us -> 3.26 us
  transfers between devices with their start and end apart: 5 -> 14, of which waited for: 3 -> 11; matrix products, arithmetic and copies ran while one was open for 1% -> 1% of each run, Pallas kernels for 28% -> 30%
where the time goes in v4:
time: 176 us; the launch traced here: 175 us
  Pallas kernels  96.4 us (55%)
  waiting for transfers between devices  36.9 us (21%)
  starting transfers between devices  32.9 us (19%)
  local copies, waits for them, and re-layouts  5.26 us (3%)
  other arithmetic  2.77 us (2%)
    pallas_call x2, Pallas kernels, backward_rows(): pl.pallas_call(functools.partial(backward_kernel, first, last, direct), g...  63.9 us
    pallas_call x2, Pallas kernels, forward_rows(): pl.pallas_call(functools.partial(forward_kernel, direct), grid=(steps,),...  23.9 us
    all_to_all x4, waiting for transfers between devices, swap(): return lax.all_to_all(array, 'tok', split_axis=0, concat_axis=0, tiled=True)  21.6 us
    all_to_all x4, starting transfers between devices, swap(): return lax.all_to_all(array, 'tok', split_axis=0, concat_axis=0, tiled=True)  19.8 us
    ppermute x5, waiting for transfers between devices, sum_over_devices(): lax.ppermute(pick(blocks, digit ^ step), 'tok', partner_list(devices, bit...  9.97 us
    pallas_call x2, Pallas kernels, attend_rows(): pl.pallas_call(functools.partial(attend_kernel, first, last), grid=(layer...  8.55 us
    ppermute x5, starting transfers between devices, sum_over_devices(): lax.ppermute(pick(blocks, digit ^ step), 'tok', partner_list(devices, bit...  6.87 us
    ppermute x5, starting transfers between devices, sum_over_devices(): lax.ppermute(held, 'tok', partner_list(devices, bits, step))  6.25 us
  transfers between devices with their start and end apart: 14, of which 11 were waited for; matrix products, arithmetic and copies ran while one was open for 1% of the time, Pallas kernels for 30%

profile of v4, /device:TPU:0, one launch (start us, length us, event | category | flops | bytes accessed | tf_op | source)
XLA Modules:
  0.0 175.2 jit_solution(18392804669759906645)
XLA Ops:
  0.6 12.0 %pair_forward.3 = bf16[32,16,512]{2,1,0:T(8,128)(2,1)} custom-call(bf16[32,512,128]{2,1,0:T(8,128)(2,1)} %pair_ref.7, bf16[128,1024]{1,0:T(8,128)(2,1)} %w_in_ref.7, bf16[512,128]{1,0:T(8,128)(2,1)} %w_out_ref.7, bf16[2,16,128]{2,1,0:T(8,128)(2,1)} %bitcast.97), custom_call_target="tpu_custom_call" | custom-call | flops 9865003008 | bytes 2621440 | tf_op jit(solution)/shard_map/pair_forward/pallas_call | solution.py:160
  12.6 7.4 %all-to-all-start.1 = ((bf16[16,2,16,512]{3,2,1,0:T(8,128)(2,1)}), bf16[16,2,16,512]{3,2,1,0:T(8,128)(2,1)S(1)}, u32[]{:S(2)}, u32[]{:S(2)}) async-start(bf16[16,2,16,512]{3,2,1,0:T(8,128)(2,1)} %bitcast.87), calls=%async_computation.1 | async-start | bytes 1048576 | tf_op jit(solution)/shard_map/all_to_all | solution.py:446
  20.3 12.0 %pair_forward.2 = bf16[32,16,512]{2,1,0:T(8,128)(2,1)} custom-call(bf16[32,512,128]{2,1,0:T(8,128)(2,1)} %pair_ref.7, bf16[128,1024]{1,0:T(8,128)(2,1)} %w_in_ref.7, bf16[512,128]{1,0:T(8,128)(2,1)} %w_out_ref.7, bf16[2,16,128]{2,1,0:T(8,128)(2,1)} %bitcast.98), custom_call_target="tpu_custom_call" | custom-call | flops 9865003008 | bytes 2621440 | tf_op jit(solution)/shard_map/pair_forward/pallas_call | solution.py:160
  32.3 2.2 %all-to-all-done.1.bias_ref = bf16[16,2,16,512]{3,2,1,0:T(8,128)(2,1)S(1)} async-done(((bf16[16,2,16,512]{3,2,1,0:T(8,128)(2,1)}), bf16[16,2,16,512]{3,2,1,0:T(8,128)(2,1)S(1)}, u32[]{:S(2)}, u32[]{:S(2)}) %all-to-all-start.1) | async-done | bytes 524320 | tf_op jit(solution)/shard_map/all_to_all | solution.py:446
  34.5 4.1 %all-to-all-start = ((bf16[16,2,16,512]{3,2,1,0:T(8,128)(2,1)}), bf16[16,2,16,512]{3,2,1,0:T(8,128)(2,1)S(1)}, u32[]{:S(2)}, u32[]{:S(2)}) async-start(bf16[16,2,16,512]{3,2,1,0:T(8,128)(2,1)} %bitcast.85), calls=%async_computation | async-start | bytes 1048576 | tf_op jit(solution)/shard_map/all_to_all | solution.py:446
  39.3 4.3 %attention_backward.2 = (bf16[2,2,48,256]{3,2,1,0:T(8,128)(2,1)S(1)}, f32[2,2,48,512]{3,2,1,0:T(8,128)S(1)}, f32[2,2,48,512]{3,2,1,0:T(8,128)S(1)}, bf16[16,2,16,512]{3,2,1,0:T(8,128)(2,1)}) custom-call(f32[2]{0:T(128)S(1)} %multiply_divide_fusion.weight_ref, bf16[16,2,16,512]{3,2,1,0:T(8,128)(2,1)S(1)} %all-to-all-done.1.bias_ref, s32[1,512]{1,0:T(1,128)S(1)} %bitcast.72, ...), custom_call_target="tpu_custom_call" | custom-call | flops 5033164800 | bytes 2228224 | tf_op jit(solution)/shard_map/attention_backward/pallas_call | solution.py:424
  43.6 9.5 %all-to-all-done.bias_ref = bf16[16,2,16,512]{3,2,1,0:T(8,128)(2,1)S(1)} async-done(((bf16[16,2,16,512]{3,2,1,0:T(8,128)(2,1)}), bf16[16,2,16,512]{3,2,1,0:T(8,128)(2,1)S(1)}, u32[]{:S(2)}, u32[]{:S(2)}) %all-to-all-start) | async-done | bytes 524320 | tf_op jit(solution)/shard_map/all_to_all | solution.py:446
  53.0 4.2 %all-to-all-start.3 = ((bf16[16,2,16,512]{3,2,1,0:T(8,128)(2,1)}), bf16[16,2,16,512]{3,2,1,0:T(8,128)(2,1)}, u32[]{:S(2)}, u32[]{:S(2)}) async-start(bf16[16,2,16,512]{3,2,1,0:T(8,128)(2,1)} %get-tuple-element.22), calls=%async_computation.3 | async-start | bytes 1048576 | tf_op jit(solution)/shard_map/all_to_all | solution.py:446
  57.6 4.3 %attention_backward.3 = (bf16[2,2,48,256]{3,2,1,0:T(8,128)(2,1)S(1)}, bf16[2,2,48,512]{3,2,1,0:T(8,128)(2,1)}, bf16[2,2,48,512]{3,2,1,0:T(8,128)(2,1)}, bf16[16,2,16,512]{3,2,1,0:T(8,128)(2,1)}) custom-call(f32[2]{0:T(128)S(1)} %multiply_divide_fusion.weight_ref, bf16[16,2,16,512]{3,2,1,0:T(8,128)(2,1)S(1)} %all-to-all-done.bias_ref, s32[1,512]{1,0:T(1,128)S(1)} %bitcast.73, ...), custom_call_target="tpu_custom_call" | custom-call | flops 5033164800 | bytes 2228224 | tf_op jit(solution)/shard_map/attention_backward/pallas_call | solution.py:424
  61.8 9.9 %all-to-all-done.3 = bf16[16,2,16,512]{3,2,1,0:T(8,128)(2,1)} async-done(((bf16[16,2,16,512]{3,2,1,0:T(8,128)(2,1)}), bf16[16,2,16,512]{3,2,1,0:T(8,128)(2,1)}, u32[]{:S(2)}, u32[]{:S(2)}) %all-to-all-start.3) | async-done | bytes 524320 | tf_op jit(solution)/shard_map/all_to_all | solution.py:446
  71.8 4.1 %all-to-all-start.2 = ((bf16[16,2,16,512]{3,2,1,0:T(8,128)(2,1)}), bf16[16,2,16,512]{3,2,1,0:T(8,128)(2,1)S(1)}, u32[]{:S(2)}, u32[]{:S(2)}) async-start(bf16[16,2,16,512]{3,2,1,0:T(8,128)(2,1)} %get-tuple-element.21), calls=%async_computation.2 | async-start | bytes 1048576 | tf_op jit(solution)/shard_map/all_to_all | solution.py:446
  75.8 31.7 %pair_backward.2 = (bf16[32,512,128]{2,1,0:T(8,128)(2,1)}, f32[1568,128]{1,0:T(8,128)}) custom-call(bf16[32,512,128]{2,1,0:T(8,128)(2,1)} %pair_ref.7, bf16[32,16,512]{2,1,0:T(8,128)(2,1)} %bitcast.17.d_bias_ref, bf16[128,1024]{1,0:T(8,128)(2,1)} %w_in_ref.7, bf16[512,128]{1,0:T(8,128)(2,1)} %w_out_ref.7, bf16[2,16,128]{2,1,0:T(8,128)(2,1)} %bitcast.99), custom_call_target="tpu_custom_call" | custom-call | flops 29393682432 | bytes 4718592 | tf_op jit(solution)/shard_map/pair_backward/pallas_call | solution.py:341
  107.6 0.8 copy-done.3
  108.4 32.2 %pair_backward.3 = (bf16[32,512,128]{2,1,0:T(8,128)(2,1)}, f32[1568,128]{1,0:T(8,128)}, bf16[1792,128]{1,0:T(8,128)(2,1)}) custom-call(bf16[32,512,128]{2,1,0:T(8,128)(2,1)} %pair_ref.7, bf16[32,16,512]{2,1,0:T(8,128)(2,1)} %bitcast.86, bf16[128,1024]{1,0:T(8,128)(2,1)} %w_in_ref.7, bf16[512,128]{1,0:T(8,128)(2,1)} %w_out_ref.7, ...), custom_call_target="tpu_custom_call", output_to_operand_aliasing={{0}: (6, {})} | custom-call | flops 29393682432 | bytes 4718592 | tf_op jit(solution)/shard_map/pair_backward/pallas_call | solution.py:341
  140.6 1.0 dynamic-slice_bitcast_fusion
  142.0 1.1 collective-permute-done
  143.1 1.0 fusion
  144.1 2.0 %collective-permute-start.1 = (bf16[448,128]{1,0:T(8,128)(2,1)S(1)}, bf16[448,128]{1,0:T(8,128)(2,1)S(1)}, u32[]{:S(2)}, u32[]{:S(2)}) collective-permute-start(bf16[448,128]{1,0:T(8,128)(2,1)S(1)} %dynamic-slice_bitcast_fusion.1), channel_id=1, source_target_pairs={{0,2},{1,3},{2,0},{3,1},{4,6},{5,7},{6,4},{7,5},{8,10},{9,11},{10,... | collective-permute-start | bytes 344072 | tf_op jit(solution)/shard_map/ppermute | solution.py:479
  146.1 3.5 %collective-permute-done.1 = bf16[448,128]{1,0:T(8,128)(2,1)S(1)} collective-permute-done((bf16[448,128]{1,0:T(8,128)(2,1)S(1)}, bf16[448,128]{1,0:T(8,128)(2,1)S(1)}, u32[]{:S(2)}, u32[]{:S(2)}) %collective-permute-start.1) | collective-permute-done | bytes 114720 | tf_op jit(solution)/shard_map/ppermute | solution.py:479
  149.7 1.7 collective-permute-start.2
  151.4 2.4 %collective-permute-start.3 = (bf16[112,128]{1,0:T(8,128)(2,1)S(1)}, bf16[112,128]{1,0:T(8,128)(2,1)S(1)}, u32[]{:S(2)}, u32[]{:S(2)}) collective-permute-start(bf16[112,128]{1,0:T(8,128)(2,1)S(1)} %get-tuple-element.59), channel_id=1, source_target_pairs={{0,8},{1,9},{2,10},{3,11},{4,12},{5,13},{6,14},{7,15},{8,0},{9,1},... | collective-permute-start | bytes 86024 | tf_op jit(solution)/shard_map/ppermute | solution.py:479
  154.1 2.1 %collective-permute-done.3 = bf16[112,128]{1,0:T(8,128)(2,1)S(1)} collective-permute-done((bf16[112,128]{1,0:T(8,128)(2,1)S(1)}, bf16[112,128]{1,0:T(8,128)(2,1)S(1)}, u32[]{:S(2)}, u32[]{:S(2)}) %collective-permute-start.3) | collective-permute-done | bytes 28704 | tf_op jit(solution)/shard_map/ppermute | solution.py:479
  156.3 3.2 %collective-permute-done.4 = bf16[112,128]{1,0:T(8,128)(2,1)S(1)} collective-permute-done((bf16[112,128]{1,0:T(8,128)(2,1)S(1)}, bf16[112,128]{1,0:T(8,128)(2,1)S(1)}, u32[]{:S(2)}, u32[]{:S(2)}) %collective-permute-start.4) | collective-permute-done | bytes 28704 | tf_op jit(solution)/shard_map/ppermute | solution.py:479
  159.6 0.9 collective-permute-start.6
  160.5 3.5 %collective-permute-start.7 = (bf16[112,128]{1,0:T(8,128)(2,1)S(1)}, bf16[112,128]{1,0:T(8,128)(2,1)S(1)}, u32[]{:S(2)}, u32[]{:S(2)}) collective-permute-start(bf16[112,128]{1,0:T(8,128)(2,1)S(1)} %fusion.4), channel_id=1, source_target_pairs={{0,12},{1,13},{2,14},{3,15},{4,8},{5,9},{6,10},{7,11},{8,4},{9,5},... | collective-permute-start | bytes 86024 | tf_op jit(solution)/shard_map/ppermute | solution.py:489
  164.4 1.7 collective-permute-done.7
  166.2 1.7 collective-permute-start.8
  167.9 3.1 %collective-permute-done.8 = bf16[448,128]{1,0:T(8,128)(2,1)S(1)} collective-permute-done((bf16[448,128]{1,0:T(8,128)(2,1)S(1)}, bf16[448,128]{1,0:T(8,128)(2,1)S(1)}, u32[]{:S(2)}, u32[]{:S(2)}) %collective-permute-start.8) | collective-permute-done | bytes 114720 | tf_op jit(solution)/shard_map/ppermute | solution.py:489
  171.7 0.9 copy.33
  172.8 0.6 maximum_convert_fusion.2
  173.4 0.7 maximum_convert_fusion.1
  174.2 1.0 copy.36
  (47 shorter events, 3.6 us)
Async XLA Ops:
  0.6 19.4 %copy-start.4 = (bf16[2,1,2,48,512]{4,3,2,1,0:T(8,128)(2,1)S(1)}, bf16[2,1,2,48,512]{4,3,2,1,0:T(8,128)(2,1)}, u32[]{:S(2)}) copy-start(bf16[2,1,2,48,512]{4,3,2,1,0:T(8,128)(2,1)} %param.16) | copy-start | bytes 589828
  12.6 21.9 %all-to-all-start.1 = ((bf16[16,2,16,512]{3,2,1,0:T(8,128)(2,1)}), bf16[16,2,16,512]{3,2,1,0:T(8,128)(2,1)S(1)}, u32[]{:S(2)}, u32[]{:S(2)}) async-start(bf16[16,2,16,512]{3,2,1,0:T(8,128)(2,1)} %bitcast.87), calls=%async_computation.1 | async-start | bytes 1048576 | tf_op jit(solution)/shard_map/all_to_all | solution.py:446
  20.3 18.4 %copy-start.5 = (bf16[2,1,2,48,512]{4,3,2,1,0:T(8,128)(2,1)S(1)}, bf16[2,1,2,48,512]{4,3,2,1,0:T(8,128)(2,1)}, u32[]{:S(2)}) copy-start(bf16[2,1,2,48,512]{4,3,2,1,0:T(8,128)(2,1)} %param.19) | copy-start | bytes 589828
  32.3 6.9 %copy-start.6 = (s32[2]{0:T(128)S(1)}, s32[2]{0:T(128)}, u32[]{:S(2)}) copy-start(s32[2]{0:T(128)} %param.15) | copy-start | bytes 28
  32.3 7.0 %copy-start = (bf16[2,1,2,48,512]{4,3,2,1,0:T(8,128)(2,1)S(1)}, bf16[2,1,2,48,512]{4,3,2,1,0:T(8,128)(2,1)}, u32[]{:S(2)}) copy-start(bf16[2,1,2,48,512]{4,3,2,1,0:T(8,128)(2,1)} %param.17) | copy-start | bytes 589828
  32.3 7.0 %copy-start.1 = (bf16[2,1,2,48,512]{4,3,2,1,0:T(8,128)(2,1)S(1)}, bf16[2,1,2,48,512]{4,3,2,1,0:T(8,128)(2,1)}, u32[]{:S(2)}) copy-start(bf16[2,1,2,48,512]{4,3,2,1,0:T(8,128)(2,1)} %param.18) | copy-start | bytes 589828
  32.3 7.0 %copy-start.2 = (s32[512]{0:T(512)S(1)}, s32[512]{0:T(512)}, u32[]{:S(2)}) copy-start(s32[512]{0:T(512)} %param.14) | copy-start | bytes 6148
  34.5 18.6 %all-to-all-start = ((bf16[16,2,16,512]{3,2,1,0:T(8,128)(2,1)}), bf16[16,2,16,512]{3,2,1,0:T(8,128)(2,1)S(1)}, u32[]{:S(2)}, u32[]{:S(2)}) async-start(bf16[16,2,16,512]{3,2,1,0:T(8,128)(2,1)} %bitcast.85), calls=%async_computation | async-start | bytes 1048576 | tf_op jit(solution)/shard_map/all_to_all | solution.py:446
  53.0 18.7 %all-to-all-start.3 = ((bf16[16,2,16,512]{3,2,1,0:T(8,128)(2,1)}), bf16[16,2,16,512]{3,2,1,0:T(8,128)(2,1)}, u32[]{:S(2)}, u32[]{:S(2)}) async-start(bf16[16,2,16,512]{3,2,1,0:T(8,128)(2,1)} %get-tuple-element.22), calls=%async_computation.3 | async-start | bytes 1048576 | tf_op jit(solution)/shard_map/all_to_all | solution.py:446
  71.8 35.8 %all-to-all-start.2 = ((bf16[16,2,16,512]{3,2,1,0:T(8,128)(2,1)}), bf16[16,2,16,512]{3,2,1,0:T(8,128)(2,1)S(1)}, u32[]{:S(2)}, u32[]{:S(2)}) async-start(bf16[16,2,16,512]{3,2,1,0:T(8,128)(2,1)} %get-tuple-element.21), calls=%async_computation.2 | async-start | bytes 1048576 | tf_op jit(solution)/shard_map/all_to_all | solution.py:446
  107.6 0.8 copy-start.3
  141.5 1.6 collective-permute-start
  144.1 5.5 %collective-permute-start.1 = (bf16[448,128]{1,0:T(8,128)(2,1)S(1)}, bf16[448,128]{1,0:T(8,128)(2,1)S(1)}, u32[]{:S(2)}, u32[]{:S(2)}) collective-permute-start(bf16[448,128]{1,0:T(8,128)(2,1)S(1)} %dynamic-slice_bitcast_fusion.1), channel_id=1, source_target_pairs={{0,2},{1,3},{2,0},{3,1},{4,6},{5,7},{6,4},{7,5},{8,10},{9,11},{10,... | collective-permute-start | bytes 344072 | tf_op jit(solution)/shard_map/ppermute | solution.py:479
  149.7 4.5 %collective-permute-start.2 = (bf16[112,128]{1,0:T(8,128)(2,1)S(1)}, bf16[112,128]{1,0:T(8,128)(2,1)S(1)}, u32[]{:S(2)}, u32[]{:S(2)}) collective-permute-start(bf16[112,128]{1,0:T(8,128)(2,1)S(1)} %get-tuple-element.57), channel_id=1, source_target_pairs={{0,4},{1,5},{2,6},{3,7},{4,0},{5,1},{6,2},{7,3},{8,12},{9,13},{10,... | collective-permute-start | bytes 86024 | tf_op jit(solution)/shard_map/ppermute | solution.py:479
  151.4 4.9 %collective-permute-start.3 = (bf16[112,128]{1,0:T(8,128)(2,1)S(1)}, bf16[112,128]{1,0:T(8,128)(2,1)S(1)}, u32[]{:S(2)}, u32[]{:S(2)}) collective-permute-start(bf16[112,128]{1,0:T(8,128)(2,1)S(1)} %get-tuple-element.59), channel_id=1, source_target_pairs={{0,8},{1,9},{2,10},{3,11},{4,12},{5,13},{6,14},{7,15},{8,0},{9,1},... | collective-permute-start | bytes 86024 | tf_op jit(solution)/shard_map/ppermute | solution.py:479
  153.8 5.7 %collective-permute-start.4 = (bf16[112,128]{1,0:T(8,128)(2,1)S(1)}, bf16[112,128]{1,0:T(8,128)(2,1)S(1)}, u32[]{:S(2)}, u32[]{:S(2)}) collective-permute-start(bf16[112,128]{1,0:T(8,128)(2,1)S(1)} %get-tuple-element.58), channel_id=1, source_target_pairs={{0,12},{1,13},{2,14},{3,15},{4,8},{5,9},{6,10},{7,11},{8,4},{9,5},... | collective-permute-start | bytes 86024 | tf_op jit(solution)/shard_map/ppermute | solution.py:479
  159.5 4.5 %collective-permute-start.5 = (bf16[112,128]{1,0:T(8,128)(2,1)S(1)}, bf16[112,128]{1,0:T(8,128)(2,1)S(1)}, u32[]{:S(2)}, u32[]{:S(2)}) collective-permute-start(bf16[112,128]{1,0:T(8,128)(2,1)S(1)} %fusion.4), channel_id=1, source_target_pairs={{0,4},{1,5},{2,6},{3,7},{4,0},{5,1},{6,2},{7,3},{8,12},{9,13},{10,... | collective-permute-start | bytes 86024 | tf_op jit(solution)/shard_map/ppermute | solution.py:489
  159.6 4.8 %collective-permute-start.6 = (bf16[112,128]{1,0:T(8,128)(2,1)S(1)}, bf16[112,128]{1,0:T(8,128)(2,1)S(1)}, u32[]{:S(2)}, u32[]{:S(2)}) collective-permute-start(bf16[112,128]{1,0:T(8,128)(2,1)S(1)} %fusion.4), channel_id=1, source_target_pairs={{0,8},{1,9},{2,10},{3,11},{4,12},{5,13},{6,14},{7,15},{8,0},{9,1},... | collective-permute-start | bytes 86024 | tf_op jit(solution)/shard_map/ppermute | solution.py:489
  160.5 5.7 %collective-permute-start.7 = (bf16[112,128]{1,0:T(8,128)(2,1)S(1)}, bf16[112,128]{1,0:T(8,128)(2,1)S(1)}, u32[]{:S(2)}, u32[]{:S(2)}) collective-permute-start(bf16[112,128]{1,0:T(8,128)(2,1)S(1)} %fusion.4), channel_id=1, source_target_pairs={{0,12},{1,13},{2,14},{3,15},{4,8},{5,9},{6,10},{7,11},{8,4},{9,5},... | collective-permute-start | bytes 86024 | tf_op jit(solution)/shard_map/ppermute | solution.py:489
  166.2 4.9 %collective-permute-start.8 = (bf16[448,128]{1,0:T(8,128)(2,1)S(1)}, bf16[448,128]{1,0:T(8,128)(2,1)S(1)}, u32[]{:S(2)}, u32[]{:S(2)}) collective-permute-start(bf16[448,128]{1,0:T(8,128)(2,1)S(1)} %pad_maximum_fusion.2), channel_id=1, source_target_pairs={{0,2},{1,3},{2,0},{3,1},{4,6},{5,7},{6,4},{7,5},{8,10},{9,11},{10,... | collective-permute-start | bytes 344072 | tf_op jit(solution)/shard_map/ppermute | solution.py:489
  171.1 1.6 collective-permute-start.9

commit v5 on v1

--- a/solution.py
+++ b/solution.py
@@ -9,7 +9,6 @@
 from jax.sharding import PartitionSpec as P
 
 LEVELS = 200
-CHUNKS = 2
 
 
 sigma_high = 160.0
@@ -66,11 +65,11 @@
         clock += 1
 
 
-def for_rows(count, group, make_stages, lag):
+def for_groups(count, group, one_group):
     group = math.gcd(count, group)
 
     def step(at, carry):
-        interleave(lambda index: make_stages(at * group + index), group, lag)
+        one_group(at * group, group)
         return carry
 
     if count == group:
@@ -79,9 +78,37 @@
         lax.fori_loop(0, count // group, step, 0)
 
 
-def forward_kernel(pair_ref, w_in_t_ref, w_out_t_ref, w_bias_ref, bias_ref):
+def row_step(rows):
+    return math.gcd(rows, 8 if rows > 8 else 4)
+
+
+def is_direct(rows, crop):
+    return rows % 8 == 0 and crop % 128 == 0
+
+
+def forward_kernel(direct, first, pair_ref, w_bias_ref, *refs):
+    if first:
+        w_in_ref, w_out_ref, bias_ref, w_in_t_ref, w_out_t_ref, w_back_ref, w_half_ref = refs[:-1]
+    else:
+        w_in_t_ref, w_out_t_ref, bias_ref = refs[:-1]
+    lines_ref = refs[-1]
     width = w_out_t_ref.shape[1]
+    layers, heads, channels = w_bias_ref.shape
     piece = split_width(width)
+    step = pair_ref.shape[0]
+    first_row = pl.program_id(0) * step
+
+    if first:
+
+        @pl.when(pl.program_id(0) == 0)
+        def _():
+            w_in_t = w_in_ref[...].T
+            w_in_t_ref[:width, :] = w_in_t[:width] * 0.5
+            w_in_t_ref[width:, :] = w_in_t[width:]
+            w_out_t_ref[...] = w_out_ref[...].T
+            w_back_ref[:, :width] = w_in_ref[:, :width]
+            w_back_ref[:, width:] = w_in_ref[:, width:] * 2.0
+            w_half_ref[...] = w_out_ref[...] * 0.5
 
     def stages(row):
         pair_float = pair_ref[row].T.astype(F32)
@@ -97,59 +124,102 @@
             yield True
         normed_out = normalize(lifted)[0].astype(BF16)
         yield True
-        bias_ref[row] = mm(w_bias_ref[...], normed_out).astype(BF16)
-
-    for_rows(pair_ref.shape[0], 4, stages, 2)
-
-
-def forward_rows(chunk, rows, pair, w_in_half_t, w_out_t, w_bias):
+        bias = mm(w_bias_ref[...].reshape(layers * heads, channels), normed_out)
+        if direct:
+            tiles, total, tile = lines_ref.shape
+            rows = total // (layers * heads)
+            for layer in range(layers):
+                at = pl.ds(layer * rows + first_row + row, heads, stride=layers * rows)
+                lines = bias[layer * heads : (layer + 1) * heads]
+                for index in range(tiles):
+                    lines_ref[index, at, :] = lines[:, index * tile : (index + 1) * tile]
+        else:
+            bias_ref[row] = bias.astype(BF16)
+
+    for_groups(step, 4, lambda at, count: interleave(lambda i: stages(at + i), count, 2))
+
+    if direct:
+
+        @pl.when(pl.program_id(0) == pl.num_programs(0) - 1)
+        def _():
+            tiles, _, tile = lines_ref.shape
+            for index in range(tiles):
+                lines = lines_ref[index].reshape(bias_ref.shape[:2] + (tile,))
+                bias_ref[:, :, index * tile : (index + 1) * tile] = lines.astype(BF16)
+
+
+def whole_spec(array):
+    return pl.BlockSpec(array.shape, lambda i: (0,) * len(array.shape))
+
+
+def forward_rows(start, rows, pair, w_in, w_out, w_bias, prepared):
     crop, channels = pair.shape[1:]
-    lanes = w_bias.shape[0]
-    step = math.gcd(rows, 8)
-    steps = rows // step
+    layers, heads, _ = w_bias.shape
+    lanes = layers * heads
+    step = row_step(rows)
+    first_step = start // step
     positions = rows * crop
-    width = w_out_t.shape[1]
-    whole = lambda i: (0, 0)
+    width = w_out.shape[0]
+    direct = is_direct(rows, crop)
+    first = prepared is None
+    line_shape = (heads * layers, rows, crop) if direct else (rows, lanes, crop)
+    shapes = [jax.ShapeDtypeStruct(line_shape, BF16)]
+    out_specs = [
+        whole_spec(shapes[0])
+        if direct
+        else pl.BlockSpec((step, lanes, crop), lambda i: (i, 0, 0))
+    ]
+    if first:
+        operands = [pair, w_bias, w_in, w_out]
+        for shape in (w_in.shape[::-1], w_out.shape[::-1], w_in.shape, w_out.shape):
+            shapes.append(jax.ShapeDtypeStruct(shape, BF16))
+            out_specs.append(whole_spec(shapes[-1]))
+    else:
+        operands = [pair, w_bias, *prepared[:2]]
     return pl.pallas_call(
-        forward_kernel,
-        grid=(steps,),
-        in_specs=[
-            pl.BlockSpec((step, crop, channels), lambda i: (chunk * steps + i, 0, 0)),
-            pl.BlockSpec(w_in_half_t.shape, whole),
-            pl.BlockSpec(w_out_t.shape, whole),
-            pl.BlockSpec(w_bias.shape, whole),
+        functools.partial(forward_kernel, direct, first),
+        grid=(rows // step,),
+        in_specs=[pl.BlockSpec((step, crop, channels), lambda i: (first_step + i, 0, 0))]
+        + [whole_spec(array) for array in operands[1:]],
+        out_specs=out_specs,
+        out_shape=shapes,
+        scratch_shapes=[
+            pltpu.VMEM((crop // 128, lanes * rows, 128) if direct else (1, 8, 128), F32),
         ],
-        out_specs=pl.BlockSpec((step, lanes, crop), lambda i: (i, 0, 0)),
-        out_shape=jax.ShapeDtypeStruct((rows, lanes, crop), BF16),
-        compiler_params=pltpu.CompilerParams(vmem_limit_bytes=48 * 2**20),
+        compiler_params=pltpu.CompilerParams(vmem_limit_bytes=56 * 2**20),
         cost_estimate=pl.CostEstimate(
-            flops=2 * positions * channels * (3 * width + lanes),
+            flops=6 * positions * channels * (3 * width + lanes),
             bytes_accessed=positions * (channels + lanes) * 2,
             transcendentals=positions * width,
         ),
         name="pair_forward",
-    )(pair, w_in_half_t, w_out_t, w_bias)
+    )(*operands)
 
 
 def backward_kernel(
     first,
     last,
+    direct,
     pair_ref,
     d_bias_ref,
+    w_bias_ref,
     w_in_t_ref,
     w_out_t_ref,
-    w_bias_t_ref,
-    w_in_ref,
-    w_out_ref,
+    w_back_ref,
+    w_half_ref,
     *refs,
 ):
     if first:
         pair_grad_ref, sums_ref = refs[:2]
     else:
         before_ref, _, pair_grad_ref, sums_ref = refs[:4]
-    width = w_out_ref.shape[0]
+    lines_ref = refs[-1]
+    width = w_half_ref.shape[0]
+    layers, heads, channels = w_bias_ref.shape
+    lanes = layers * heads
     piece = split_width(width)
-    lanes = w_bias_t_ref.shape[1]
+    step = pair_ref.shape[0]
+    first_row = pl.program_id(0) * step
 
     @pl.when(pl.program_id(0) == 0)
     def _():
@@ -157,6 +227,22 @@
             sums_ref[...] = jnp.zeros_like(sums_ref)
         else:
             sums_ref[...] = before_ref[...]
+        if direct:
+            tiles, total, tile = lines_ref.shape
+            for index in range(tiles):
+                lines = d_bias_ref[:, :, index * tile : (index + 1) * tile].astype(F32)
+                lines_ref[index] = lines.reshape(total, tile)
+
+    def read_lines(row):
+        if not direct:
+            return d_bias_ref[row]
+        tiles, total, _ = lines_ref.shape
+        rows = total // lanes
+        found = []
+        for layer in range(layers):
+            at = pl.ds(layer * rows + first_row + row, heads, stride=layers * rows)
+            found.append(jnp.concatenate([lines_ref[index, at, :] for index in range(tiles)], 1))
+        return jnp.concatenate(found, 0).astype(BF16)
 
     def stages(row):
         pair_float = pair_ref[row].T.astype(F32)
@@ -179,81 +265,85 @@
         out_float, inv_out = normalize(lifted)
         normed_out = out_float.astype(BF16)
         yield True
-        d_bias = d_bias_ref[row]
-        d_normed = mm(w_bias_t_ref[...], d_bias)
-        sums_ref[3 * width : 3 * width + lanes, :] += mm(d_bias, normed_out, 1, 1)
+        d_bias = read_lines(row)
+        d_normed = mm(w_bias_ref[...].reshape(lanes, channels), d_bias, 0, 0)
+        sums_ref[3 * width :, :] += mm(d_bias, normed_out, 1, 1)
         d_lifted = norm_back(out_float, inv_out, d_normed)
         lifted_half = d_lifted.astype(BF16)
         yield True
-        d_normed_in = jnp.zeros_like(pair_float)
+        d_normed_in = None
         for index, (silu, slope, hidden) in enumerate(kept):
             at = index * piece
             cols = slice(at, at + piece)
             up_cols = slice(width + at, width + at + piece)
-            out_cols = slice(2 * width + at, 2 * width + at + piece)
-            d_hidden = mm(w_out_ref[cols, :], lifted_half)
-            sums_ref[out_cols, :] += mm(hidden, lifted_half, 1, 1)
+            d_hidden = mm(w_half_ref[cols, :], lifted_half)
+            sums_ref[2 * width + at : 2 * width + at + piece, :] += mm(hidden, lifted_half, 1, 1)
             yield True
-            d_gate = (0.5 * d_hidden * slope).astype(BF16)
+            d_gate = (d_hidden * slope).astype(BF16)
             d_up = (d_hidden * silu).astype(BF16)
-            d_normed_in = d_normed_in + mm(w_in_ref[:, cols], d_gate)
+            part = mm(w_back_ref[:, cols], d_gate)
             sums_ref[cols, :] += mm(d_gate, normed_in, 1, 1)
-            d_normed_in = d_normed_in + mm(w_in_ref[:, up_cols], d_up)
+            part = part + mm(w_back_ref[:, up_cols], d_up)
             sums_ref[up_cols, :] += mm(d_up, normed_in, 1, 1)
+            d_normed_in = part if d_normed_in is None else d_normed_in + part
             yield True
         pair_grad = d_lifted + norm_back(normed_float, inv_in, d_normed_in)
         pair_grad_ref[row] = pair_grad.astype(BF16).T
 
-    for_rows(pair_ref.shape[0], 4, stages, 3)
+    for_groups(step, 4, lambda at, count: interleave(lambda i: stages(at + i), count, 3))
 
     if last:
-        packed_ref = refs[-1]
+        packed_ref = refs[-2]
 
         @pl.when(pl.program_id(0) == pl.num_programs(0) - 1)
         def _():
             done = sums_ref.shape[0]
             packed_ref[:done, :] = sums_ref[...].astype(BF16)
+            packed_ref[width : 2 * width, :] = (2.0 * sums_ref[width : 2 * width, :]).astype(BF16)
             packed_ref[done:, :] = jnp.zeros((packed_ref.shape[0] - done, packed_ref.shape[1]), BF16)
 
 
-def backward_rows(chunk, chunks, rows, packed_rows, pair, d_bias, weights, state):
-    w_in_half_t, w_out_t, w_bias_t, w_in, w_out = weights
+def backward_rows(start, rows, packed_rows, pair, d_bias, w_bias, prepared, state):
     crop, channels = pair.shape[1:]
-    lanes = w_bias_t.shape[1]
-    width = w_out.shape[0]
-    step = math.gcd(rows, 8)
-    steps = rows // step
+    layers, heads, _ = w_bias.shape
+    lanes = layers * heads
+    width = prepared[3].shape[0]
+    step = row_step(rows)
+    first_step = start // step
     positions = rows * crop
-    first, last = chunk == 0, chunk == chunks - 1
-    whole = lambda i: (0, 0)
-    pair_spec = pl.BlockSpec((step, crop, channels), lambda i: (chunk * steps + i, 0, 0))
-    in_specs = [pair_spec, pl.BlockSpec((step, lanes, crop), lambda i: (i, 0, 0))]
-    in_specs += [pl.BlockSpec(w.shape, whole) for w in weights]
-    operands = [pair, d_bias, *weights]
+    first, last = start == 0, start + rows == pair.shape[0]
+    direct = is_direct(rows, crop)
+    pair_spec = pl.BlockSpec((step, crop, channels), lambda i: (first_step + i, 0, 0))
+    line_spec = whole_spec(d_bias) if direct else pl.BlockSpec((step, lanes, crop), lambda i: (i, 0, 0))
+    operands = [pair, d_bias, w_bias, *prepared]
+    in_specs = [pair_spec, line_spec] + [whole_spec(array) for array in operands[2:]]
     aliases = {}
     if not first:
         pair_grad, sums = state
         operands += [sums, pair_grad]
-        in_specs += [pl.BlockSpec(sums.shape, whole), pl.BlockSpec(memory_space=pl.ANY)]
+        in_specs += [whole_spec(sums), pl.BlockSpec(memory_space=pl.ANY)]
         aliases = {len(operands) - 1: 0}
     shapes = [
         jax.ShapeDtypeStruct(pair.shape, BF16),
         jax.ShapeDtypeStruct((3 * width + lanes, channels), F32),
     ]
-    out_specs = [pair_spec, pl.BlockSpec(shapes[1].shape, whole)]
+    out_specs = [pair_spec, whole_spec(shapes[1])]
     if last:
         shapes.append(jax.ShapeDtypeStruct((packed_rows, channels), BF16))
-        out_specs.append(pl.BlockSpec(shapes[2].shape, whole))
+        out_specs.append(whole_spec(shapes[2]))
     return pl.pallas_call(
-        functools.partial(backward_kernel, first, last),
-        grid=(steps,),
+        functools.partial(backward_kernel, first, last, direct),
+        grid=(rows // step,),
         in_specs=in_specs,
         out_specs=out_specs,
         out_shape=shapes,
         input_output_aliases=aliases,
+        scratch_shapes=[
+            pltpu.VMEM((crop // 128, lanes * rows, 128) if direct else (1, 8, 128), F32),
+        ],
         compiler_params=pltpu.CompilerParams(vmem_limit_bytes=56 * 2**20),
         cost_estimate=pl.CostEstimate(
-            flops=2 * positions * channels * (9 * width + 2 * lanes),
+            flops=6 * positions * channels * (9 * width + 2 * lanes),
             bytes_accessed=positions * (2 * channels + lanes) * 2,
             transcendentals=positions * width,
         ),
@@ -300,10 +390,9 @@
     d_bias_ref[:, 0] = total.astype(BF16).reshape(sources, rows, crop)
 
 
-def attend_rows(chunk, chunks, weights, bias, valid, query, key, value, grad, state):
+def attend_rows(first, last, weights, bias, valid, query, key, value, grad, state):
     sources, layers, rows, crop = bias.shape
     samples, depth, row_count = query.shape[1:]
-    first, last = chunk == 0, chunk == chunks - 1
     vec = lambda shape: pl.BlockSpec((1,) + shape[1:], lambda l: (l, 0, 0, 0))
     plane = pl.BlockSpec((sources, 1, rows, crop), lambda l: (0, l, 0, 0))
     in_specs = [
@@ -333,7 +422,7 @@
         ],
         compiler_params=pltpu.CompilerParams(vmem_limit_bytes=48 * 2**20),
         cost_estimate=pl.CostEstimate(
-            flops=10 * layers * samples * depth * row_count * crop,
+            flops=200 * layers * samples * depth * row_count * crop,
             bytes_accessed=layers * crop * (4 * row_count + 12 * samples * depth),
             transcendentals=layers * samples * row_count * crop,
         ),
@@ -341,8 +430,31 @@
     )(*operands)
 
 
-def swap(array):
-    return lax.all_to_all(array, "tok", split_axis=0, concat_axis=0, tiled=True)
+def swap(array, teams=None):
+    return lax.all_to_all(
+        array, "tok", split_axis=0, concat_axis=0, tiled=True, axis_index_groups=teams
+    )
+
+
+def sum_over_devices(array):
+    devices = lax.axis_size("tok")
+    parity = lax.axis_index("tok") % 2
+    across = [(index, index ^ 1) for index in range(devices)]
+    teams = [list(range(odd, devices, 2)) for odd in range(2)]
+    total, channels = array.shape
+    share = total // devices
+    halves = array.reshape(2, total // 2, channels)
+    theirs = lax.ppermute(lax.dynamic_index_in_dim(halves, 1 - parity, 0, False), "tok", across)
+    mine = lax.dynamic_index_in_dim(halves, parity, 0, False)
+    mine = (mine.astype(F32) + theirs.astype(F32)).astype(BF16)
+    parts = swap(mine.reshape(devices // 2, share, channels), teams)
+    summed = jnp.sum(parts.astype(F32), 0).astype(BF16)
+    copies = jnp.broadcast_to(summed[None], (devices // 2, share, channels))
+    mine = swap(copies, teams).reshape(total // 2, channels)
+    theirs = lax.ppermute(mine, "tok", across)
+    even = parity == 0
+    summed = jnp.concatenate([jnp.where(even, mine, theirs), jnp.where(even, theirs, mine)], 0)
+    return summed.astype(F32)
 
 
 def body(
@@ -363,90 +475,92 @@
     devices = lax.axis_size("tok")
     groups = devices // heads
     samples, depth = query_states.shape[2:4]
-    chunks = CHUNKS
-    rows = row_count // chunks
     lanes = heads * layers
-
-    halves = jnp.concatenate([jnp.full((width,), 0.5, BF16), jnp.ones((width,), BF16)])
-    w_in_half_t = (weight_in * halves[None, :]).T
-    w_out_t = weight_out.T
-    w_bias = jnp.transpose(weight_bias, (2, 0, 1)).reshape(lanes, channels)
-    pair_weights = (w_in_half_t, w_out_t, w_bias.T, weight_in, weight_out)
+    sizes = [row_count]
+    if row_count % 32 == 0:
+        sizes = [row_count // 4, row_count - row_count // 4]
+    starts = [sum(sizes[:index]) for index in range(len(sizes))]
+    w_bias = jnp.transpose(weight_bias, (0, 2, 1))
 
     group = lax.axis_index("tok") // heads
     weights = sample_weight(lax.dynamic_slice_in_dim(noise_level, group * samples, samples))
     valid = key_mask[None, :]
 
-    def by_chunk(array):
-        cut = array[:, 0].reshape(layers, samples, depth, devices, chunks, rows)
-        cut = jnp.transpose(cut, (4, 0, 1, 2, 3, 5))
-        return cut.reshape(chunks, layers, samples, depth, devices * rows)
-
-    queries, grads = by_chunk(query_states), by_chunk(output_grad)
+    def take_rows(array, start, rows):
+        cut = array[:, 0].reshape(layers, samples, depth, devices, row_count)
+        cut = cut[..., start : start + rows]
+        return cut.reshape(layers, samples, depth, devices * rows)
 
     arrived = []
-    for chunk in range(chunks):
-        bias = forward_rows(chunk, rows, pair_states, w_in_half_t, w_out_t, w_bias)
-        bias = jnp.transpose(bias, (1, 0, 2)).reshape(heads, layers, rows, crop)
-        arrived.append(swap(jnp.tile(bias, (groups, 1, 1, 1))))
+    prepared = None
+    for start, rows in zip(starts, sizes):
+        bias, *made = forward_rows(
+            start, rows, pair_states, weight_in, weight_out, w_bias, prepared
+        )
+        prepared = prepared or made
+        if is_direct(rows, crop):
+            bias = bias.reshape(heads, layers, rows, crop)
+        else:
+            bias = jnp.transpose(bias.reshape(rows, layers, heads, crop), (2, 1, 0, 3))
+        if groups > 1:
+            bias = jnp.tile(bias, (groups, 1, 1, 1))
+        arrived.append(swap(bias))
 
     returned = []
     d_queries = []
     state = None
-    for chunk in range(chunks):
-        bias = arrived[chunk]
-        flat = rows % 16 != 0
-        if flat:
+    for start, rows, bias in zip(starts, sizes, arrived):
+        direct = is_direct(rows, crop)
+        if not direct:
             bias = jnp.transpose(bias, (1, 0, 2, 3)).reshape(1, layers, devices * rows, crop)
         d_query, d_key, d_value, d_bias = attend_rows(
-            chunk,
-            chunks,
+            start == 0,
+            start + rows == row_count,
             weights,
             bias,
             valid,
-            queries[chunk],
+            take_rows(query_states, start, rows),
             key_states[:, 0],
             value_states[:, 0],
-            grads[chunk],
+            take_rows(output_grad, start, rows),
             state,
         )
         state = (d_key, d_value)
-        d_queries.append(d_query)
-        if flat:
+        d_queries.append(d_query.reshape(layers, samples, depth, devices, rows))
+        if not direct:
             d_bias = jnp.transpose(d_bias.reshape(layers, devices, rows, crop), (1, 0, 2, 3))
         returned.append(swap(d_bias))
 
     sum_rows = 3 * width + lanes
-    share = 16 * -(-sum_rows // (16 * devices))
+    packed_rows = 8 * devices * -(-sum_rows // (8 * devices))
     pair_state = None
-    for chunk in range(chunks):
-        d_bias = returned[chunk]
+    for start, rows, d_bias in zip(starts, sizes, returned):
         if groups > 1:
             d_bias = d_bias.reshape(groups, heads, layers, rows, crop).astype(F32)
             d_bias = jnp.sum(d_bias, 0).astype(BF16)
-        d_bias = jnp.transpose(d_bias.reshape(lanes, rows, crop), (1, 0, 2))
+        if is_direct(rows, crop):
+            d_bias = d_bias.reshape(lanes, rows, crop)
+        else:
+            d_bias = jnp.transpose(d_bias, (2, 1, 0, 3)).reshape(rows, lanes, crop)
         pair_state = backward_rows(
-            chunk,
-            chunks,
+            start,
             rows,
-            share * devices,
+            packed_rows,
             pair_states,
             d_bias,
-            pair_weights,
+            w_bias,
+            prepared,
             pair_state and pair_state[:2],
         )
     pair_grad, _, packed = pair_state
 
-    parts = swap(packed.reshape(devices, share, channels))
-    summed = jnp.sum(parts.astype(F32), 0).astype(BF16)
-    summed = lax.all_gather(summed, "tok", axis=0, tiled=True).astype(F32)
+    summed = sum_over_devices(packed)
     grad_in = summed[: 2 * width].T
     grad_out = summed[2 * width : 3 * width]
-    grad_bias = summed[3 * width : sum_rows].reshape(heads, layers, channels)
-    grad_bias = jnp.transpose(grad_bias, (1, 2, 0))
-
-    d_query = jnp.stack(d_queries, 0).reshape(chunks, layers, samples, depth, devices, rows)
-    d_query = jnp.transpose(d_query, (1, 2, 3, 4, 0, 5)).reshape(query_states.shape)
+    grad_bias = summed[3 * width : sum_rows].reshape(layers, heads, channels)
+    grad_bias = jnp.transpose(grad_bias, (0, 2, 1))
+
+    d_query = jnp.concatenate(d_queries, -1).reshape(query_states.shape)
     return (
         pair_grad,
         d_query,

time: 199 us -> 171 us (0.86)
  waiting for transfers between devices: 34.4 us -> 18.7 us
  blocking collectives: 39.2 us -> 24.7 us
  local copies, waits for them, and re-layouts: 17.2 us -> 10.8 us
  Pallas kernels: 84.9 us -> 89.8 us
  starting transfers between devices: 20.6 us -> 22.9 us
    all_gather x1 -> x0, blocking collectives: 20.9 us -> none  [body(): summed = lax.all_gather(summed, 'tok', axis=0, tiled=True).astype(F32)]
    all_to_all x4, waiting for transfers between devices: 34.4 us -> 17.4 us  [swap(): lax.all_to_all(array, 'tok', split_axis=0, concat_axis=0, tiled=True, axi...]
    unnamed x27 -> x18, local copies, waits for them, and re-layouts: 9.7 us -> 2.79 us
    all_to_all x1 -> x2, blocking collectives: 18.4 us -> 24.7 us  [swap(): lax.all_to_all(array, 'tok', split_axis=0, concat_axis=0, tiled=True, axi...]
    pallas_call x4, Pallas kernels: 76.4 us -> 81.4 us  [the longest x2 56.3 us: backward_rows(): pl.pallas_call(functools.partial(backward_kernel, first, last, direct), g...]
    slice x4 -> x6, local copies, waits for them, and re-layouts: 0.8 us -> 5.19 us  [take_rows(): cut = cut[..., start:start + rows]]
    transpose x4 -> x0, local copies, waits for them, and re-layouts: 2.91 us -> none  [the longest x2 2.17 us: body(): bias = jnp.transpose(bias, (1, 0, 2)).reshape(heads, layers, rows, crop)]
    reshape x3 -> x4, local copies, waits for them, and re-layouts: 2.89 us -> 0.55 us  [take_rows(): return cut.reshape(layers, samples, depth, devices * rows)]
  transfers between devices with their start and end apart: 4 -> 6, of which waited for: 4 -> 5; matrix products, arithmetic and copies ran while one was open for 3% -> 5% of each run, Pallas kernels for 7% -> 24%
where the time goes in v5:
time: 171 us; the launch traced here: 170 us
  Pallas kernels  89.8 us (53%)
  blocking collectives  24.7 us (14%)
  starting transfers between devices  22.9 us (13%)
  waiting for transfers between devices  18.7 us (11%)
  local copies, waits for them, and re-layouts  10.8 us (6%)
  other arithmetic  2.57 us (2%)
    pallas_call x2, Pallas kernels, backward_rows(): pl.pallas_call(functools.partial(backward_kernel, first, last, direct), g...  56.3 us
    pallas_call x2, Pallas kernels, forward_rows(): pl.pallas_call(functools.partial(forward_kernel, direct, first), grid=(ro...  25.2 us
    all_to_all x2, blocking collectives, swap(): lax.all_to_all(array, 'tok', split_axis=0, concat_axis=0, tiled=True, axi...  24.7 us
    all_to_all x4, starting transfers between devices, swap(): lax.all_to_all(array, 'tok', split_axis=0, concat_axis=0, tiled=True, axi...  22.6 us
    all_to_all x4, waiting for transfers between devices, swap(): lax.all_to_all(array, 'tok', split_axis=0, concat_axis=0, tiled=True, axi...  17.4 us
    pallas_call x2, Pallas kernels, attend_rows(): pl.pallas_call(functools.partial(attend_kernel, first, last), grid=(layer...  8.33 us
    slice x6, local copies, waits for them, and re-layouts, take_rows(): cut = cut[..., start:start + rows]  5.19 us
  transfers between devices with their start and end apart: 6, of which 5 were waited for; matrix products, arithmetic and copies ran while one was open for 5% of the time, Pallas kernels for 24%

profile of v5, /device:TPU:0, one launch (start us, length us, event | category | flops | bytes accessed | tf_op | source)
XLA Modules:
  0.0 170.4 jit_solution(9051944066019722516)
XLA Ops:
  0.6 7.4 %pair_forward.2 = (bf16[32,8,512]{2,1,0:T(8,128)(2,1)}, bf16[1024,128]{1,0:T(8,128)(2,1)}, bf16[128,512]{1,0:T(8,128)(2,1)}, bf16[128,1024]{1,0:T(8,128)(2,1)}, bf16[512,128]{1,0:T(8,128)(2,1)}) custom-call(bf16[32,512,128]{2,1,0:T(8,128)(2,1)} %pair_ref.7, bf16[2,16,128]{2,1,0:T(8,128)(2,1)} %bitcast.66, bf16[128,1024]{1,0:T(8,128)(2,1)} %refs_0_.1, ...), custom_call_target="tpu_custom_call" | custom-call | flops 4932501504 | bytes 1310720 | tf_op jit(solution)/shard_map/pair_forward/pallas_call | solution.py:179
  8.1 7.4 %all-to-all-start.1 = ((bf16[16,2,8,512]{3,2,1,0:T(8,128)(2,1)}), bf16[16,2,8,512]{3,2,1,0:T(8,128)(2,1)S(1)}, u32[]{:S(2)}, u32[]{:S(2)}) async-start(bf16[16,2,8,512]{3,2,1,0:T(8,128)(2,1)} %bitcast.64), calls=%async_computation.1 | async-start | bytes 524288 | tf_op jit(solution)/shard_map/all_to_all | solution.py:434
  15.5 17.7 %pair_forward.3 = bf16[32,24,512]{2,1,0:T(8,128)(2,1)} custom-call(bf16[32,512,128]{2,1,0:T(8,128)(2,1)} %pair_ref.7, bf16[2,16,128]{2,1,0:T(8,128)(2,1)} %bitcast.67, bf16[1024,128]{1,0:T(8,128)(2,1)} %get-tuple-element.24.refs_0_.w_in_t_ref, bf16[128,512]{1,0:T(8,128)(2,1)} %get-tuple-element.25.refs_1_.w_out_t_ref), custom_call_target="tpu_custom_call" | custom-call | flops 14797504512 | bytes 3932160 | tf_op jit(solution)/shard_map/pair_forward/pallas_call | solution.py:179
  33.2 6.1 %all-to-all-start = ((bf16[16,2,24,512]{3,2,1,0:T(8,128)(2,1)}), bf16[16,2,24,512]{3,2,1,0:T(8,128)(2,1)S(1)}, u32[]{:S(2)}, u32[]{:S(2)}) async-start(bf16[16,2,24,512]{3,2,1,0:T(8,128)(2,1)} %bitcast.57), calls=%async_computation | async-start | bytes 1572864 | tf_op jit(solution)/shard_map/all_to_all | solution.py:434
  39.4 0.4 reshape_squeeze.8
  39.8 0.3 slice.28
  40.1 0.7 copy.23
  40.9 0.4 reshape_squeeze.9
  41.4 1.2 slice.29
  42.5 0.7 copy.24
  43.3 0.7 copy.21
  44.2 1.7 %copy.22 = bf16[2,2,48,16,24]{2,4,3,1,0:T(8,128)(2,1)S(1)} copy(bf16[2,2,48,16,24]{4,3,2,1,0:T(8,128)(2,1)} %slice.29) | data formatting | bytes 294912 | tf_op jit(solution)/shard_map/slice | solution.py:491
  46.1 3.5 %attention_backward.2 = (bf16[2,2,48,128]{3,2,1,0:T(8,128)(2,1)S(1)}, f32[2,2,48,512]{3,2,1,0:T(8,128)S(1)}, f32[2,2,48,512]{3,2,1,0:T(8,128)S(1)}, bf16[16,2,8,512]{3,2,1,0:T(8,128)(2,1)}) custom-call(f32[2]{0:T(128)S(1)} %multiply_divide_fusion.weight_ref, bf16[16,2,8,512]{3,2,1,0:T(8,128)(2,1)S(1)} %all-to-all-done.1.bias_ref, s32[1,512]{1,0:T(1,128)S(1)} %bitcast.46, ...), custom_call_target="tpu_custom_call" | custom-call | flops 2516582400 | bytes 1703936 | tf_op jit(solution)/shard_map/attention_backward/pallas_call | solution.py:412
  49.7 8.4 %all-to-all-done.bias_ref = bf16[16,2,24,512]{3,2,1,0:T(8,128)(2,1)S(1)} async-done(((bf16[16,2,24,512]{3,2,1,0:T(8,128)(2,1)}), bf16[16,2,24,512]{3,2,1,0:T(8,128)(2,1)S(1)}, u32[]{:S(2)}, u32[]{:S(2)}) %all-to-all-start) | async-done | bytes 786464 | tf_op jit(solution)/shard_map/all_to_all | solution.py:434
  58.1 5.5 %all-to-all-start.3 = ((bf16[16,2,8,512]{3,2,1,0:T(8,128)(2,1)}), bf16[16,2,8,512]{3,2,1,0:T(8,128)(2,1)S(1)}, u32[]{:S(2)}, u32[]{:S(2)}) async-start(bf16[16,2,8,512]{3,2,1,0:T(8,128)(2,1)} %get-tuple-element.32), calls=%async_computation.3 | async-start | bytes 524288 | tf_op jit(solution)/shard_map/all_to_all | solution.py:434
  63.5 4.8 %attention_backward.3 = (bf16[2,2,48,384]{3,2,1,0:T(8,128)(2,1)S(1)}, bf16[2,2,48,512]{3,2,1,0:T(8,128)(2,1)}, bf16[2,2,48,512]{3,2,1,0:T(8,128)(2,1)}, bf16[16,2,24,512]{3,2,1,0:T(8,128)(2,1)}) custom-call(f32[2]{0:T(128)S(1)} %multiply_divide_fusion.weight_ref, bf16[16,2,24,512]{3,2,1,0:T(8,128)(2,1)S(1)} %all-to-all-done.bias_ref, s32[1,512]{1,0:T(1,128)S(1)} %bitcast.47, ...), custom_call_target="tpu_custom_call" | custom-call | flops 7549747200 | bytes 2752512 | tf_op jit(solution)/shard_map/attention_backward/pallas_call | solution.py:412
  68.3 5.2 %all-to-all-done.3 = bf16[16,2,8,512]{3,2,1,0:T(8,128)(2,1)S(1)} async-done(((bf16[16,2,8,512]{3,2,1,0:T(8,128)(2,1)}), bf16[16,2,8,512]{3,2,1,0:T(8,128)(2,1)S(1)}, u32[]{:S(2)}, u32[]{:S(2)}) %all-to-all-start.3) | async-done | bytes 262176 | tf_op jit(solution)/shard_map/all_to_all | solution.py:434
  73.6 3.6 %all-to-all-start.2 = ((bf16[16,2,24,512]{3,2,1,0:T(8,128)(2,1)}), bf16[16,2,24,512]{3,2,1,0:T(8,128)(2,1)S(1)}, u32[]{:S(2)}, u32[]{:S(2)}) async-start(bf16[16,2,24,512]{3,2,1,0:T(8,128)(2,1)} %get-tuple-element.29), calls=%async_computation.2 | async-start | bytes 1572864 | tf_op jit(solution)/shard_map/all_to_all | solution.py:434
  77.2 14.9 %pair_backward.2 = (bf16[32,512,128]{2,1,0:T(8,128)(2,1)}, f32[1568,128]{1,0:T(8,128)}) custom-call(bf16[32,512,128]{2,1,0:T(8,128)(2,1)} %pair_ref.7, bf16[32,8,512]{2,1,0:T(8,128)(2,1)} %bitcast.63, bf16[2,16,128]{2,1,0:T(8,128)(2,1)} %bitcast.68, bf16[1024,128]{1,0:T(8,128)(2,1)} %get-tuple-element.24.refs_0_.w_in_t_ref, ...), custom_call_target="tpu_custom_call" | custom-call | flops 14696841216 | bytes 2359296 | tf_op jit(solution)/shard_map/pair_backward/pallas_call | solution.py:334
  92.1 3.8 %all-to-all-done.2 = bf16[16,2,24,512]{3,2,1,0:T(8,128)(2,1)S(1)} async-done(((bf16[16,2,24,512]{3,2,1,0:T(8,128)(2,1)}), bf16[16,2,24,512]{3,2,1,0:T(8,128)(2,1)S(1)}, u32[]{:S(2)}, u32[]{:S(2)}) %all-to-all-start.2) | async-done | bytes 786464 | tf_op jit(solution)/shard_map/all_to_all | solution.py:434
  95.9 0.9 copy-done.3
  96.8 41.4 %pair_backward.3 = (bf16[32,512,128]{2,1,0:T(8,128)(2,1)}, f32[1568,128]{1,0:T(8,128)}, bf16[1664,128]{1,0:T(8,128)(2,1)}) custom-call(bf16[32,512,128]{2,1,0:T(8,128)(2,1)} %pair_ref.7, bf16[32,24,512]{2,1,0:T(8,128)(2,1)} %bitcast.56, bf16[2,16,128]{2,1,0:T(8,128)(2,1)} %bitcast.69, ...), custom_call_target="tpu_custom_call", output_to_operand_aliasing={{0}: (8, {})} | custom-call | flops 44090523648 | bytes 7077888 | tf_op jit(solution)/shard_map/pair_backward/pallas_call | solution.py:334
  138.1 0.9 dynamic-slice_bitcast_fusion
  139.1 0.3 collective-permute-start
  139.4 1.2 collective-permute-done
  140.6 1.0 fusion
  141.6 13.8 %all_to_all.30 = bf16[8,104,128]{2,1,0:T(8,128)(2,1)S(1)} all-to-all(bf16[8,104,128]{2,1,0:T(8,128)(2,1)S(1)} %bitcast.55), channel_id=1, replica_groups={{0,2,4,6,8,10,12,14},{1,3,5,7,9,11,13,15},{16,18,20,22,24,26,28,30},{17..., dimensions={0} | all-to-all | bytes 425984 | tf_op jit(solution)/shard_map/all_to_all | solution.py:434
  155.5 11.0 %all_to_all.31 = bf16[8,104,128]{2,1,0:T(8,128)(2,1)S(1)} all-to-all(bf16[8,104,128]{2,1,0:T(8,128)(2,1)S(1)} %broadcast_in_dim.18), channel_id=1, replica_groups={{0,2,4,6,8,10,12,14},{1,3,5,7,9,11,13,15},{16,18,20,22,24,26,28,30},{17..., dimensions={0} | all-to-all | bytes 425984 | tf_op jit(solution)/shard_map/all_to_all | solution.py:434
  166.9 0.9 copy.32
  167.9 0.6 maximum_convert_fusion.2
  168.6 0.7 maximum_convert_fusion.1
  169.4 1.0 copy.35
  (31 shorter events, 1.4 us)
Async XLA Ops:
  8.1 25.1 %all-to-all-start.1 = ((bf16[16,2,8,512]{3,2,1,0:T(8,128)(2,1)}), bf16[16,2,8,512]{3,2,1,0:T(8,128)(2,1)S(1)}, u32[]{:S(2)}, u32[]{:S(2)}) async-start(bf16[16,2,8,512]{3,2,1,0:T(8,128)(2,1)} %bitcast.64), calls=%async_computation.1 | async-start | bytes 524288 | tf_op jit(solution)/shard_map/all_to_all | solution.py:434
  15.5 23.9 %copy-start.5 = (bf16[2,1,2,48,512]{4,3,2,1,0:T(8,128)(2,1)S(1)}, bf16[2,1,2,48,512]{4,3,2,1,0:T(8,128)(2,1)}, u32[]{:S(2)}) copy-start(bf16[2,1,2,48,512]{4,3,2,1,0:T(8,128)(2,1)} %param.16) | copy-start | bytes 589828
  33.2 7.7 %copy-start.6 = (bf16[2,1,2,48,512]{4,3,2,1,0:T(8,128)(2,1)S(1)}, bf16[2,1,2,48,512]{4,3,2,1,0:T(8,128)(2,1)}, u32[]{:S(2)}) copy-start(bf16[2,1,2,48,512]{4,3,2,1,0:T(8,128)(2,1)} %param.19) | copy-start | bytes 589828
  33.2 24.8 %all-to-all-start = ((bf16[16,2,24,512]{3,2,1,0:T(8,128)(2,1)}), bf16[16,2,24,512]{3,2,1,0:T(8,128)(2,1)S(1)}, u32[]{:S(2)}, u32[]{:S(2)}) async-start(bf16[16,2,24,512]{3,2,1,0:T(8,128)(2,1)} %bitcast.57), calls=%async_computation | async-start | bytes 1572864 | tf_op jit(solution)/shard_map/all_to_all | solution.py:434
  40.1 6.0 %copy-start.7 = (s32[2]{0:T(128)S(1)}, s32[2]{0:T(128)}, u32[]{:S(2)}) copy-start(s32[2]{0:T(128)} %param.15) | copy-start | bytes 28
  40.1 6.0 %copy-start = (bf16[2,1,2,48,512]{4,3,2,1,0:T(8,128)(2,1)S(1)}, bf16[2,1,2,48,512]{4,3,2,1,0:T(8,128)(2,1)}, u32[]{:S(2)}) copy-start(bf16[2,1,2,48,512]{4,3,2,1,0:T(8,128)(2,1)} %param.17) | copy-start | bytes 589828
  40.1 6.0 %copy-start.1 = (bf16[2,1,2,48,512]{4,3,2,1,0:T(8,128)(2,1)S(1)}, bf16[2,1,2,48,512]{4,3,2,1,0:T(8,128)(2,1)}, u32[]{:S(2)}) copy-start(bf16[2,1,2,48,512]{4,3,2,1,0:T(8,128)(2,1)} %param.18) | copy-start | bytes 589828
  40.1 6.0 %copy-start.2 = (s32[512]{0:T(512)S(1)}, s32[512]{0:T(512)}, u32[]{:S(2)}) copy-start(s32[512]{0:T(512)} %param.14) | copy-start | bytes 6148
  58.1 15.5 %all-to-all-start.3 = ((bf16[16,2,8,512]{3,2,1,0:T(8,128)(2,1)}), bf16[16,2,8,512]{3,2,1,0:T(8,128)(2,1)S(1)}, u32[]{:S(2)}, u32[]{:S(2)}) async-start(bf16[16,2,8,512]{3,2,1,0:T(8,128)(2,1)} %get-tuple-element.32), calls=%async_computation.3 | async-start | bytes 524288 | tf_op jit(solution)/shard_map/all_to_all | solution.py:434
  73.6 3.6 %copy-start.4 = (bf16[16,2,8,512]{3,2,1,0:T(8,128)(2,1)}, bf16[16,2,8,512]{3,2,1,0:T(8,128)(2,1)S(1)}, u32[]{:S(2)}) copy-start(bf16[16,2,8,512]{3,2,1,0:T(8,128)(2,1)S(1)} %all-to-all-done.3) | copy-start | bytes 786436
  73.6 22.3 %all-to-all-start.2 = ((bf16[16,2,24,512]{3,2,1,0:T(8,128)(2,1)}), bf16[16,2,24,512]{3,2,1,0:T(8,128)(2,1)S(1)}, u32[]{:S(2)}, u32[]{:S(2)}) async-start(bf16[16,2,24,512]{3,2,1,0:T(8,128)(2,1)} %get-tuple-element.29), calls=%async_computation.2 | async-start | bytes 1572864 | tf_op jit(solution)/shard_map/all_to_all | solution.py:434
  95.9 0.9 copy-start.3
  139.1 1.5 collective-permute-start
  166.4 1.5 collective-permute-start.1

commit v6 on v5

--- a/solution.py
+++ b/solution.py
@@ -88,7 +88,7 @@
 
 def forward_kernel(direct, first, pair_ref, w_bias_ref, *refs):
     if first:
-        w_in_ref, w_out_ref, bias_ref, w_in_t_ref, w_out_t_ref, w_back_ref, w_half_ref = refs[:-1]
+        w_in_ref, w_out_ref, bias_ref, w_in_t_ref, w_out_t_ref = refs[:-1]
     else:
         w_in_t_ref, w_out_t_ref, bias_ref = refs[:-1]
     lines_ref = refs[-1]
@@ -106,9 +106,6 @@
             w_in_t_ref[:width, :] = w_in_t[:width] * 0.5
             w_in_t_ref[width:, :] = w_in_t[width:]
             w_out_t_ref[...] = w_out_ref[...].T
-            w_back_ref[:, :width] = w_in_ref[:, :width]
-            w_back_ref[:, width:] = w_in_ref[:, width:] * 2.0
-            w_half_ref[...] = w_out_ref[...] * 0.5
 
     def stages(row):
         pair_float = pair_ref[row].T.astype(F32)
@@ -136,7 +133,7 @@
         else:
             bias_ref[row] = bias.astype(BF16)
 
-    for_groups(step, 4, lambda at, count: interleave(lambda i: stages(at + i), count, 2))
+    for_groups(step, 4, lambda at, count: interleave(lambda i: stages(at + i), count, 3))
 
     if direct:
 
@@ -171,11 +168,11 @@
     ]
     if first:
         operands = [pair, w_bias, w_in, w_out]
-        for shape in (w_in.shape[::-1], w_out.shape[::-1], w_in.shape, w_out.shape):
+        for shape in (w_in.shape[::-1], w_out.shape[::-1]):
             shapes.append(jax.ShapeDtypeStruct(shape, BF16))
             out_specs.append(whole_spec(shapes[-1]))
     else:
-        operands = [pair, w_bias, *prepared[:2]]
+        operands = [pair, w_bias, *prepared]
     return pl.pallas_call(
         functools.partial(forward_kernel, direct, first),
         grid=(rows // step,),
@@ -199,7 +196,10 @@
 def backward_kernel(
     first,
     last,
+    sums,
+    grads,
     direct,
+    base,
     pair_ref,
     d_bias_ref,
     w_bias_ref,
@@ -209,23 +209,28 @@
     w_half_ref,
     *refs,
 ):
-    if first:
-        pair_grad_ref, sums_ref = refs[:2]
-    else:
-        before_ref, _, pair_grad_ref, sums_ref = refs[:4]
+    outs = list(refs[:-1])
+    if sums and not first:
+        before_ref = outs.pop(0)
+    if not first:
+        outs.pop(0)
+    if not sums:
+        outs.pop(0)
+    pair_grad_ref = outs.pop(0)
+    sums_ref = outs.pop(0) if sums else None
     lines_ref = refs[-1]
     width = w_half_ref.shape[0]
     layers, heads, channels = w_bias_ref.shape
     lanes = layers * heads
     piece = split_width(width)
     step = pair_ref.shape[0]
-    first_row = pl.program_id(0) * step
+    first_row = base + pl.program_id(0) * step
 
     @pl.when(pl.program_id(0) == 0)
     def _():
-        if first:
+        if sums and first:
             sums_ref[...] = jnp.zeros_like(sums_ref)
-        else:
+        elif sums:
             sums_ref[...] = before_ref[...]
         if direct:
             tiles, total, tile = lines_ref.shape
@@ -267,7 +272,8 @@
         yield True
         d_bias = read_lines(row)
         d_normed = mm(w_bias_ref[...].reshape(lanes, channels), d_bias, 0, 0)
-        sums_ref[3 * width :, :] += mm(d_bias, normed_out, 1, 1)
+        if sums:
+            sums_ref[3 * width :, :] += mm(d_bias, normed_out, 1, 1)
         d_lifted = norm_back(out_float, inv_out, d_normed)
         lifted_half = d_lifted.astype(BF16)
         yield True
@@ -277,23 +283,27 @@
             cols = slice(at, at + piece)
             up_cols = slice(width + at, width + at + piece)
             d_hidden = mm(w_half_ref[cols, :], lifted_half)
-            sums_ref[2 * width + at : 2 * width + at + piece, :] += mm(hidden, lifted_half, 1, 1)
+            if sums:
+                out_cols = slice(2 * width + at, 2 * width + at + piece)
+                sums_ref[out_cols, :] += mm(hidden, lifted_half, 1, 1)
             yield True
             d_gate = (d_hidden * slope).astype(BF16)
             d_up = (d_hidden * silu).astype(BF16)
-            part = mm(w_back_ref[:, cols], d_gate)
-            sums_ref[cols, :] += mm(d_gate, normed_in, 1, 1)
-            part = part + mm(w_back_ref[:, up_cols], d_up)
-            sums_ref[up_cols, :] += mm(d_up, normed_in, 1, 1)
-            d_normed_in = part if d_normed_in is None else d_normed_in + part
+            if sums:
+                sums_ref[cols, :] += mm(d_gate, normed_in, 1, 1)
+                sums_ref[up_cols, :] += mm(d_up, normed_in, 1, 1)
+            if grads:
+                part = mm(w_back_ref[:, cols], d_gate) + mm(w_back_ref[:, up_cols], d_up)
+                d_normed_in = part if d_normed_in is None else d_normed_in + part
             yield True
-        pair_grad = d_lifted + norm_back(normed_float, inv_in, d_normed_in)
-        pair_grad_ref[row] = pair_grad.astype(BF16).T
-
-    for_groups(step, 4, lambda at, count: interleave(lambda i: stages(at + i), count, 3))
+        if grads:
+            pair_grad = d_lifted + norm_back(normed_float, inv_in, d_normed_in)
+            pair_grad_ref[row] = pair_grad.astype(BF16).T
+
+    for_groups(step, 4, lambda at, count: interleave(lambda i: stages(at + i), count, 5))
 
     if last:
-        packed_ref = refs[-2]
+        packed_ref = outs.pop(0)
 
         @pl.when(pl.program_id(0) == pl.num_programs(0) - 1)
         def _():
@@ -303,7 +313,20 @@
             packed_ref[done:, :] = jnp.zeros((packed_ref.shape[0] - done, packed_ref.shape[1]), BF16)
 
 
-def backward_rows(start, rows, packed_rows, pair, d_bias, w_bias, prepared, state):
+def backward_rows(
+    start,
+    rows,
+    base,
+    direct,
+    packed_rows,
+    pair,
+    d_bias,
+    w_bias,
+    prepared,
+    state,
+    grads=True,
+    after=None,
+):
     crop, channels = pair.shape[1:]
     layers, heads, _ = w_bias.shape
     lanes = layers * heads
@@ -311,35 +334,42 @@
     step = row_step(rows)
     first_step = start // step
     positions = rows * crop
-    first, last = start == 0, start + rows == pair.shape[0]
-    direct = is_direct(rows, crop)
+    sums = after is None
+    first = start == 0
+    last = sums and start + rows == pair.shape[0]
     pair_spec = pl.BlockSpec((step, crop, channels), lambda i: (first_step + i, 0, 0))
     line_spec = whole_spec(d_bias) if direct else pl.BlockSpec((step, lanes, crop), lambda i: (i, 0, 0))
+    held_spec = pl.BlockSpec(memory_space=pl.ANY)
     operands = [pair, d_bias, w_bias, *prepared]
     in_specs = [pair_spec, line_spec] + [whole_spec(array) for array in operands[2:]]
     aliases = {}
+    if sums and not first:
+        operands.append(state[1])
+        in_specs.append(whole_spec(state[1]))
     if not first:
-        pair_grad, sums = state
-        operands += [sums, pair_grad]
-        in_specs += [whole_spec(sums), pl.BlockSpec(memory_space=pl.ANY)]
-        aliases = {len(operands) - 1: 0}
-    shapes = [
-        jax.ShapeDtypeStruct(pair.shape, BF16),
-        jax.ShapeDtypeStruct((3 * width + lanes, channels), F32),
-    ]
-    out_specs = [pair_spec, whole_spec(shapes[1])]
+        aliases = {len(operands): 0}
+        operands.append(state[0])
+        in_specs.append(held_spec)
+    if not sums:
+        operands.append(after)
+        in_specs.append(held_spec)
+    shapes = [jax.ShapeDtypeStruct(pair.shape, BF16)]
+    out_specs = [pair_spec if grads else held_spec]
+    if sums:
+        shapes.append(jax.ShapeDtypeStruct((3 * width + lanes, channels), F32))
+        out_specs.append(whole_spec(shapes[-1]))
     if last:
         shapes.append(jax.ShapeDtypeStruct((packed_rows, channels), BF16))
-        out_specs.append(whole_spec(shapes[2]))
+        out_specs.append(whole_spec(shapes[-1]))
     return pl.pallas_call(
-        functools.partial(backward_kernel, first, last, direct),
+        functools.partial(backward_kernel, first, last, sums, grads, direct, base),
         grid=(rows // step,),
         in_specs=in_specs,
         out_specs=out_specs,
         out_shape=shapes,
         input_output_aliases=aliases,
         scratch_shapes=[
-            pltpu.VMEM((crop // 128, lanes * rows, 128) if direct else (1, 8, 128), F32),
+            pltpu.VMEM((crop // 128, lanes * d_bias.shape[1], 128) if direct else (1, 8, 128), F32),
         ],
         compiler_params=pltpu.CompilerParams(vmem_limit_bytes=56 * 2**20),
         cost_estimate=pl.CostEstimate(
@@ -347,7 +377,7 @@
             bytes_accessed=positions * (2 * channels + lanes) * 2,
             transcendentals=positions * width,
         ),
-        name="pair_backward",
+        name="pair_backward" if sums else "pair_grad_rows",
     )(*operands)
 
 
@@ -436,25 +466,30 @@
     )
 
 
-def sum_over_devices(array):
+def sum_pairs(array):
     devices = lax.axis_size("tok")
     parity = lax.axis_index("tok") % 2
     across = [(index, index ^ 1) for index in range(devices)]
-    teams = [list(range(odd, devices, 2)) for odd in range(2)]
-    total, channels = array.shape
-    share = total // devices
-    halves = array.reshape(2, total // 2, channels)
+    halves = array.reshape(2, array.shape[0] // 2, array.shape[1])
     theirs = lax.ppermute(lax.dynamic_index_in_dim(halves, 1 - parity, 0, False), "tok", across)
     mine = lax.dynamic_index_in_dim(halves, parity, 0, False)
-    mine = (mine.astype(F32) + theirs.astype(F32)).astype(BF16)
-    parts = swap(mine.reshape(devices // 2, share, channels), teams)
-    summed = jnp.sum(parts.astype(F32), 0).astype(BF16)
-    copies = jnp.broadcast_to(summed[None], (devices // 2, share, channels))
-    mine = swap(copies, teams).reshape(total // 2, channels)
-    theirs = lax.ppermute(mine, "tok", across)
-    even = parity == 0
-    summed = jnp.concatenate([jnp.where(even, mine, theirs), jnp.where(even, theirs, mine)], 0)
-    return summed.astype(F32)
+    return (mine.astype(F32) + theirs.astype(F32)).astype(BF16)
+
+
+def sum_team(array):
+    devices = lax.axis_size("tok")
+    teams = [list(range(odd, devices, 2)) for odd in range(2)]
+    members = devices // 2
+    parts = swap(array.reshape(members, array.shape[0] // members, array.shape[1]), teams)
+    return jnp.sum(parts.astype(F32), 0).astype(BF16)
+
+
+def gather_shares(share):
+    devices = lax.axis_size("tok")
+    parts = swap(jnp.broadcast_to(share[None], (devices,) + share.shape))
+    parts = parts.reshape(devices // 2, 2, *share.shape)
+    parts = jnp.transpose(parts, (1, 0, 2, 3)).reshape(devices * share.shape[0], share.shape[1])
+    return parts.astype(F32)
 
 
 def body(
@@ -477,8 +512,8 @@
     samples, depth = query_states.shape[2:4]
     lanes = heads * layers
     sizes = [row_count]
-    if row_count % 32 == 0:
-        sizes = [row_count // 4, row_count - row_count // 4]
+    if row_count % 16 == 0:
+        sizes = [row_count // 2] * 2
     starts = [sum(sizes[:index]) for index in range(len(sizes))]
     w_bias = jnp.transpose(weight_bias, (0, 2, 1))
 
@@ -533,6 +568,8 @@
 
     sum_rows = 3 * width + lanes
     packed_rows = 8 * devices * -(-sum_rows // (8 * devices))
+    doubled = jnp.concatenate([jnp.ones((width,), BF16), jnp.full((width,), 2.0, BF16)])
+    prepared = (*prepared, weight_in * doubled[None, :], weight_out * jnp.asarray(0.5, BF16))
     pair_state = None
     for start, rows, d_bias in zip(starts, sizes, returned):
         if groups > 1:
@@ -542,19 +579,27 @@
             d_bias = d_bias.reshape(lanes, rows, crop)
         else:
             d_bias = jnp.transpose(d_bias, (2, 1, 0, 3)).reshape(rows, lanes, crop)
-        pair_state = backward_rows(
-            start,
-            rows,
-            packed_rows,
-            pair_states,
-            d_bias,
-            w_bias,
-            prepared,
-            pair_state and pair_state[:2],
+        later = start > 0 and is_direct(rows, crop)
+        make = functools.partial(
+            backward_rows,
+            direct=is_direct(rows, crop),
+            packed_rows=packed_rows,
+            pair=pair_states,
+            d_bias=d_bias,
+            w_bias=w_bias,
+            prepared=prepared,
         )
+        pair_state = make(start, rows, 0, state=pair_state, grads=not later)
     pair_grad, _, packed = pair_state
 
-    summed = sum_over_devices(packed)
+    half = rows // 2
+    packed = sum_pairs(packed)
+    if later:
+        (pair_grad,) = make(start, half, 0, state=(pair_grad,), after=packed)
+    share = sum_team(packed)
+    if later:
+        (pair_grad,) = make(start + half, half, half, state=(pair_grad,), after=share)
+    summed = gather_shares(share)
     grad_in = summed[: 2 * width].T
     grad_out = summed[2 * width : 3 * width]
     grad_bias = summed[3 * width : sum_rows].reshape(layers, heads, channels)

time: 171 us -> 200 us (1.17); the launches traced: 170 us -> 196 us
  Pallas kernels: 89.8 us -> 122 us
  blocking collectives: 24.7 us -> 0 us
  starting transfers between devices: 22.9 us -> 44.3 us
  waiting for transfers between devices: 18.7 us -> 8.33 us
  local copies, waits for them, and re-layouts: 10.8 us -> 16.2 us
    pallas_call x2 -> x4, Pallas kernels: 56.3 us -> 83 us  [backward_rows(): pl.pallas_call(functools.partial(backward_kernel, first, last, sums, grad...]
    all_to_all x2 -> x0, blocking collectives: 24.7 us -> none  [swap(): lax.all_to_all(array, 'tok', split_axis=0, concat_axis=0, tiled=True, axi...]
    all_to_all x4 -> x6, starting transfers between devices: 22.6 us -> 43.9 us  [swap(): lax.all_to_all(array, 'tok', split_axis=0, concat_axis=0, tiled=True, axi...]
    all_to_all x4 -> x6, waiting for transfers between devices: 17.4 us -> 8.32 us  [swap(): lax.all_to_all(array, 'tok', split_axis=0, concat_axis=0, tiled=True, axi...]
    pallas_call x2, Pallas kernels: 25.2 us -> 30.2 us  [forward_rows(): pl.pallas_call(functools.partial(forward_kernel, direct, first), grid=(ro...]
    slice x6, local copies, waits for them, and re-layouts: 5.19 us -> 8.61 us  [take_rows(): cut = cut[..., start:start + rows]]
    mul x0 -> x2, other arithmetic: none -> 2.33 us  [the longest x1 1.67 us: body(): weight_in * doubled[None, :]]
  transfers between devices with their start and end apart: 6 -> 7, of which waited for: 5 -> 2; matrix products, arithmetic and copies ran while one was open for 5% -> 7% of each run, Pallas kernels for 24% -> 41%
where the time goes in v6:
time: 200 us; the launch traced here: 196 us
  Pallas kernels  122 us (61%)
  starting transfers between devices  44.3 us (22%)
  local copies, waits for them, and re-layouts  16.2 us (8%)
  waiting for transfers between devices  8.33 us (4%)
  other arithmetic  4.23 us (2%)
    pallas_call x4, Pallas kernels, backward_rows(): pl.pallas_call(functools.partial(backward_kernel, first, last, sums, grad...  83 us
    all_to_all x6, starting transfers between devices, swap(): lax.all_to_all(array, 'tok', split_axis=0, concat_axis=0, tiled=True, axi...  43.9 us
    pallas_call x2, Pallas kernels, forward_rows(): pl.pallas_call(functools.partial(forward_kernel, direct, first), grid=(ro...  30.2 us
    slice x6, local copies, waits for them, and re-layouts, take_rows(): cut = cut[..., start:start + rows]  8.61 us
    pallas_call x2, Pallas kernels, attend_rows(): pl.pallas_call(functools.partial(attend_kernel, first, last), grid=(layer...  8.54 us
    all_to_all x6, waiting for transfers between devices, swap(): lax.all_to_all(array, 'tok', split_axis=0, concat_axis=0, tiled=True, axi...  8.32 us
  transfers between devices with their start and end apart: 7, of which 2 were waited for; matrix products, arithmetic and copies ran while one was open for 7% of the time, Pallas kernels for 41%

profile of v6, /device:TPU:0, one launch (start us, length us, event | category | flops | bytes accessed | tf_op | source)
XLA Modules:
  0.0 196.2 jit_solution(14222557485864784422)
XLA Ops:
  0.6 15.3 %pair_forward.2 = (bf16[32,16,512]{2,1,0:T(8,128)(2,1)}, bf16[1024,128]{1,0:T(8,128)(2,1)}, bf16[128,512]{1,0:T(8,128)(2,1)}) custom-call(bf16[32,512,128]{2,1,0:T(8,128)(2,1)} %pair_ref.11, bf16[2,16,128]{2,1,0:T(8,128)(2,1)} %bitcast.68, bf16[128,1024]{1,0:T(8,128)(2,1)} %refs_0_.1, bf16[512,128]{1,0:T(8,128)(2,1)} %refs_1_.1), custom_call_target="tpu_custom_call" | custom-call | flops 9865003008 | bytes 2621440 | tf_op jit(solution)/shard_map/pair_forward/pallas_call | solution.py:176
  15.9 7.4 %all-to-all-start.1 = ((bf16[16,2,16,512]{3,2,1,0:T(8,128)(2,1)}), bf16[16,2,16,512]{3,2,1,0:T(8,128)(2,1)S(1)}, u32[]{:S(2)}, u32[]{:S(2)}) async-start(bf16[16,2,16,512]{3,2,1,0:T(8,128)(2,1)} %bitcast.64), calls=%async_computation.1 | async-start | bytes 1048576 | tf_op jit(solution)/shard_map/all_to_all | solution.py:464
  23.8 15.0 %pair_forward.3 = bf16[32,16,512]{2,1,0:T(8,128)(2,1)} custom-call(bf16[32,512,128]{2,1,0:T(8,128)(2,1)} %pair_ref.11, bf16[2,16,128]{2,1,0:T(8,128)(2,1)} %bitcast.69, bf16[1024,128]{1,0:T(8,128)(2,1)} %get-tuple-element.22.refs_0_.w_in_t_ref, bf16[128,512]{1,0:T(8,128)(2,1)} %get-tuple-element.23.refs_1_.w_out_t_ref), custom_call_target="tpu_custom_call" | custom-call | flops 9865003008 | bytes 2621440 | tf_op jit(solution)/shard_map/pair_forward/pallas_call | solution.py:176
  38.7 6.1 %all-to-all-start = ((bf16[16,2,16,512]{3,2,1,0:T(8,128)(2,1)}), bf16[16,2,16,512]{3,2,1,0:T(8,128)(2,1)S(1)}, u32[]{:S(2)}, u32[]{:S(2)}) async-start(bf16[16,2,16,512]{3,2,1,0:T(8,128)(2,1)} %bitcast.63), calls=%async_computation | async-start | bytes 1048576 | tf_op jit(solution)/shard_map/all_to_all | solution.py:464
  44.9 1.2 fusion.2
  46.1 1.8 copy.40
  48.5 1.5 fusion.1
  50.0 1.7 copy.41
  51.9 4.3 %attention_backward.2 = (bf16[2,2,48,256]{3,2,1,0:T(8,128)(2,1)S(1)}, f32[2,2,48,512]{3,2,1,0:T(8,128)S(1)}, f32[2,2,48,512]{3,2,1,0:T(8,128)S(1)}, bf16[16,2,16,512]{3,2,1,0:T(8,128)(2,1)}) custom-call(f32[2]{0:T(128)S(1)} %multiply_divide_fusion.weight_ref, bf16[16,2,16,512]{3,2,1,0:T(8,128)(2,1)S(1)} %all-to-all-done.1.bias_ref, s32[1,512]{1,0:T(1,128)S(1)} %bitcast.46, ...), custom_call_target="tpu_custom_call" | custom-call | flops 5033164800 | bytes 2228224 | tf_op jit(solution)/shard_map/attention_backward/pallas_call | solution.py:442
  56.2 3.1 %all-to-all-done.bias_ref = bf16[16,2,16,512]{3,2,1,0:T(8,128)(2,1)S(1)} async-done(((bf16[16,2,16,512]{3,2,1,0:T(8,128)(2,1)}), bf16[16,2,16,512]{3,2,1,0:T(8,128)(2,1)S(1)}, u32[]{:S(2)}, u32[]{:S(2)}) %all-to-all-start) | async-done | bytes 524320 | tf_op jit(solution)/shard_map/all_to_all | solution.py:464
  59.3 14.2 %all-to-all-start.3 = ((bf16[16,2,16,512]{3,2,1,0:T(8,128)(2,1)}), bf16[16,2,16,512]{3,2,1,0:T(8,128)(2,1)S(1)}, u32[]{:S(2)}, u32[]{:S(2)}) async-start(bf16[16,2,16,512]{3,2,1,0:T(8,128)(2,1)} %get-tuple-element.28), calls=%async_computation.3 | async-start | bytes 1048576 | tf_op jit(solution)/shard_map/all_to_all | solution.py:464
  73.6 0.7 copy.38
  74.4 1.7 copy.39
  76.2 0.7 broadcast_multiply_fusion.1.w_half_ref
  76.9 1.7 broadcast_multiply_fusion.w_back_ref
  78.6 4.3 %attention_backward.3 = (bf16[2,2,48,256]{3,2,1,0:T(8,128)(2,1)S(1)}, bf16[2,2,48,512]{3,2,1,0:T(8,128)(2,1)}, bf16[2,2,48,512]{3,2,1,0:T(8,128)(2,1)}, bf16[16,2,16,512]{3,2,1,0:T(8,128)(2,1)}) custom-call(f32[2]{0:T(128)S(1)} %multiply_divide_fusion.weight_ref, bf16[16,2,16,512]{3,2,1,0:T(8,128)(2,1)S(1)} %all-to-all-done.bias_ref, s32[1,512]{1,0:T(1,128)S(1)} %bitcast.47, ...), custom_call_target="tpu_custom_call" | custom-call | flops 5033164800 | bytes 2228224 | tf_op jit(solution)/shard_map/attention_backward/pallas_call | solution.py:442
  82.8 5.2 %all-to-all-done.3 = bf16[16,2,16,512]{3,2,1,0:T(8,128)(2,1)S(1)} async-done(((bf16[16,2,16,512]{3,2,1,0:T(8,128)(2,1)}), bf16[16,2,16,512]{3,2,1,0:T(8,128)(2,1)S(1)}, u32[]{:S(2)}, u32[]{:S(2)}) %all-to-all-start.3) | async-done | bytes 524320 | tf_op jit(solution)/shard_map/all_to_all | solution.py:464
  88.0 4.1 %all-to-all-start.2 = ((bf16[16,2,16,512]{3,2,1,0:T(8,128)(2,1)}), bf16[16,2,16,512]{3,2,1,0:T(8,128)(2,1)S(1)}, u32[]{:S(2)}, u32[]{:S(2)}) async-start(bf16[16,2,16,512]{3,2,1,0:T(8,128)(2,1)} %get-tuple-element.27), calls=%async_computation.2 | async-start | bytes 1048576 | tf_op jit(solution)/shard_map/all_to_all | solution.py:464
  92.1 28.7 %pair_backward.2 = (bf16[32,512,128]{2,1,0:T(8,128)(2,1)}, f32[1568,128]{1,0:T(8,128)}) custom-call(bf16[32,512,128]{2,1,0:T(8,128)(2,1)} %pair_ref.11, bf16[32,16,512]{2,1,0:T(8,128)(2,1)} %bitcast.62, bf16[2,16,128]{2,1,0:T(8,128)(2,1)} %bitcast.70, bf16[1024,128]{1,0:T(8,128)(2,1)} %get-tuple-element.22.refs_0_.w_in_t_ref, ...), custom_call_target="tpu_custom_call" | custom-call | flops 29393682432 | bytes 4718592 | tf_op jit(solution)/shard_map/pair_backward/pallas_call | solution.py:364
  120.8 0.8 copy-done.3
  121.6 25.8 %pair_backward.3 = (bf16[32,512,128]{2,1,0:T(8,128)(2,1)}, f32[1568,128]{1,0:T(8,128)}, bf16[1664,128]{1,0:T(8,128)(2,1)}) custom-call(bf16[32,512,128]{2,1,0:T(8,128)(2,1)} %pair_ref.11, bf16[32,16,512]{2,1,0:T(8,128)(2,1)} %bitcast.59, bf16[2,16,128]{2,1,0:T(8,128)(2,1)} %bitcast.71, ...), custom_call_target="tpu_custom_call", output_to_operand_aliasing={{0}: (8, {})} | custom-call | flops 29393682432 | bytes 4718592 | tf_op jit(solution)/shard_map/pair_backward/pallas_call | solution.py:364
  147.5 0.9 dynamic-slice_bitcast_fusion
  149.3 0.9 copy.50
  150.2 1.7 fusion.refs_1_
  151.9 5.7 %all-to-all-start.4 = ((bf16[8,104,128]{2,1,0:T(8,128)(2,1)}), bf16[8,104,128]{2,1,0:T(8,128)(2,1)S(1)}, u32[]{:S(2)}, u32[]{:S(2)}) async-start(bf16[8,104,128]{2,1,0:T(8,128)(2,1)} %bitcast.15), calls=%async_computation.4 | async-start | bytes 425984 | tf_op jit(solution)/shard_map/all_to_all | solution.py:464
  157.6 14.3 %pair_grad_rows.2.refs_0_ = bf16[32,512,128]{2,1,0:T(8,128)(2,1)} custom-call(bf16[32,512,128]{2,1,0:T(8,128)(2,1)} %pair_ref.11, bf16[32,16,512]{2,1,0:T(8,128)(2,1)} %bitcast.60, bf16[2,16,128]{2,1,0:T(8,128)(2,1)} %bitcast.72, bf16[1024,128]{1,0:T(8,128)(2,1)} %get-tuple-element.22.refs_0_.w_in_t_ref, ...), custom_call_target="tpu_custom_call", output_to_operand_aliasing={{}: (7, {})} | custom-call | flops 14696841216 | bytes 2359296 | tf_op jit(solution)/shard_map/pair_grad_rows/pallas_call | solution.py:364
  171.9 0.8 broadcast_in_dim.18
  172.7 6.3 %all-to-all-start.5 = ((bf16[16,104,128]{2,1,0:T(8,128)(2,1)}), bf16[16,104,128]{2,1,0:T(8,128)(2,1)S(1)}, u32[]{:S(2)}, u32[]{:S(2)}) async-start(bf16[16,104,128]{2,1,0:T(8,128)(2,1)} %broadcast_in_dim.18), calls=%async_computation.5 | async-start | bytes 851968 | tf_op jit(solution)/shard_map/all_to_all | solution.py:464
  179.1 14.2 %pair_grad_rows.3 = bf16[32,512,128]{2,1,0:T(8,128)(2,1)} custom-call(bf16[32,512,128]{2,1,0:T(8,128)(2,1)} %pair_ref.11, bf16[32,16,512]{2,1,0:T(8,128)(2,1)} %bitcast.61, bf16[2,16,128]{2,1,0:T(8,128)(2,1)} %bitcast.73, bf16[1024,128]{1,0:T(8,128)(2,1)} %get-tuple-element.22.refs_0_.w_in_t_ref, ...), custom_call_target="tpu_custom_call", output_to_operand_aliasing={{}: (7, {})} | custom-call | flops 14696841216 | bytes 2359296 | tf_op jit(solution)/shard_map/pair_grad_rows/pallas_call | solution.py:364
  193.5 0.7 slice.33
  194.2 0.6 slice.34
  194.8 1.0 copy.53
  (41 shorter events, 2.6 us)
Async XLA Ops:
  0.6 22.7 %copy-start.5 = (bf16[2,1,2,48,512]{4,3,2,1,0:T(8,128)(2,1)S(1)}, bf16[2,1,2,48,512]{4,3,2,1,0:T(8,128)(2,1)}, u32[]{:S(2)}) copy-start(bf16[2,1,2,48,512]{4,3,2,1,0:T(8,128)(2,1)} %param.16) | copy-start | bytes 589828
  15.9 22.8 %all-to-all-start.1 = ((bf16[16,2,16,512]{3,2,1,0:T(8,128)(2,1)}), bf16[16,2,16,512]{3,2,1,0:T(8,128)(2,1)S(1)}, u32[]{:S(2)}, u32[]{:S(2)}) async-start(bf16[16,2,16,512]{3,2,1,0:T(8,128)(2,1)} %bitcast.64), calls=%async_computation.1 | async-start | bytes 1048576 | tf_op jit(solution)/shard_map/all_to_all | solution.py:464
  38.7 9.3 %copy-start.6 = (bf16[2,1,2,48,512]{4,3,2,1,0:T(8,128)(2,1)S(1)}, bf16[2,1,2,48,512]{4,3,2,1,0:T(8,128)(2,1)}, u32[]{:S(2)}) copy-start(bf16[2,1,2,48,512]{4,3,2,1,0:T(8,128)(2,1)} %param.19) | copy-start | bytes 589828
  38.7 20.6 %all-to-all-start = ((bf16[16,2,16,512]{3,2,1,0:T(8,128)(2,1)}), bf16[16,2,16,512]{3,2,1,0:T(8,128)(2,1)S(1)}, u32[]{:S(2)}, u32[]{:S(2)}) async-start(bf16[16,2,16,512]{3,2,1,0:T(8,128)(2,1)} %bitcast.63), calls=%async_computation | async-start | bytes 1048576 | tf_op jit(solution)/shard_map/all_to_all | solution.py:464
  46.1 5.7 %copy-start.10 = (s32[2]{0:T(128)S(1)}, s32[2]{0:T(128)}, u32[]{:S(2)}) copy-start(s32[2]{0:T(128)} %param.15) | copy-start | bytes 28
  46.1 5.8 %copy-start = (bf16[2,1,2,48,512]{4,3,2,1,0:T(8,128)(2,1)S(1)}, bf16[2,1,2,48,512]{4,3,2,1,0:T(8,128)(2,1)}, u32[]{:S(2)}) copy-start(bf16[2,1,2,48,512]{4,3,2,1,0:T(8,128)(2,1)} %param.17) | copy-start | bytes 589828
  46.1 5.8 %copy-start.1 = (bf16[2,1,2,48,512]{4,3,2,1,0:T(8,128)(2,1)S(1)}, bf16[2,1,2,48,512]{4,3,2,1,0:T(8,128)(2,1)}, u32[]{:S(2)}) copy-start(bf16[2,1,2,48,512]{4,3,2,1,0:T(8,128)(2,1)} %param.18) | copy-start | bytes 589828
  46.1 5.8 %copy-start.2 = (s32[512]{0:T(512)S(1)}, s32[512]{0:T(512)}, u32[]{:S(2)}) copy-start(s32[512]{0:T(512)} %param.14) | copy-start | bytes 6148
  51.9 24.3 %copy-start.7 = (bf16[512,128]{1,0:T(8,128)(2,1)S(1)}, bf16[512,128]{1,0:T(8,128)(2,1)}, u32[]{:S(2)}) copy-start(bf16[512,128]{1,0:T(8,128)(2,1)} %refs_1_.1) | copy-start | bytes 393220
  51.9 25.0 %copy-start.9 = (bf16[1024]{0:T(1024)(128)(2,1)S(1)}, bf16[1024]{0:T(1024)(128)(2,1)}, u32[]{:S(2)}) copy-start(bf16[1024]{0:T(1024)(128)(2,1)} %constant.49.clone.1) | copy-start | bytes 6148
  59.3 28.7 %all-to-all-start.3 = ((bf16[16,2,16,512]{3,2,1,0:T(8,128)(2,1)}), bf16[16,2,16,512]{3,2,1,0:T(8,128)(2,1)S(1)}, u32[]{:S(2)}, u32[]{:S(2)}) async-start(bf16[16,2,16,512]{3,2,1,0:T(8,128)(2,1)} %get-tuple-element.28), calls=%async_computation.3 | async-start | bytes 1048576 | tf_op jit(solution)/shard_map/all_to_all | solution.py:464
  88.0 4.1 %copy-start.4 = (bf16[16,2,16,512]{3,2,1,0:T(8,128)(2,1)}, bf16[16,2,16,512]{3,2,1,0:T(8,128)(2,1)S(1)}, u32[]{:S(2)}) copy-start(bf16[16,2,16,512]{3,2,1,0:T(8,128)(2,1)S(1)} %all-to-all-done.3) | copy-start | bytes 1572868
  88.0 32.8 %all-to-all-start.2 = ((bf16[16,2,16,512]{3,2,1,0:T(8,128)(2,1)}), bf16[16,2,16,512]{3,2,1,0:T(8,128)(2,1)S(1)}, u32[]{:S(2)}, u32[]{:S(2)}) async-start(bf16[16,2,16,512]{3,2,1,0:T(8,128)(2,1)} %get-tuple-element.27), calls=%async_computation.2 | async-start | bytes 1048576 | tf_op jit(solution)/shard_map/all_to_all | solution.py:464
  120.8 0.8 copy-start.3
  148.4 1.8 collective-permute-start
  151.9 19.9 %all-to-all-start.4 = ((bf16[8,104,128]{2,1,0:T(8,128)(2,1)}), bf16[8,104,128]{2,1,0:T(8,128)(2,1)S(1)}, u32[]{:S(2)}, u32[]{:S(2)}) async-start(bf16[8,104,128]{2,1,0:T(8,128)(2,1)} %bitcast.15), calls=%async_computation.4 | async-start | bytes 425984 | tf_op jit(solution)/shard_map/all_to_all | solution.py:464
  171.9 7.2 %copy-start.8 = (bf16[104,128]{1,0:T(8,128)(2,1)}, bf16[104,128]{1,0:T(8,128)(2,1)S(1)}, u32[]{:S(2)}) copy-start(bf16[104,128]{1,0:T(8,128)(2,1)S(1)} %reduce_sum.12.refs_1_) | copy-start | bytes 79876
  172.7 20.6 %all-to-all-start.5 = ((bf16[16,104,128]{2,1,0:T(8,128)(2,1)}), bf16[16,104,128]{2,1,0:T(8,128)(2,1)S(1)}, u32[]{:S(2)}, u32[]{:S(2)}) async-start(bf16[16,104,128]{2,1,0:T(8,128)(2,1)} %broadcast_in_dim.18), calls=%async_computation.5 | async-start | bytes 851968 | tf_op jit(solution)/shard_map/all_to_all | solution.py:464

commit v7 on v6

--- a/solution.py
+++ b/solution.py
@@ -59,7 +59,7 @@
     running = []
     clock = 0
     while rows or running:
-        if rows and clock % lag == 0:
+        while rows and clock >= lag * (count - len(rows)):
             running.append(rows.pop(0))
         running = [row for row in running if next(row, None) is not None]
         clock += 1
@@ -133,7 +133,7 @@
         else:
             bias_ref[row] = bias.astype(BF16)
 
-    for_groups(step, 4, lambda at, count: interleave(lambda i: stages(at + i), count, 3))
+    for_groups(step, 4, lambda at, count: interleave(lambda i: stages(at + i), count, 0))
 
     if direct:
 
@@ -300,7 +300,7 @@
             pair_grad = d_lifted + norm_back(normed_float, inv_in, d_normed_in)
             pair_grad_ref[row] = pair_grad.astype(BF16).T
 
-    for_groups(step, 4, lambda at, count: interleave(lambda i: stages(at + i), count, 5))
+    for_groups(step, 4, lambda at, count: interleave(lambda i: stages(at + i), count, 2))
 
     if last:
         packed_ref = outs.pop(0)
@@ -486,10 +486,15 @@
 
 def gather_shares(share):
     devices = lax.axis_size("tok")
-    parts = swap(jnp.broadcast_to(share[None], (devices,) + share.shape))
-    parts = parts.reshape(devices // 2, 2, *share.shape)
-    parts = jnp.transpose(parts, (1, 0, 2, 3)).reshape(devices * share.shape[0], share.shape[1])
-    return parts.astype(F32)
+    members = devices // 2
+    across = [(index, index ^ 1) for index in range(devices)]
+    teams = [list(range(odd, devices, 2)) for odd in range(2)]
+    mine = swap(jnp.broadcast_to(share[None], (members,) + share.shape), teams)
+    mine = mine.reshape(members * share.shape[0], share.shape[1])
+    theirs = lax.ppermute(mine, "tok", across)
+    even = lax.axis_index("tok") % 2 == 0
+    both = jnp.concatenate([jnp.where(even, mine, theirs), jnp.where(even, theirs, mine)], 0)
+    return both.astype(F32)
 
 
 def body(
@@ -521,10 +526,12 @@
     weights = sample_weight(lax.dynamic_slice_in_dim(noise_level, group * samples, samples))
     valid = key_mask[None, :]
 
-    def take_rows(array, start, rows):
-        cut = array[:, 0].reshape(layers, samples, depth, devices, row_count)
-        cut = cut[..., start : start + rows]
-        return cut.reshape(layers, samples, depth, devices * rows)
+    def by_chunk(array):
+        cut = array[:, 0].reshape(layers, samples, depth, devices, len(sizes), sizes[0])
+        cut = jnp.transpose(cut, (4, 0, 1, 2, 3, 5))
+        return cut.reshape(len(sizes), layers, samples, depth, devices * sizes[0])
+
+    queries, grads = by_chunk(query_states), by_chunk(output_grad)
 
     arrived = []
     prepared = None
@@ -554,10 +561,10 @@
             weights,
             bias,
             valid,
-            take_rows(query_states, start, rows),
+            queries[start // rows],
             key_states[:, 0],
             value_states[:, 0],
-            take_rows(output_grad, start, rows),
+            grads[start // rows],
             state,
         )
         state = (d_key, d_value)
@@ -579,7 +586,6 @@
             d_bias = d_bias.reshape(lanes, rows, crop)
         else:
             d_bias = jnp.transpose(d_bias, (2, 1, 0, 3)).reshape(rows, lanes, crop)
-        later = start > 0 and is_direct(rows, crop)
         make = functools.partial(
             backward_rows,
             direct=is_direct(rows, crop),
@@ -589,17 +595,10 @@
             w_bias=w_bias,
             prepared=prepared,
         )
-        pair_state = make(start, rows, 0, state=pair_state, grads=not later)
+        pair_state = make(start, rows, 0, state=pair_state)
     pair_grad, _, packed = pair_state
 
-    half = rows // 2
-    packed = sum_pairs(packed)
-    if later:
-        (pair_grad,) = make(start, half, 0, state=(pair_grad,), after=packed)
-    share = sum_team(packed)
-    if later:
-        (pair_grad,) = make(start + half, half, half, state=(pair_grad,), after=share)
-    summed = gather_shares(share)
+    summed = gather_shares(sum_team(sum_pairs(packed)))
     grad_in = summed[: 2 * width].T
     grad_out = summed[2 * width : 3 * width]
     grad_bias = summed[3 * width : sum_rows].reshape(layers, heads, channels)

time: 200 us -> 166 us (0.83); the launches traced: 196 us -> 165 us
  Pallas kernels: 122 us -> 87.8 us
  blocking collectives: 0 us -> 25.1 us
  starting transfers between devices: 44.3 us -> 20.2 us
  waiting for transfers between devices: 8.33 us -> 22 us
  local copies, waits for them, and re-layouts: 16.2 us -> 5.21 us
    pallas_call x4 -> x2, Pallas kernels: 83 us -> 56.4 us  [backward_rows(): pl.pallas_call(functools.partial(backward_kernel, first, last, sums, grad...]
    all_to_all x0 -> x2, blocking collectives: none -> 25.1 us  [swap(): lax.all_to_all(array, 'tok', split_axis=0, concat_axis=0, tiled=True, axi...]
    all_to_all x6 -> x4, starting transfers between devices: 43.9 us -> 19.8 us  [swap(): lax.all_to_all(array, 'tok', split_axis=0, concat_axis=0, tiled=True, axi...]
    all_to_all x6 -> x4, waiting for transfers between devices: 8.32 us -> 20.8 us  [swap(): lax.all_to_all(array, 'tok', split_axis=0, concat_axis=0, tiled=True, axi...]
    slice x8 -> x2, local copies, waits for them, and re-layouts: 9.93 us -> 0.07 us  [the longest x1 0.04 us: body(): grads[start // rows]]
    pallas_call x2, Pallas kernels: 30.2 us -> 22.8 us  [forward_rows(): pl.pallas_call(functools.partial(forward_kernel, direct, first), grid=(ro...]
  transfers between devices with their start and end apart: 7 -> 6, of which waited for: 2 -> 5; matrix products, arithmetic and copies ran while one was open for 7% -> 2% of each run, Pallas kernels for 41% -> 29%
where the time goes in v7:
time: 166 us; the launch traced here: 165 us
  Pallas kernels  87.8 us (53%)
  blocking collectives  25.1 us (15%)
  waiting for transfers between devices  22 us (13%)
  starting transfers between devices  20.2 us (12%)
  local copies, waits for them, and re-layouts  5.21 us (3%)
  other arithmetic  3.96 us (2%)
    pallas_call x2, Pallas kernels, backward_rows(): pl.pallas_call(functools.partial(backward_kernel, first, last, sums, grad...  56.4 us
    all_to_all x2, blocking collectives, swap(): lax.all_to_all(array, 'tok', split_axis=0, concat_axis=0, tiled=True, axi...  25.1 us
    pallas_call x2, Pallas kernels, forward_rows(): pl.pallas_call(functools.partial(forward_kernel, direct, first), grid=(ro...  22.8 us
    all_to_all x4, waiting for transfers between devices, swap(): lax.all_to_all(array, 'tok', split_axis=0, concat_axis=0, tiled=True, axi...  20.8 us
    all_to_all x4, starting transfers between devices, swap(): lax.all_to_all(array, 'tok', split_axis=0, concat_axis=0, tiled=True, axi...  19.8 us
    pallas_call x2, Pallas kernels, attend_rows(): pl.pallas_call(functools.partial(attend_kernel, first, last), grid=(layer...  8.53 us
  transfers between devices with their start and end apart: 6, of which 5 were waited for; matrix products, arithmetic and copies ran while one was open for 2% of the time, Pallas kernels for 29%

profile of v7, /device:TPU:0, one launch (start us, length us, event | category | flops | bytes accessed | tf_op | source)
XLA Modules:
  0.0 165.3 jit_solution(3942058986677072212)
XLA Ops:
  0.6 11.5 %pair_forward.2 = (bf16[32,16,512]{2,1,0:T(8,128)(2,1)}, bf16[1024,128]{1,0:T(8,128)(2,1)}, bf16[128,512]{1,0:T(8,128)(2,1)}) custom-call(bf16[32,512,128]{2,1,0:T(8,128)(2,1)} %pair_ref.7, bf16[2,16,128]{2,1,0:T(8,128)(2,1)} %bitcast.65, bf16[128,1024]{1,0:T(8,128)(2,1)} %refs_0_.1, bf16[512,128]{1,0:T(8,128)(2,1)} %refs_1_.1), custom_call_target="tpu_custom_call" | custom-call | flops 9865003008 | bytes 2621440 | tf_op jit(solution)/shard_map/pair_forward/pallas_call | solution.py:176
  12.2 7.4 %all-to-all-start.1 = ((bf16[16,2,16,512]{3,2,1,0:T(8,128)(2,1)}), bf16[16,2,16,512]{3,2,1,0:T(8,128)(2,1)S(1)}, u32[]{:S(2)}, u32[]{:S(2)}) async-start(bf16[16,2,16,512]{3,2,1,0:T(8,128)(2,1)} %bitcast.61), calls=%async_computation.1 | async-start | bytes 1048576 | tf_op jit(solution)/shard_map/all_to_all | solution.py:464
  19.6 0.3 copy.23
  19.9 11.3 %pair_forward.3 = bf16[32,16,512]{2,1,0:T(8,128)(2,1)} custom-call(bf16[32,512,128]{2,1,0:T(8,128)(2,1)} %pair_ref.7, bf16[2,16,128]{2,1,0:T(8,128)(2,1)} %bitcast.66, bf16[1024,128]{1,0:T(8,128)(2,1)} %get-tuple-element.22.refs_0_.w_in_t_ref, bf16[128,512]{1,0:T(8,128)(2,1)} %get-tuple-element.23.refs_1_.w_out_t_ref), custom_call_target="tpu_custom_call" | custom-call | flops 9865003008 | bytes 2621440 | tf_op jit(solution)/shard_map/pair_forward/pallas_call | solution.py:176
  31.2 2.9 %all-to-all-done.1.bias_ref = bf16[16,2,16,512]{3,2,1,0:T(8,128)(2,1)S(1)} async-done(((bf16[16,2,16,512]{3,2,1,0:T(8,128)(2,1)}), bf16[16,2,16,512]{3,2,1,0:T(8,128)(2,1)S(1)}, u32[]{:S(2)}, u32[]{:S(2)}) %all-to-all-start.1) | async-done | bytes 524320 | tf_op jit(solution)/shard_map/all_to_all | solution.py:464
  34.0 4.1 %all-to-all-start = ((bf16[16,2,16,512]{3,2,1,0:T(8,128)(2,1)}), bf16[16,2,16,512]{3,2,1,0:T(8,128)(2,1)S(1)}, u32[]{:S(2)}, u32[]{:S(2)}) async-start(bf16[16,2,16,512]{3,2,1,0:T(8,128)(2,1)} %bitcast.59), calls=%async_computation | async-start | bytes 1048576 | tf_op jit(solution)/shard_map/all_to_all | solution.py:464
  38.2 0.1 copy.25.q_ref
  38.3 0.3 copy.24
  38.9 4.3 %attention_backward.2 = (bf16[2,2,48,256]{3,2,1,0:T(8,128)(2,1)S(1)}, f32[2,2,48,512]{3,2,1,0:T(8,128)S(1)}, f32[2,2,48,512]{3,2,1,0:T(8,128)S(1)}, bf16[16,2,16,512]{3,2,1,0:T(8,128)(2,1)}) custom-call(f32[2]{0:T(128)S(1)} %multiply_divide_fusion.weight_ref, bf16[16,2,16,512]{3,2,1,0:T(8,128)(2,1)S(1)} %all-to-all-done.1.bias_ref, s32[1,512]{1,0:T(1,128)S(1)} %bitcast.46, ...), custom_call_target="tpu_custom_call" | custom-call | flops 5033164800 | bytes 2228224 | tf_op jit(solution)/shard_map/attention_backward/pallas_call | solution.py:442
  43.2 9.4 %all-to-all-done.bias_ref = bf16[16,2,16,512]{3,2,1,0:T(8,128)(2,1)S(1)} async-done(((bf16[16,2,16,512]{3,2,1,0:T(8,128)(2,1)}), bf16[16,2,16,512]{3,2,1,0:T(8,128)(2,1)S(1)}, u32[]{:S(2)}, u32[]{:S(2)}) %all-to-all-start) | async-done | bytes 524320 | tf_op jit(solution)/shard_map/all_to_all | solution.py:464
  52.6 4.3 %all-to-all-start.3 = ((bf16[16,2,16,512]{3,2,1,0:T(8,128)(2,1)}), bf16[16,2,16,512]{3,2,1,0:T(8,128)(2,1)}, u32[]{:S(2)}, u32[]{:S(2)}) async-start(bf16[16,2,16,512]{3,2,1,0:T(8,128)(2,1)} %get-tuple-element.28), calls=%async_computation.3 | async-start | bytes 1048576 | tf_op jit(solution)/shard_map/all_to_all | solution.py:464
  57.0 0.1 copy.28.g_ref
  57.2 0.7 broadcast_multiply_fusion.1.w_half_ref
  57.8 0.7 broadcast_multiply_fusion.w_back_ref
  58.6 4.2 %attention_backward.3 = (bf16[2,2,48,256]{3,2,1,0:T(8,128)(2,1)S(1)}, bf16[2,2,48,512]{3,2,1,0:T(8,128)(2,1)}, bf16[2,2,48,512]{3,2,1,0:T(8,128)(2,1)}, bf16[16,2,16,512]{3,2,1,0:T(8,128)(2,1)}) custom-call(f32[2]{0:T(128)S(1)} %multiply_divide_fusion.weight_ref, bf16[16,2,16,512]{3,2,1,0:T(8,128)(2,1)S(1)} %all-to-all-done.bias_ref, s32[1,512]{1,0:T(1,128)S(1)} %bitcast.47, ...), custom_call_target="tpu_custom_call" | custom-call | flops 5033164800 | bytes 2228224 | tf_op jit(solution)/shard_map/attention_backward/pallas_call | solution.py:442
  62.8 8.5 %all-to-all-done.3 = bf16[16,2,16,512]{3,2,1,0:T(8,128)(2,1)} async-done(((bf16[16,2,16,512]{3,2,1,0:T(8,128)(2,1)}), bf16[16,2,16,512]{3,2,1,0:T(8,128)(2,1)}, u32[]{:S(2)}, u32[]{:S(2)}) %all-to-all-start.3) | async-done | bytes 524320 | tf_op jit(solution)/shard_map/all_to_all | solution.py:464
  71.3 4.0 %all-to-all-start.2 = ((bf16[16,2,16,512]{3,2,1,0:T(8,128)(2,1)}), bf16[16,2,16,512]{3,2,1,0:T(8,128)(2,1)S(1)}, u32[]{:S(2)}, u32[]{:S(2)}) async-start(bf16[16,2,16,512]{3,2,1,0:T(8,128)(2,1)} %get-tuple-element.27), calls=%async_computation.2 | async-start | bytes 1048576 | tf_op jit(solution)/shard_map/all_to_all | solution.py:464
  75.4 28.0 %pair_backward.2 = (bf16[32,512,128]{2,1,0:T(8,128)(2,1)}, f32[1568,128]{1,0:T(8,128)}) custom-call(bf16[32,512,128]{2,1,0:T(8,128)(2,1)} %pair_ref.7, bf16[32,16,512]{2,1,0:T(8,128)(2,1)} %bitcast.17.d_bias_ref, bf16[2,16,128]{2,1,0:T(8,128)(2,1)} %bitcast.67, bf16[1024,128]{1,0:T(8,128)(2,1)} %get-tuple-element.22.refs_0_.w_in_t_ref, ...), custom_call_target="tpu_custom_call" | custom-call | flops 29393682432 | bytes 4718592 | tf_op jit(solution)/shard_map/pair_backward/pallas_call | solution.py:364
  103.4 0.8 copy-done.3
  104.2 28.4 %pair_backward.3 = (bf16[32,512,128]{2,1,0:T(8,128)(2,1)}, f32[1568,128]{1,0:T(8,128)}, bf16[1664,128]{1,0:T(8,128)(2,1)}) custom-call(bf16[32,512,128]{2,1,0:T(8,128)(2,1)} %pair_ref.7, bf16[32,16,512]{2,1,0:T(8,128)(2,1)} %bitcast.60, bf16[2,16,128]{2,1,0:T(8,128)(2,1)} %bitcast.68, ...), custom_call_target="tpu_custom_call", output_to_operand_aliasing={{0}: (8, {})} | custom-call | flops 29393682432 | bytes 4718592 | tf_op jit(solution)/shard_map/pair_backward/pallas_call | solution.py:364
  132.6 0.9 dynamic-slice_bitcast_fusion
  133.6 0.5 collective-permute-start
  134.1 1.1 collective-permute-done
  135.2 1.0 fusion
  136.1 14.2 %all_to_all.30 = bf16[8,104,128]{2,1,0:T(8,128)(2,1)S(1)} all-to-all(bf16[8,104,128]{2,1,0:T(8,128)(2,1)S(1)} %bitcast.58), channel_id=1, replica_groups={{0,2,4,6,8,10,12,14},{1,3,5,7,9,11,13,15},{16,18,20,22,24,26,28,30},{17..., dimensions={0} | all-to-all | bytes 425984 | tf_op jit(solution)/shard_map/all_to_all | solution.py:464
  150.4 11.0 %all_to_all.31 = bf16[8,104,128]{2,1,0:T(8,128)(2,1)S(1)} all-to-all(bf16[8,104,128]{2,1,0:T(8,128)(2,1)S(1)} %broadcast_in_dim.18), channel_id=1, replica_groups={{0,2,4,6,8,10,12,14},{1,3,5,7,9,11,13,15},{16,18,20,22,24,26,28,30},{17..., dimensions={0} | all-to-all | bytes 425984 | tf_op jit(solution)/shard_map/all_to_all | solution.py:464
  161.4 0.2 copy.30
  161.5 0.2 copy.29
  161.8 0.9 copy.32
  162.9 0.6 maximum_convert_fusion.2
  163.5 0.7 maximum_convert_fusion.1
  164.3 1.0 copy.35
  (33 shorter events, 0.8 us)
Async XLA Ops:
  0.6 18.9 %copy-start.5 = (bf16[2,1,2,48,512]{4,3,2,1,0:T(8,128)(2,1)S(1)}, bf16[2,1,2,48,512]{4,3,2,1,0:T(8,128)(2,1)}, u32[]{:S(2)}) copy-start(bf16[2,1,2,48,512]{4,3,2,1,0:T(8,128)(2,1)} %param.16) | copy-start | bytes 589828
  12.2 21.9 %all-to-all-start.1 = ((bf16[16,2,16,512]{3,2,1,0:T(8,128)(2,1)}), bf16[16,2,16,512]{3,2,1,0:T(8,128)(2,1)S(1)}, u32[]{:S(2)}, u32[]{:S(2)}) async-start(bf16[16,2,16,512]{3,2,1,0:T(8,128)(2,1)} %bitcast.61), calls=%async_computation.1 | async-start | bytes 1048576 | tf_op jit(solution)/shard_map/all_to_all | solution.py:464
  19.9 18.4 %copy-start.6 = (bf16[2,1,2,48,512]{4,3,2,1,0:T(8,128)(2,1)S(1)}, bf16[2,1,2,48,512]{4,3,2,1,0:T(8,128)(2,1)}, u32[]{:S(2)}) copy-start(bf16[2,1,2,48,512]{4,3,2,1,0:T(8,128)(2,1)} %param.19) | copy-start | bytes 589828
  31.2 7.7 %copy-start.9 = (s32[2]{0:T(128)S(1)}, s32[2]{0:T(128)}, u32[]{:S(2)}) copy-start(s32[2]{0:T(128)} %param.15) | copy-start | bytes 28
  31.2 7.7 %copy-start = (bf16[2,1,2,48,512]{4,3,2,1,0:T(8,128)(2,1)S(1)}, bf16[2,1,2,48,512]{4,3,2,1,0:T(8,128)(2,1)}, u32[]{:S(2)}) copy-start(bf16[2,1,2,48,512]{4,3,2,1,0:T(8,128)(2,1)} %param.17) | copy-start | bytes 589828
  31.2 7.7 %copy-start.1 = (bf16[2,1,2,48,512]{4,3,2,1,0:T(8,128)(2,1)S(1)}, bf16[2,1,2,48,512]{4,3,2,1,0:T(8,128)(2,1)}, u32[]{:S(2)}) copy-start(bf16[2,1,2,48,512]{4,3,2,1,0:T(8,128)(2,1)} %param.18) | copy-start | bytes 589828
  31.2 7.7 %copy-start.2 = (s32[512]{0:T(512)S(1)}, s32[512]{0:T(512)}, u32[]{:S(2)}) copy-start(s32[512]{0:T(512)} %param.14) | copy-start | bytes 6148
  34.0 18.6 %all-to-all-start = ((bf16[16,2,16,512]{3,2,1,0:T(8,128)(2,1)}), bf16[16,2,16,512]{3,2,1,0:T(8,128)(2,1)S(1)}, u32[]{:S(2)}, u32[]{:S(2)}) async-start(bf16[16,2,16,512]{3,2,1,0:T(8,128)(2,1)} %bitcast.59), calls=%async_computation | async-start | bytes 1048576 | tf_op jit(solution)/shard_map/all_to_all | solution.py:464
  38.9 18.3 %copy-start.7 = (bf16[512,128]{1,0:T(8,128)(2,1)S(1)}, bf16[512,128]{1,0:T(8,128)(2,1)}, u32[]{:S(2)}) copy-start(bf16[512,128]{1,0:T(8,128)(2,1)} %refs_1_.1) | copy-start | bytes 393220
  38.9 19.0 %copy-start.4 = (bf16[128,1024]{1,0:T(8,128)(2,1)S(1)}, bf16[128,1024]{1,0:T(8,128)(2,1)}, u32[]{:S(2)}) copy-start(bf16[128,1024]{1,0:T(8,128)(2,1)} %refs_0_.1) | copy-start | bytes 786436
  38.9 19.0 %copy-start.8 = (bf16[1024]{0:T(1024)(128)(2,1)S(1)}, bf16[1024]{0:T(1024)(128)(2,1)}, u32[]{:S(2)}) copy-start(bf16[1024]{0:T(1024)(128)(2,1)} %constant.51.clone.1) | copy-start | bytes 6148
  52.6 18.7 %all-to-all-start.3 = ((bf16[16,2,16,512]{3,2,1,0:T(8,128)(2,1)}), bf16[16,2,16,512]{3,2,1,0:T(8,128)(2,1)}, u32[]{:S(2)}, u32[]{:S(2)}) async-start(bf16[16,2,16,512]{3,2,1,0:T(8,128)(2,1)} %get-tuple-element.28), calls=%async_computation.3 | async-start | bytes 1048576 | tf_op jit(solution)/shard_map/all_to_all | solution.py:464
  71.3 32.1 %all-to-all-start.2 = ((bf16[16,2,16,512]{3,2,1,0:T(8,128)(2,1)}), bf16[16,2,16,512]{3,2,1,0:T(8,128)(2,1)S(1)}, u32[]{:S(2)}, u32[]{:S(2)}) async-start(bf16[16,2,16,512]{3,2,1,0:T(8,128)(2,1)} %get-tuple-element.27), calls=%async_computation.2 | async-start | bytes 1048576 | tf_op jit(solution)/shard_map/all_to_all | solution.py:464
  103.4 0.8 copy-start.3
  133.6 1.6 collective-permute-start
  161.4 1.5 collective-permute-start.1

commit v8 on v7

--- a/solution.py
+++ b/solution.py
@@ -133,7 +133,7 @@
         else:
             bias_ref[row] = bias.astype(BF16)
 
-    for_groups(step, 4, lambda at, count: interleave(lambda i: stages(at + i), count, 0))
+    for_groups(step, 2, lambda at, count: interleave(lambda i: stages(at + i), count, 0))
 
     if direct:
 
@@ -224,6 +224,7 @@
     lanes = layers * heads
     piece = split_width(width)
     step = pair_ref.shape[0]
+    one, two = jnp.asarray(1.0, BF16), jnp.asarray(2.0, BF16)
     first_row = base + pl.program_id(0) * step
 
     @pl.when(pl.program_id(0) == 0)
@@ -260,10 +261,11 @@
             half_gate = mm(w_in_t_ref[at : at + piece, :], normed_in)
             up_in = mm(w_in_t_ref[width + at : width + at + piece, :], normed_in)
             yield True
-            one_plus = 1.0 + jnp.tanh(half_gate)
+            one_plus = (1.0 + jnp.tanh(half_gate)).astype(BF16)
+            half_gate, up_in = half_gate.astype(BF16), up_in.astype(BF16)
             silu = half_gate * one_plus
-            hidden = (silu * up_in).astype(BF16)
-            slope = one_plus * (1.0 + half_gate * (2.0 - one_plus)) * up_in
+            hidden = silu * up_in
+            slope = one_plus * (one + half_gate * (two - one_plus)) * up_in
             kept.append((silu, slope, hidden))
             lifted = lifted + mm(w_out_t_ref[:, at : at + piece], hidden)
             yield True
@@ -282,13 +284,13 @@
             at = index * piece
             cols = slice(at, at + piece)
             up_cols = slice(width + at, width + at + piece)
-            d_hidden = mm(w_half_ref[cols, :], lifted_half)
+            d_hidden = mm(w_half_ref[cols, :], lifted_half).astype(BF16)
             if sums:
                 out_cols = slice(2 * width + at, 2 * width + at + piece)
                 sums_ref[out_cols, :] += mm(hidden, lifted_half, 1, 1)
             yield True
-            d_gate = (d_hidden * slope).astype(BF16)
-            d_up = (d_hidden * silu).astype(BF16)
+            d_gate = d_hidden * slope
+            d_up = d_hidden * silu
             if sums:
                 sums_ref[cols, :] += mm(d_gate, normed_in, 1, 1)
                 sums_ref[up_cols, :] += mm(d_up, normed_in, 1, 1)

time: 166 us -> 164 us (0.988)
  waiting for transfers between devices: 22 us -> 19.4 us
  starting transfers between devices: 20.2 us -> 22.1 us
  Pallas kernels: 87.8 us -> 86.1 us
    pallas_call x2, Pallas kernels: 56.4 us -> 49.6 us  [backward_rows(): pl.pallas_call(functools.partial(backward_kernel, first, last, sums, grad...]
    pallas_call x2, Pallas kernels: 22.8 us -> 28 us  [forward_rows(): pl.pallas_call(functools.partial(forward_kernel, direct, first), grid=(ro...]
    all_to_all x4, waiting for transfers between devices: 20.8 us -> 18.2 us  [swap(): lax.all_to_all(array, 'tok', split_axis=0, concat_axis=0, tiled=True, axi...]
    all_to_all x4, starting transfers between devices: 19.8 us -> 21.6 us  [swap(): lax.all_to_all(array, 'tok', split_axis=0, concat_axis=0, tiled=True, axi...]
where the time goes in v8:
time: 164 us; the launch traced here: 163 us
  Pallas kernels  86.1 us (52%)
  blocking collectives  25.1 us (15%)
  starting transfers between devices  22.1 us (13%)
  waiting for transfers between devices  19.4 us (12%)
  local copies, waits for them, and re-layouts  5.21 us (3%)
  other arithmetic  3.96 us (2%)
    pallas_call x2, Pallas kernels, backward_rows(): pl.pallas_call(functools.partial(backward_kernel, first, last, sums, grad...  49.6 us
    pallas_call x2, Pallas kernels, forward_rows(): pl.pallas_call(functools.partial(forward_kernel, direct, first), grid=(ro...  28 us
    all_to_all x2, blocking collectives, swap(): lax.all_to_all(array, 'tok', split_axis=0, concat_axis=0, tiled=True, axi...  25.1 us
    all_to_all x4, starting transfers between devices, swap(): lax.all_to_all(array, 'tok', split_axis=0, concat_axis=0, tiled=True, axi...  21.6 us
    all_to_all x4, waiting for transfers between devices, swap(): lax.all_to_all(array, 'tok', split_axis=0, concat_axis=0, tiled=True, axi...  18.2 us
    pallas_call x2, Pallas kernels, attend_rows(): pl.pallas_call(functools.partial(attend_kernel, first, last), grid=(layer...  8.53 us
  transfers between devices with their start and end apart: 6, of which 5 were waited for; matrix products, arithmetic and copies ran while one was open for 2% of the time, Pallas kernels for 29%

profile of v8, /device:TPU:0, one launch (start us, length us, event | category | flops | bytes accessed | tf_op | source)
XLA Modules:
  0.0 162.8 jit_solution(8164727106101874565)
XLA Ops:
  0.6 14.1 %pair_forward.2 = (bf16[32,16,512]{2,1,0:T(8,128)(2,1)}, bf16[1024,128]{1,0:T(8,128)(2,1)}, bf16[128,512]{1,0:T(8,128)(2,1)}) custom-call(bf16[32,512,128]{2,1,0:T(8,128)(2,1)} %pair_ref.7, bf16[2,16,128]{2,1,0:T(8,128)(2,1)} %bitcast.65, bf16[128,1024]{1,0:T(8,128)(2,1)} %refs_0_.1, bf16[512,128]{1,0:T(8,128)(2,1)} %refs_1_.1), custom_call_target="tpu_custom_call" | custom-call | flops 9865003008 | bytes 2621440 | tf_op jit(solution)/shard_map/pair_forward/pallas_call | solution.py:176
  14.8 7.4 %all-to-all-start.1 = ((bf16[16,2,16,512]{3,2,1,0:T(8,128)(2,1)}), bf16[16,2,16,512]{3,2,1,0:T(8,128)(2,1)S(1)}, u32[]{:S(2)}, u32[]{:S(2)}) async-start(bf16[16,2,16,512]{3,2,1,0:T(8,128)(2,1)} %bitcast.61), calls=%async_computation.1 | async-start | bytes 1048576 | tf_op jit(solution)/shard_map/all_to_all | solution.py:466
  22.2 0.3 copy.23
  22.5 13.9 %pair_forward.3 = bf16[32,16,512]{2,1,0:T(8,128)(2,1)} custom-call(bf16[32,512,128]{2,1,0:T(8,128)(2,1)} %pair_ref.7, bf16[2,16,128]{2,1,0:T(8,128)(2,1)} %bitcast.66, bf16[1024,128]{1,0:T(8,128)(2,1)} %get-tuple-element.22.refs_0_.w_in_t_ref, bf16[128,512]{1,0:T(8,128)(2,1)} %get-tuple-element.23.refs_1_.w_out_t_ref), custom_call_target="tpu_custom_call" | custom-call | flops 9865003008 | bytes 2621440 | tf_op jit(solution)/shard_map/pair_forward/pallas_call | solution.py:176
  36.4 0.3 all-to-all-done.1.bias_ref
  36.7 5.9 %all-to-all-start = ((bf16[16,2,16,512]{3,2,1,0:T(8,128)(2,1)}), bf16[16,2,16,512]{3,2,1,0:T(8,128)(2,1)S(1)}, u32[]{:S(2)}, u32[]{:S(2)}) async-start(bf16[16,2,16,512]{3,2,1,0:T(8,128)(2,1)} %bitcast.59), calls=%async_computation | async-start | bytes 1048576 | tf_op jit(solution)/shard_map/all_to_all | solution.py:466
  42.6 0.1 copy.25.q_ref
  42.8 0.3 copy.24
  43.3 4.3 %attention_backward.2 = (bf16[2,2,48,256]{3,2,1,0:T(8,128)(2,1)S(1)}, f32[2,2,48,512]{3,2,1,0:T(8,128)S(1)}, f32[2,2,48,512]{3,2,1,0:T(8,128)S(1)}, bf16[16,2,16,512]{3,2,1,0:T(8,128)(2,1)}) custom-call(f32[2]{0:T(128)S(1)} %multiply_divide_fusion.weight_ref, bf16[16,2,16,512]{3,2,1,0:T(8,128)(2,1)S(1)} %all-to-all-done.1.bias_ref, s32[1,512]{1,0:T(1,128)S(1)} %bitcast.46, ...), custom_call_target="tpu_custom_call" | custom-call | flops 5033164800 | bytes 2228224 | tf_op jit(solution)/shard_map/attention_backward/pallas_call | solution.py:444
  47.6 9.4 %all-to-all-done.bias_ref = bf16[16,2,16,512]{3,2,1,0:T(8,128)(2,1)S(1)} async-done(((bf16[16,2,16,512]{3,2,1,0:T(8,128)(2,1)}), bf16[16,2,16,512]{3,2,1,0:T(8,128)(2,1)S(1)}, u32[]{:S(2)}, u32[]{:S(2)}) %all-to-all-start) | async-done | bytes 524320 | tf_op jit(solution)/shard_map/all_to_all | solution.py:466
  57.0 4.3 %all-to-all-start.3 = ((bf16[16,2,16,512]{3,2,1,0:T(8,128)(2,1)}), bf16[16,2,16,512]{3,2,1,0:T(8,128)(2,1)}, u32[]{:S(2)}, u32[]{:S(2)}) async-start(bf16[16,2,16,512]{3,2,1,0:T(8,128)(2,1)} %get-tuple-element.28), calls=%async_computation.3 | async-start | bytes 1048576 | tf_op jit(solution)/shard_map/all_to_all | solution.py:466
  61.3 0.1 copy.27.q_ref
  61.6 0.7 broadcast_multiply_fusion.1.w_half_ref
  62.3 0.7 broadcast_multiply_fusion.w_back_ref
  63.0 4.3 %attention_backward.3 = (bf16[2,2,48,256]{3,2,1,0:T(8,128)(2,1)S(1)}, bf16[2,2,48,512]{3,2,1,0:T(8,128)(2,1)}, bf16[2,2,48,512]{3,2,1,0:T(8,128)(2,1)}, bf16[16,2,16,512]{3,2,1,0:T(8,128)(2,1)}) custom-call(f32[2]{0:T(128)S(1)} %multiply_divide_fusion.weight_ref, bf16[16,2,16,512]{3,2,1,0:T(8,128)(2,1)S(1)} %all-to-all-done.bias_ref, s32[1,512]{1,0:T(1,128)S(1)} %bitcast.47, ...), custom_call_target="tpu_custom_call" | custom-call | flops 5033164800 | bytes 2228224 | tf_op jit(solution)/shard_map/attention_backward/pallas_call | solution.py:444
  67.2 8.5 %all-to-all-done.3 = bf16[16,2,16,512]{3,2,1,0:T(8,128)(2,1)} async-done(((bf16[16,2,16,512]{3,2,1,0:T(8,128)(2,1)}), bf16[16,2,16,512]{3,2,1,0:T(8,128)(2,1)}, u32[]{:S(2)}, u32[]{:S(2)}) %all-to-all-start.3) | async-done | bytes 524320 | tf_op jit(solution)/shard_map/all_to_all | solution.py:466
  75.8 4.0 %all-to-all-start.2 = ((bf16[16,2,16,512]{3,2,1,0:T(8,128)(2,1)}), bf16[16,2,16,512]{3,2,1,0:T(8,128)(2,1)S(1)}, u32[]{:S(2)}, u32[]{:S(2)}) async-start(bf16[16,2,16,512]{3,2,1,0:T(8,128)(2,1)} %get-tuple-element.27), calls=%async_computation.2 | async-start | bytes 1048576 | tf_op jit(solution)/shard_map/all_to_all | solution.py:466
  79.8 24.6 %pair_backward.2 = (bf16[32,512,128]{2,1,0:T(8,128)(2,1)}, f32[1568,128]{1,0:T(8,128)}) custom-call(bf16[32,512,128]{2,1,0:T(8,128)(2,1)} %pair_ref.7, bf16[32,16,512]{2,1,0:T(8,128)(2,1)} %bitcast.17.d_bias_ref, bf16[2,16,128]{2,1,0:T(8,128)(2,1)} %bitcast.67, bf16[1024,128]{1,0:T(8,128)(2,1)} %get-tuple-element.22.refs_0_.w_in_t_ref, ...), custom_call_target="tpu_custom_call" | custom-call | flops 29393682432 | bytes 4718592 | tf_op jit(solution)/shard_map/pair_backward/pallas_call | solution.py:366
  104.4 0.8 copy-done.3
  105.2 25.0 %pair_backward.3 = (bf16[32,512,128]{2,1,0:T(8,128)(2,1)}, f32[1568,128]{1,0:T(8,128)}, bf16[1664,128]{1,0:T(8,128)(2,1)}) custom-call(bf16[32,512,128]{2,1,0:T(8,128)(2,1)} %pair_ref.7, bf16[32,16,512]{2,1,0:T(8,128)(2,1)} %bitcast.60, bf16[2,16,128]{2,1,0:T(8,128)(2,1)} %bitcast.68, ...), custom_call_target="tpu_custom_call", output_to_operand_aliasing={{0}: (8, {})} | custom-call | flops 29393682432 | bytes 4718592 | tf_op jit(solution)/shard_map/pair_backward/pallas_call | solution.py:366
  130.2 0.9 dynamic-slice_bitcast_fusion
  131.1 0.5 collective-permute-start
  131.6 1.1 collective-permute-done
  132.7 1.0 fusion
  133.7 14.2 %all_to_all.30 = bf16[8,104,128]{2,1,0:T(8,128)(2,1)S(1)} all-to-all(bf16[8,104,128]{2,1,0:T(8,128)(2,1)S(1)} %bitcast.58), channel_id=1, replica_groups={{0,2,4,6,8,10,12,14},{1,3,5,7,9,11,13,15},{16,18,20,22,24,26,28,30},{17..., dimensions={0} | all-to-all | bytes 425984 | tf_op jit(solution)/shard_map/all_to_all | solution.py:466
  147.9 11.0 %all_to_all.31 = bf16[8,104,128]{2,1,0:T(8,128)(2,1)S(1)} all-to-all(bf16[8,104,128]{2,1,0:T(8,128)(2,1)S(1)} %broadcast_in_dim.18), channel_id=1, replica_groups={{0,2,4,6,8,10,12,14},{1,3,5,7,9,11,13,15},{16,18,20,22,24,26,28,30},{17..., dimensions={0} | all-to-all | bytes 425984 | tf_op jit(solution)/shard_map/all_to_all | solution.py:466
  158.9 0.2 copy.30
  159.1 0.2 copy.29
  159.4 0.9 copy.32
  160.4 0.6 maximum_convert_fusion.2
  161.0 0.7 maximum_convert_fusion.1
  161.9 1.0 copy.35
  (33 shorter events, 0.8 us)
Async XLA Ops:
  0.6 21.6 %copy-start.5 = (bf16[2,1,2,48,512]{4,3,2,1,0:T(8,128)(2,1)S(1)}, bf16[2,1,2,48,512]{4,3,2,1,0:T(8,128)(2,1)}, u32[]{:S(2)}) copy-start(bf16[2,1,2,48,512]{4,3,2,1,0:T(8,128)(2,1)} %param.16) | copy-start | bytes 589828
  14.8 21.9 %all-to-all-start.1 = ((bf16[16,2,16,512]{3,2,1,0:T(8,128)(2,1)}), bf16[16,2,16,512]{3,2,1,0:T(8,128)(2,1)S(1)}, u32[]{:S(2)}, u32[]{:S(2)}) async-start(bf16[16,2,16,512]{3,2,1,0:T(8,128)(2,1)} %bitcast.61), calls=%async_computation.1 | async-start | bytes 1048576 | tf_op jit(solution)/shard_map/all_to_all | solution.py:466
  22.5 20.2 %copy-start.6 = (bf16[2,1,2,48,512]{4,3,2,1,0:T(8,128)(2,1)S(1)}, bf16[2,1,2,48,512]{4,3,2,1,0:T(8,128)(2,1)}, u32[]{:S(2)}) copy-start(bf16[2,1,2,48,512]{4,3,2,1,0:T(8,128)(2,1)} %param.19) | copy-start | bytes 589828
  36.4 6.8 %copy-start.9 = (s32[2]{0:T(128)S(1)}, s32[2]{0:T(128)}, u32[]{:S(2)}) copy-start(s32[2]{0:T(128)} %param.15) | copy-start | bytes 28
  36.4 6.9 %copy-start = (bf16[2,1,2,48,512]{4,3,2,1,0:T(8,128)(2,1)S(1)}, bf16[2,1,2,48,512]{4,3,2,1,0:T(8,128)(2,1)}, u32[]{:S(2)}) copy-start(bf16[2,1,2,48,512]{4,3,2,1,0:T(8,128)(2,1)} %param.17) | copy-start | bytes 589828
  36.4 6.9 %copy-start.1 = (bf16[2,1,2,48,512]{4,3,2,1,0:T(8,128)(2,1)S(1)}, bf16[2,1,2,48,512]{4,3,2,1,0:T(8,128)(2,1)}, u32[]{:S(2)}) copy-start(bf16[2,1,2,48,512]{4,3,2,1,0:T(8,128)(2,1)} %param.18) | copy-start | bytes 589828
  36.4 6.9 %copy-start.2 = (s32[512]{0:T(512)S(1)}, s32[512]{0:T(512)}, u32[]{:S(2)}) copy-start(s32[512]{0:T(512)} %param.14) | copy-start | bytes 6148
  36.7 20.4 %all-to-all-start = ((bf16[16,2,16,512]{3,2,1,0:T(8,128)(2,1)}), bf16[16,2,16,512]{3,2,1,0:T(8,128)(2,1)S(1)}, u32[]{:S(2)}, u32[]{:S(2)}) async-start(bf16[16,2,16,512]{3,2,1,0:T(8,128)(2,1)} %bitcast.59), calls=%async_computation | async-start | bytes 1048576 | tf_op jit(solution)/shard_map/all_to_all | solution.py:466
  43.3 18.3 %copy-start.7 = (bf16[512,128]{1,0:T(8,128)(2,1)S(1)}, bf16[512,128]{1,0:T(8,128)(2,1)}, u32[]{:S(2)}) copy-start(bf16[512,128]{1,0:T(8,128)(2,1)} %refs_1_.1) | copy-start | bytes 393220
  43.3 19.0 %copy-start.4 = (bf16[128,1024]{1,0:T(8,128)(2,1)S(1)}, bf16[128,1024]{1,0:T(8,128)(2,1)}, u32[]{:S(2)}) copy-start(bf16[128,1024]{1,0:T(8,128)(2,1)} %refs_0_.1) | copy-start | bytes 786436
  43.3 19.0 %copy-start.8 = (bf16[1024]{0:T(1024)(128)(2,1)S(1)}, bf16[1024]{0:T(1024)(128)(2,1)}, u32[]{:S(2)}) copy-start(bf16[1024]{0:T(1024)(128)(2,1)} %constant.51.clone.1) | copy-start | bytes 6148
  57.0 18.7 %all-to-all-start.3 = ((bf16[16,2,16,512]{3,2,1,0:T(8,128)(2,1)}), bf16[16,2,16,512]{3,2,1,0:T(8,128)(2,1)}, u32[]{:S(2)}, u32[]{:S(2)}) async-start(bf16[16,2,16,512]{3,2,1,0:T(8,128)(2,1)} %get-tuple-element.28), calls=%async_computation.3 | async-start | bytes 1048576 | tf_op jit(solution)/shard_map/all_to_all | solution.py:466
  75.8 28.6 %all-to-all-start.2 = ((bf16[16,2,16,512]{3,2,1,0:T(8,128)(2,1)}), bf16[16,2,16,512]{3,2,1,0:T(8,128)(2,1)S(1)}, u32[]{:S(2)}, u32[]{:S(2)}) async-start(bf16[16,2,16,512]{3,2,1,0:T(8,128)(2,1)} %get-tuple-element.27), calls=%async_computation.2 | async-start | bytes 1048576 | tf_op jit(solution)/shard_map/all_to_all | solution.py:466
  104.4 0.8 copy-start.3
  131.1 1.6 collective-permute-start
  158.9 1.5 collective-permute-start.1

commit v9 on v8

--- a/solution.py
+++ b/solution.py
@@ -133,7 +133,7 @@
         else:
             bias_ref[row] = bias.astype(BF16)
 
-    for_groups(step, 2, lambda at, count: interleave(lambda i: stages(at + i), count, 0))
+    for_groups(step, 8, lambda at, count: interleave(lambda i: stages(at + i), count, 0))
 
     if direct:
 
@@ -302,7 +302,7 @@
             pair_grad = d_lifted + norm_back(normed_float, inv_in, d_normed_in)
             pair_grad_ref[row] = pair_grad.astype(BF16).T
 
-    for_groups(step, 4, lambda at, count: interleave(lambda i: stages(at + i), count, 2))
+    for_groups(step, 8, lambda at, count: interleave(lambda i: stages(at + i), count, 0))
 
     if last:
         packed_ref = outs.pop(0)

time: 164 us -> 158 us (0.963)
  Pallas kernels: 86.1 us -> 78.9 us
  waiting for transfers between devices: 19.4 us -> 22.2 us
  starting transfers between devices: 22.1 us -> 20.4 us
    pallas_call x2, Pallas kernels: 28 us -> 22 us  [forward_rows(): pl.pallas_call(functools.partial(forward_kernel, direct, first), grid=(ro...]
    all_to_all x4, waiting for transfers between devices: 18.2 us -> 21 us  [swap(): lax.all_to_all(array, 'tok', split_axis=0, concat_axis=0, tiled=True, axi...]
    all_to_all x4, starting transfers between devices: 21.6 us -> 19.9 us  [swap(): lax.all_to_all(array, 'tok', split_axis=0, concat_axis=0, tiled=True, axi...]
  transfers between devices with their start and end apart: 6 -> 6, of which waited for: 5 -> 5; matrix products, arithmetic and copies ran while one was open for 2% -> 2% of each run, Pallas kernels for 29% -> 28%
where the time goes in v9:
time: 158 us; the launch traced here: 157 us
  Pallas kernels  78.9 us (50%)
  blocking collectives  25.1 us (16%)
  waiting for transfers between devices  22.2 us (14%)
  starting transfers between devices  20.4 us (13%)
  local copies, waits for them, and re-layouts  5.21 us (3%)
  other arithmetic  3.96 us (3%)
    pallas_call x2, Pallas kernels, backward_rows(): pl.pallas_call(functools.partial(backward_kernel, first, last, sums, grad...  48.4 us
    all_to_all x2, blocking collectives, swap(): lax.all_to_all(array, 'tok', split_axis=0, concat_axis=0, tiled=True, axi...  25.1 us
    pallas_call x2, Pallas kernels, forward_rows(): pl.pallas_call(functools.partial(forward_kernel, direct, first), grid=(ro...  22 us
    all_to_all x4, waiting for transfers between devices, swap(): lax.all_to_all(array, 'tok', split_axis=0, concat_axis=0, tiled=True, axi...  21 us
    all_to_all x4, starting transfers between devices, swap(): lax.all_to_all(array, 'tok', split_axis=0, concat_axis=0, tiled=True, axi...  19.9 us
    pallas_call x2, Pallas kernels, attend_rows(): pl.pallas_call(functools.partial(attend_kernel, first, last), grid=(layer...  8.52 us
    unnamed x24, local copies, waits for them, and re-layouts  3.28 us
  transfers between devices with their start and end apart: 6, of which 5 were waited for; matrix products, arithmetic and copies ran while one was open for 2% of the time, Pallas kernels for 28%

profile of v9, /device:TPU:0, one launch (start us, length us, event | category | flops | bytes accessed | tf_op | source)
XLA Modules:
  0.0 156.8 jit_solution(6023337382633323441)
XLA Ops:
  0.6 11.1 %pair_forward.2 = (bf16[32,16,512]{2,1,0:T(8,128)(2,1)}, bf16[1024,128]{1,0:T(8,128)(2,1)}, bf16[128,512]{1,0:T(8,128)(2,1)}) custom-call(bf16[32,512,128]{2,1,0:T(8,128)(2,1)} %pair_ref.7, bf16[2,16,128]{2,1,0:T(8,128)(2,1)} %bitcast.65, bf16[128,1024]{1,0:T(8,128)(2,1)} %refs_0_.1, bf16[512,128]{1,0:T(8,128)(2,1)} %refs_1_.1), custom_call_target="tpu_custom_call" | custom-call | flops 9865003008 | bytes 2621440 | tf_op jit(solution)/shard_map/pair_forward/pallas_call | solution.py:176
  11.8 7.4 %all-to-all-start.1 = ((bf16[16,2,16,512]{3,2,1,0:T(8,128)(2,1)}), bf16[16,2,16,512]{3,2,1,0:T(8,128)(2,1)S(1)}, u32[]{:S(2)}, u32[]{:S(2)}) async-start(bf16[16,2,16,512]{3,2,1,0:T(8,128)(2,1)} %bitcast.61), calls=%async_computation.1 | async-start | bytes 1048576 | tf_op jit(solution)/shard_map/all_to_all | solution.py:466
  19.2 0.3 copy.23
  19.5 10.9 %pair_forward.3 = bf16[32,16,512]{2,1,0:T(8,128)(2,1)} custom-call(bf16[32,512,128]{2,1,0:T(8,128)(2,1)} %pair_ref.7, bf16[2,16,128]{2,1,0:T(8,128)(2,1)} %bitcast.66, bf16[1024,128]{1,0:T(8,128)(2,1)} %get-tuple-element.22.refs_0_.w_in_t_ref, bf16[128,512]{1,0:T(8,128)(2,1)} %get-tuple-element.23.refs_1_.w_out_t_ref), custom_call_target="tpu_custom_call" | custom-call | flops 9865003008 | bytes 2621440 | tf_op jit(solution)/shard_map/pair_forward/pallas_call | solution.py:176
  30.4 3.2 %all-to-all-done.1.bias_ref = bf16[16,2,16,512]{3,2,1,0:T(8,128)(2,1)S(1)} async-done(((bf16[16,2,16,512]{3,2,1,0:T(8,128)(2,1)}), bf16[16,2,16,512]{3,2,1,0:T(8,128)(2,1)S(1)}, u32[]{:S(2)}, u32[]{:S(2)}) %all-to-all-start.1) | async-done | bytes 524320 | tf_op jit(solution)/shard_map/all_to_all | solution.py:466
  33.7 4.1 %all-to-all-start = ((bf16[16,2,16,512]{3,2,1,0:T(8,128)(2,1)}), bf16[16,2,16,512]{3,2,1,0:T(8,128)(2,1)S(1)}, u32[]{:S(2)}, u32[]{:S(2)}) async-start(bf16[16,2,16,512]{3,2,1,0:T(8,128)(2,1)} %bitcast.59), calls=%async_computation | async-start | bytes 1048576 | tf_op jit(solution)/shard_map/all_to_all | solution.py:466
  37.8 0.1 copy.25.q_ref
  37.9 0.3 copy.24
  38.5 4.3 %attention_backward.2 = (bf16[2,2,48,256]{3,2,1,0:T(8,128)(2,1)S(1)}, f32[2,2,48,512]{3,2,1,0:T(8,128)S(1)}, f32[2,2,48,512]{3,2,1,0:T(8,128)S(1)}, bf16[16,2,16,512]{3,2,1,0:T(8,128)(2,1)}) custom-call(f32[2]{0:T(128)S(1)} %multiply_divide_fusion.weight_ref, bf16[16,2,16,512]{3,2,1,0:T(8,128)(2,1)S(1)} %all-to-all-done.1.bias_ref, s32[1,512]{1,0:T(1,128)S(1)} %bitcast.46, ...), custom_call_target="tpu_custom_call" | custom-call | flops 5033164800 | bytes 2228224 | tf_op jit(solution)/shard_map/attention_backward/pallas_call | solution.py:444
  42.8 9.4 %all-to-all-done.bias_ref = bf16[16,2,16,512]{3,2,1,0:T(8,128)(2,1)S(1)} async-done(((bf16[16,2,16,512]{3,2,1,0:T(8,128)(2,1)}), bf16[16,2,16,512]{3,2,1,0:T(8,128)(2,1)S(1)}, u32[]{:S(2)}, u32[]{:S(2)}) %all-to-all-start) | async-done | bytes 524320 | tf_op jit(solution)/shard_map/all_to_all | solution.py:466
  52.2 4.4 %all-to-all-start.3 = ((bf16[16,2,16,512]{3,2,1,0:T(8,128)(2,1)}), bf16[16,2,16,512]{3,2,1,0:T(8,128)(2,1)}, u32[]{:S(2)}, u32[]{:S(2)}) async-start(bf16[16,2,16,512]{3,2,1,0:T(8,128)(2,1)} %get-tuple-element.28), calls=%async_computation.3 | async-start | bytes 1048576 | tf_op jit(solution)/shard_map/all_to_all | solution.py:466
  56.7 0.1 copy.27.q_ref
  57.0 0.7 broadcast_multiply_fusion.1.w_half_ref
  57.6 0.7 broadcast_multiply_fusion.w_back_ref
  58.4 4.2 %attention_backward.3 = (bf16[2,2,48,256]{3,2,1,0:T(8,128)(2,1)S(1)}, bf16[2,2,48,512]{3,2,1,0:T(8,128)(2,1)}, bf16[2,2,48,512]{3,2,1,0:T(8,128)(2,1)}, bf16[16,2,16,512]{3,2,1,0:T(8,128)(2,1)}) custom-call(f32[2]{0:T(128)S(1)} %multiply_divide_fusion.weight_ref, bf16[16,2,16,512]{3,2,1,0:T(8,128)(2,1)S(1)} %all-to-all-done.bias_ref, s32[1,512]{1,0:T(1,128)S(1)} %bitcast.47, ...), custom_call_target="tpu_custom_call" | custom-call | flops 5033164800 | bytes 2228224 | tf_op jit(solution)/shard_map/attention_backward/pallas_call | solution.py:444
  62.6 8.4 %all-to-all-done.3 = bf16[16,2,16,512]{3,2,1,0:T(8,128)(2,1)} async-done(((bf16[16,2,16,512]{3,2,1,0:T(8,128)(2,1)}), bf16[16,2,16,512]{3,2,1,0:T(8,128)(2,1)}, u32[]{:S(2)}, u32[]{:S(2)}) %all-to-all-start.3) | async-done | bytes 524320 | tf_op jit(solution)/shard_map/all_to_all | solution.py:466
  71.0 4.0 %all-to-all-start.2 = ((bf16[16,2,16,512]{3,2,1,0:T(8,128)(2,1)}), bf16[16,2,16,512]{3,2,1,0:T(8,128)(2,1)S(1)}, u32[]{:S(2)}, u32[]{:S(2)}) async-start(bf16[16,2,16,512]{3,2,1,0:T(8,128)(2,1)} %get-tuple-element.27), calls=%async_computation.2 | async-start | bytes 1048576 | tf_op jit(solution)/shard_map/all_to_all | solution.py:466
  75.0 23.9 %pair_backward.2 = (bf16[32,512,128]{2,1,0:T(8,128)(2,1)}, f32[1568,128]{1,0:T(8,128)}) custom-call(bf16[32,512,128]{2,1,0:T(8,128)(2,1)} %pair_ref.7, bf16[32,16,512]{2,1,0:T(8,128)(2,1)} %bitcast.17.d_bias_ref, bf16[2,16,128]{2,1,0:T(8,128)(2,1)} %bitcast.67, bf16[1024,128]{1,0:T(8,128)(2,1)} %get-tuple-element.22.refs_0_.w_in_t_ref, ...), custom_call_target="tpu_custom_call" | custom-call | flops 29393682432 | bytes 4718592 | tf_op jit(solution)/shard_map/pair_backward/pallas_call | solution.py:366
  98.9 0.8 copy-done.3
  99.7 24.5 %pair_backward.3 = (bf16[32,512,128]{2,1,0:T(8,128)(2,1)}, f32[1568,128]{1,0:T(8,128)}, bf16[1664,128]{1,0:T(8,128)(2,1)}) custom-call(bf16[32,512,128]{2,1,0:T(8,128)(2,1)} %pair_ref.7, bf16[32,16,512]{2,1,0:T(8,128)(2,1)} %bitcast.60, bf16[2,16,128]{2,1,0:T(8,128)(2,1)} %bitcast.68, ...), custom_call_target="tpu_custom_call", output_to_operand_aliasing={{0}: (8, {})} | custom-call | flops 29393682432 | bytes 4718592 | tf_op jit(solution)/shard_map/pair_backward/pallas_call | solution.py:366
  124.2 0.9 dynamic-slice_bitcast_fusion
  125.1 0.5 collective-permute-start
  125.6 1.1 collective-permute-done
  126.7 1.0 fusion
  127.7 14.2 %all_to_all.30 = bf16[8,104,128]{2,1,0:T(8,128)(2,1)S(1)} all-to-all(bf16[8,104,128]{2,1,0:T(8,128)(2,1)S(1)} %bitcast.58), channel_id=1, replica_groups={{0,2,4,6,8,10,12,14},{1,3,5,7,9,11,13,15},{16,18,20,22,24,26,28,30},{17..., dimensions={0} | all-to-all | bytes 425984 | tf_op jit(solution)/shard_map/all_to_all | solution.py:466
  141.9 11.0 %all_to_all.31 = bf16[8,104,128]{2,1,0:T(8,128)(2,1)S(1)} all-to-all(bf16[8,104,128]{2,1,0:T(8,128)(2,1)S(1)} %broadcast_in_dim.18), channel_id=1, replica_groups={{0,2,4,6,8,10,12,14},{1,3,5,7,9,11,13,15},{16,18,20,22,24,26,28,30},{17..., dimensions={0} | all-to-all | bytes 425984 | tf_op jit(solution)/shard_map/all_to_all | solution.py:466
  152.9 0.2 copy.30
  153.0 0.2 copy.29
  153.3 0.9 copy.32
  154.4 0.6 maximum_convert_fusion.2
  155.0 0.7 maximum_convert_fusion.1
  155.8 1.0 copy.35
  (33 shorter events, 0.8 us)
Async XLA Ops:
  0.6 18.6 %copy-start.5 = (bf16[2,1,2,48,512]{4,3,2,1,0:T(8,128)(2,1)S(1)}, bf16[2,1,2,48,512]{4,3,2,1,0:T(8,128)(2,1)}, u32[]{:S(2)}) copy-start(bf16[2,1,2,48,512]{4,3,2,1,0:T(8,128)(2,1)} %param.16) | copy-start | bytes 589828
  11.8 21.9 %all-to-all-start.1 = ((bf16[16,2,16,512]{3,2,1,0:T(8,128)(2,1)}), bf16[16,2,16,512]{3,2,1,0:T(8,128)(2,1)S(1)}, u32[]{:S(2)}, u32[]{:S(2)}) async-start(bf16[16,2,16,512]{3,2,1,0:T(8,128)(2,1)} %bitcast.61), calls=%async_computation.1 | async-start | bytes 1048576 | tf_op jit(solution)/shard_map/all_to_all | solution.py:466
  19.5 18.4 %copy-start.6 = (bf16[2,1,2,48,512]{4,3,2,1,0:T(8,128)(2,1)S(1)}, bf16[2,1,2,48,512]{4,3,2,1,0:T(8,128)(2,1)}, u32[]{:S(2)}) copy-start(bf16[2,1,2,48,512]{4,3,2,1,0:T(8,128)(2,1)} %param.19) | copy-start | bytes 589828
  30.4 8.0 %copy-start.9 = (s32[2]{0:T(128)S(1)}, s32[2]{0:T(128)}, u32[]{:S(2)}) copy-start(s32[2]{0:T(128)} %param.15) | copy-start | bytes 28
  30.4 8.1 %copy-start = (bf16[2,1,2,48,512]{4,3,2,1,0:T(8,128)(2,1)S(1)}, bf16[2,1,2,48,512]{4,3,2,1,0:T(8,128)(2,1)}, u32[]{:S(2)}) copy-start(bf16[2,1,2,48,512]{4,3,2,1,0:T(8,128)(2,1)} %param.17) | copy-start | bytes 589828
  30.4 8.1 %copy-start.1 = (bf16[2,1,2,48,512]{4,3,2,1,0:T(8,128)(2,1)S(1)}, bf16[2,1,2,48,512]{4,3,2,1,0:T(8,128)(2,1)}, u32[]{:S(2)}) copy-start(bf16[2,1,2,48,512]{4,3,2,1,0:T(8,128)(2,1)} %param.18) | copy-start | bytes 589828
  30.4 8.1 %copy-start.2 = (s32[512]{0:T(512)S(1)}, s32[512]{0:T(512)}, u32[]{:S(2)}) copy-start(s32[512]{0:T(512)} %param.14) | copy-start | bytes 6148
  33.7 18.6 %all-to-all-start = ((bf16[16,2,16,512]{3,2,1,0:T(8,128)(2,1)}), bf16[16,2,16,512]{3,2,1,0:T(8,128)(2,1)S(1)}, u32[]{:S(2)}, u32[]{:S(2)}) async-start(bf16[16,2,16,512]{3,2,1,0:T(8,128)(2,1)} %bitcast.59), calls=%async_computation | async-start | bytes 1048576 | tf_op jit(solution)/shard_map/all_to_all | solution.py:466
  38.5 18.5 %copy-start.7 = (bf16[512,128]{1,0:T(8,128)(2,1)S(1)}, bf16[512,128]{1,0:T(8,128)(2,1)}, u32[]{:S(2)}) copy-start(bf16[512,128]{1,0:T(8,128)(2,1)} %refs_1_.1) | copy-start | bytes 393220
  38.5 19.1 %copy-start.4 = (bf16[128,1024]{1,0:T(8,128)(2,1)S(1)}, bf16[128,1024]{1,0:T(8,128)(2,1)}, u32[]{:S(2)}) copy-start(bf16[128,1024]{1,0:T(8,128)(2,1)} %refs_0_.1) | copy-start | bytes 786436
  38.5 19.1 %copy-start.8 = (bf16[1024]{0:T(1024)(128)(2,1)S(1)}, bf16[1024]{0:T(1024)(128)(2,1)}, u32[]{:S(2)}) copy-start(bf16[1024]{0:T(1024)(128)(2,1)} %constant.51.clone.1) | copy-start | bytes 6148
  52.2 18.7 %all-to-all-start.3 = ((bf16[16,2,16,512]{3,2,1,0:T(8,128)(2,1)}), bf16[16,2,16,512]{3,2,1,0:T(8,128)(2,1)}, u32[]{:S(2)}, u32[]{:S(2)}) async-start(bf16[16,2,16,512]{3,2,1,0:T(8,128)(2,1)} %get-tuple-element.28), calls=%async_computation.3 | async-start | bytes 1048576 | tf_op jit(solution)/shard_map/all_to_all | solution.py:466
  71.0 27.9 %all-to-all-start.2 = ((bf16[16,2,16,512]{3,2,1,0:T(8,128)(2,1)}), bf16[16,2,16,512]{3,2,1,0:T(8,128)(2,1)S(1)}, u32[]{:S(2)}, u32[]{:S(2)}) async-start(bf16[16,2,16,512]{3,2,1,0:T(8,128)(2,1)} %get-tuple-element.27), calls=%async_computation.2 | async-start | bytes 1048576 | tf_op jit(solution)/shard_map/all_to_all | solution.py:466
  98.9 0.8 copy-start.3
  125.1 1.6 collective-permute-start
  152.9 1.5 collective-permute-start.1

commit v10 on v5

--- a/solution.py
+++ b/solution.py
@@ -59,7 +59,7 @@
     running = []
     clock = 0
     while rows or running:
-        if rows and clock % lag == 0:
+        while rows and clock >= lag * (count - len(rows)):
             running.append(rows.pop(0))
         running = [row for row in running if next(row, None) is not None]
         clock += 1
@@ -86,17 +86,30 @@
     return rows % 8 == 0 and crop % 128 == 0
 
 
-def forward_kernel(direct, first, pair_ref, w_bias_ref, *refs):
+def forward_kernel(direct, first, taken, emit, base, after, pair_ref, w_bias_ref, *refs):
+    refs = list(refs)
     if first:
-        w_in_ref, w_out_ref, bias_ref, w_in_t_ref, w_out_t_ref, w_back_ref, w_half_ref = refs[:-1]
+        w_in_ref, w_out_ref = refs.pop(0), refs.pop(0)
     else:
-        w_in_t_ref, w_out_t_ref, bias_ref = refs[:-1]
-    lines_ref = refs[-1]
+        w_in_t_ref, w_out_t_ref = refs.pop(0), refs.pop(0)
+    taken_ref = refs.pop(0) if taken else None
+    if after:
+        refs.pop(0)
+    bias_ref = refs.pop(0) if emit else None
+    if first:
+        w_in_t_ref, w_out_t_ref = refs.pop(0), refs.pop(0)
+    lines_ref = refs.pop(0)
     width = w_out_t_ref.shape[1]
     layers, heads, channels = w_bias_ref.shape
     piece = split_width(width)
     step = pair_ref.shape[0]
-    first_row = pl.program_id(0) * step
+    first_row = base + pl.program_id(0) * step
+
+    if taken:
+
+        @pl.when(pl.program_id(0) == 0)
+        def _():
+            lines_ref[...] = taken_ref[...]
 
     if first:
 
@@ -106,9 +119,6 @@
             w_in_t_ref[:width, :] = w_in_t[:width] * 0.5
             w_in_t_ref[width:, :] = w_in_t[width:]
             w_out_t_ref[...] = w_out_ref[...].T
-            w_back_ref[:, :width] = w_in_ref[:, :width]
-            w_back_ref[:, width:] = w_in_ref[:, width:] * 2.0
-            w_half_ref[...] = w_out_ref[...] * 0.5
 
     def stages(row):
         pair_float = pair_ref[row].T.astype(F32)
@@ -136,9 +146,9 @@
         else:
             bias_ref[row] = bias.astype(BF16)
 
-    for_groups(step, 4, lambda at, count: interleave(lambda i: stages(at + i), count, 2))
-
-    if direct:
+    for_groups(step, 8, lambda at, count: interleave(lambda i: stages(at + i), count, 0))
+
+    if direct and emit:
 
         @pl.when(pl.program_id(0) == pl.num_programs(0) - 1)
         def _():
@@ -152,40 +162,54 @@
     return pl.BlockSpec(array.shape, lambda i: (0,) * len(array.shape))
 
 
-def forward_rows(start, rows, pair, w_in, w_out, w_bias, prepared):
+def forward_rows(
+    start, rows, pair, w_in, w_out, w_bias, prepared, base=0, chunk_rows=None, taken=None, after=None
+):
     crop, channels = pair.shape[1:]
     layers, heads, _ = w_bias.shape
     lanes = layers * heads
+    chunk_rows = chunk_rows or rows
     step = row_step(rows)
     first_step = start // step
     positions = rows * crop
     width = w_out.shape[0]
-    direct = is_direct(rows, crop)
+    direct = is_direct(chunk_rows, crop)
     first = prepared is None
-    line_shape = (heads * layers, rows, crop) if direct else (rows, lanes, crop)
-    shapes = [jax.ShapeDtypeStruct(line_shape, BF16)]
-    out_specs = [
-        whole_spec(shapes[0])
-        if direct
-        else pl.BlockSpec((step, lanes, crop), lambda i: (i, 0, 0))
-    ]
+    emit = base + rows == chunk_rows
+    shapes, out_specs, scratch = [], [], []
+    line_shape = (crop // 128, lanes * chunk_rows, 128) if direct else (1, 8, 128)
+    if not emit:
+        shapes.append(jax.ShapeDtypeStruct(line_shape, F32))
+        out_specs.append(whole_spec(shapes[0]))
+    elif direct:
+        shapes.append(jax.ShapeDtypeStruct((lanes, chunk_rows, crop), BF16))
+        out_specs.append(whole_spec(shapes[0]))
+    else:
+        shapes.append(jax.ShapeDtypeStruct((rows, lanes, crop), BF16))
+        out_specs.append(pl.BlockSpec((step, lanes, crop), lambda i: (i, 0, 0)))
+    if emit:
+        scratch.append(pltpu.VMEM(line_shape, F32))
+    operands = [pair, w_bias, *((w_in, w_out) if first else prepared)]
     if first:
-        operands = [pair, w_bias, w_in, w_out]
-        for shape in (w_in.shape[::-1], w_out.shape[::-1], w_in.shape, w_out.shape):
+        for shape in (w_in.shape[::-1], w_out.shape[::-1]):
             shapes.append(jax.ShapeDtypeStruct(shape, BF16))
             out_specs.append(whole_spec(shapes[-1]))
-    else:
-        operands = [pair, w_bias, *prepared[:2]]
+    if taken is not None:
+        operands.append(taken)
+    in_specs = [pl.BlockSpec((step, crop, channels), lambda i: (first_step + i, 0, 0))]
+    in_specs += [whole_spec(array) for array in operands[1:]]
+    if after is not None:
+        operands.append(after)
+        in_specs.append(pl.BlockSpec(memory_space=pl.ANY))
     return pl.pallas_call(
-        functools.partial(forward_kernel, direct, first),
+        functools.partial(
+            forward_kernel, direct, first, taken is not None, emit, base, after is not None
+        ),
         grid=(rows // step,),
-        in_specs=[pl.BlockSpec((step, crop, channels), lambda i: (first_step + i, 0, 0))]
-        + [whole_spec(array) for array in operands[1:]],
+        in_specs=in_specs,
         out_specs=out_specs,
         out_shape=shapes,
-        scratch_shapes=[
-            pltpu.VMEM((crop // 128, lanes * rows, 128) if direct else (1, 8, 128), F32),
-        ],
+        scratch_shapes=scratch,
         compiler_params=pltpu.CompilerParams(vmem_limit_bytes=56 * 2**20),
         cost_estimate=pl.CostEstimate(
             flops=6 * positions * channels * (3 * width + lanes),
@@ -200,6 +224,7 @@
     first,
     last,
     direct,
+    base,
     pair_ref,
     d_bias_ref,
     w_bias_ref,
@@ -209,17 +234,20 @@
     w_half_ref,
     *refs,
 ):
-    if first:
-        pair_grad_ref, sums_ref = refs[:2]
-    else:
-        before_ref, _, pair_grad_ref, sums_ref = refs[:4]
+    outs = list(refs[:-1])
+    parity_ref = outs.pop(0) if last else None
+    if not first:
+        before_ref = outs.pop(0)
+        outs.pop(0)
+    pair_grad_ref, sums_ref = outs.pop(0), outs.pop(0)
     lines_ref = refs[-1]
     width = w_half_ref.shape[0]
     layers, heads, channels = w_bias_ref.shape
     lanes = layers * heads
     piece = split_width(width)
     step = pair_ref.shape[0]
-    first_row = pl.program_id(0) * step
+    one, two = jnp.asarray(1.0, BF16), jnp.asarray(2.0, BF16)
+    first_row = base + pl.program_id(0) * step
 
     @pl.when(pl.program_id(0) == 0)
     def _():
@@ -255,10 +283,11 @@
             half_gate = mm(w_in_t_ref[at : at + piece, :], normed_in)
             up_in = mm(w_in_t_ref[width + at : width + at + piece, :], normed_in)
             yield True
-            one_plus = 1.0 + jnp.tanh(half_gate)
+            one_plus = (1.0 + jnp.tanh(half_gate)).astype(BF16)
+            half_gate, up_in = half_gate.astype(BF16), up_in.astype(BF16)
             silu = half_gate * one_plus
-            hidden = (silu * up_in).astype(BF16)
-            slope = one_plus * (1.0 + half_gate * (2.0 - one_plus)) * up_in
+            hidden = silu * up_in
+            slope = one_plus * (one + half_gate * (two - one_plus)) * up_in
             kept.append((silu, slope, hidden))
             lifted = lifted + mm(w_out_t_ref[:, at : at + piece], hidden)
             yield True
@@ -267,7 +296,7 @@
         yield True
         d_bias = read_lines(row)
         d_normed = mm(w_bias_ref[...].reshape(lanes, channels), d_bias, 0, 0)
-        sums_ref[3 * width :, :] += mm(d_bias, normed_out, 1, 1)
+        sums_ref[3 * width : 3 * width + lanes, :] += mm(d_bias, normed_out, 1, 1)
         d_lifted = norm_back(out_float, inv_out, d_normed)
         lifted_half = d_lifted.astype(BF16)
         yield True
@@ -276,34 +305,36 @@
             at = index * piece
             cols = slice(at, at + piece)
             up_cols = slice(width + at, width + at + piece)
-            d_hidden = mm(w_half_ref[cols, :], lifted_half)
-            sums_ref[2 * width + at : 2 * width + at + piece, :] += mm(hidden, lifted_half, 1, 1)
+            d_hidden = mm(w_half_ref[cols, :], lifted_half).astype(BF16)
+            out_cols = slice(2 * width + at, 2 * width + at + piece)
+            sums_ref[out_cols, :] += mm(hidden, lifted_half, 1, 1)
             yield True
-            d_gate = (d_hidden * slope).astype(BF16)
-            d_up = (d_hidden * silu).astype(BF16)
-            part = mm(w_back_ref[:, cols], d_gate)
+            d_gate = d_hidden * slope
+            d_up = d_hidden * silu
             sums_ref[cols, :] += mm(d_gate, normed_in, 1, 1)
-            part = part + mm(w_back_ref[:, up_cols], d_up)
             sums_ref[up_cols, :] += mm(d_up, normed_in, 1, 1)
+            part = mm(w_back_ref[:, cols], d_gate) + mm(w_back_ref[:, up_cols], d_up)
             d_normed_in = part if d_normed_in is None else d_normed_in + part
             yield True
         pair_grad = d_lifted + norm_back(normed_float, inv_in, d_normed_in)
         pair_grad_ref[row] = pair_grad.astype(BF16).T
 
-    for_groups(step, 4, lambda at, count: interleave(lambda i: stages(at + i), count, 3))
+    for_groups(step, 8, lambda at, count: interleave(lambda i: stages(at + i), count, 0))
 
     if last:
-        packed_ref = refs[-2]
+        keep_ref, send_ref = outs
 
         @pl.when(pl.program_id(0) == pl.num_programs(0) - 1)
         def _():
-            done = sums_ref.shape[0]
-            packed_ref[:done, :] = sums_ref[...].astype(BF16)
-            packed_ref[width : 2 * width, :] = (2.0 * sums_ref[width : 2 * width, :]).astype(BF16)
-            packed_ref[done:, :] = jnp.zeros((packed_ref.shape[0] - done, packed_ref.shape[1]), BF16)
-
-
-def backward_rows(start, rows, packed_rows, pair, d_bias, w_bias, prepared, state):
+            half = sums_ref.shape[0] // 2
+            parity = parity_ref[0]
+            sums_ref[width : 2 * width, :] = 2.0 * sums_ref[width : 2 * width, :]
+            keep_ref[...] = sums_ref[pl.ds(pl.multiple_of(parity * half, 8), half), :]
+            other = pl.ds(pl.multiple_of((1 - parity) * half, 8), half)
+            send_ref[...] = sums_ref[other, :].astype(BF16)
+
+
+def backward_rows(start, rows, base, direct, sum_rows, pair, d_bias, w_bias, prepared, state, parity):
     crop, channels = pair.shape[1:]
     layers, heads, _ = w_bias.shape
     lanes = layers * heads
@@ -312,12 +343,14 @@
     first_step = start // step
     positions = rows * crop
     first, last = start == 0, start + rows == pair.shape[0]
-    direct = is_direct(rows, crop)
     pair_spec = pl.BlockSpec((step, crop, channels), lambda i: (first_step + i, 0, 0))
     line_spec = whole_spec(d_bias) if direct else pl.BlockSpec((step, lanes, crop), lambda i: (i, 0, 0))
     operands = [pair, d_bias, w_bias, *prepared]
     in_specs = [pair_spec, line_spec] + [whole_spec(array) for array in operands[2:]]
     aliases = {}
+    if last:
+        operands.append(parity)
+        in_specs.append(pl.BlockSpec(memory_space=pltpu.SMEM))
     if not first:
         pair_grad, sums = state
         operands += [sums, pair_grad]
@@ -325,21 +358,22 @@
         aliases = {len(operands) - 1: 0}
     shapes = [
         jax.ShapeDtypeStruct(pair.shape, BF16),
-        jax.ShapeDtypeStruct((3 * width + lanes, channels), F32),
+        jax.ShapeDtypeStruct((sum_rows, channels), F32),
     ]
-    out_specs = [pair_spec, whole_spec(shapes[1])]
     if last:
-        shapes.append(jax.ShapeDtypeStruct((packed_rows, channels), BF16))
-        out_specs.append(whole_spec(shapes[2]))
+        shapes.append(jax.ShapeDtypeStruct((sum_rows // 2, channels), F32))
+        shapes.append(jax.ShapeDtypeStruct((sum_rows // 2, channels), BF16))
+    out_specs = [pair_spec] + [whole_spec(shape) for shape in shapes[1:]]
+    line_rows = lanes * d_bias.shape[1]
     return pl.pallas_call(
-        functools.partial(backward_kernel, first, last, direct),
+        functools.partial(backward_kernel, first, last, direct, base),
         grid=(rows // step,),
         in_specs=in_specs,
         out_specs=out_specs,
         out_shape=shapes,
         input_output_aliases=aliases,
         scratch_shapes=[
-            pltpu.VMEM((crop // 128, lanes * rows, 128) if direct else (1, 8, 128), F32),
+            pltpu.VMEM((crop // 128, line_rows, 128) if direct else (1, 8, 128), F32),
         ],
         compiler_params=pltpu.CompilerParams(vmem_limit_bytes=56 * 2**20),
         cost_estimate=pl.CostEstimate(
@@ -357,7 +391,7 @@
     if first:
         dq_ref, dk_ref, dv_ref, d_bias_ref = refs
     else:
-        dk_before_ref, dv_before_ref, dq_ref, dk_ref, dv_ref, d_bias_ref = refs
+        dk_before_ref, dv_before_ref, _, dq_ref, dk_ref, dv_ref, d_bias_ref = refs
     samples, depth = q_ref.shape[1:3]
     sources, _, rows, crop = bias_ref.shape
     scaling = 1.0 / math.sqrt(depth)
@@ -390,7 +424,7 @@
     d_bias_ref[:, 0] = total.astype(BF16).reshape(sources, rows, crop)
 
 
-def attend_rows(first, last, weights, bias, valid, query, key, value, grad, state):
+def attend_rows(first, last, weights, bias, valid, query, key, value, grad, state, after):
     sources, layers, rows, crop = bias.shape
     samples, depth, row_count = query.shape[1:]
     vec = lambda shape: pl.BlockSpec((1,) + shape[1:], lambda l: (l, 0, 0, 0))
@@ -406,8 +440,8 @@
     ]
     operands = [weights, bias, valid, query, key, value, grad]
     if not first:
-        operands += list(state)
-        in_specs += [vec(key.shape), vec(value.shape)]
+        operands += [*state, after]
+        in_specs += [vec(key.shape), vec(value.shape), pl.BlockSpec(memory_space=pl.ANY)]
     kind = BF16 if last else F32
     return pl.pallas_call(
         functools.partial(attend_kernel, first, last),
@@ -436,25 +470,30 @@
     )
 
 
-def sum_over_devices(array):
+def sum_pairs(keep, send):
+    across = [(index, index ^ 1) for index in range(lax.axis_size("tok"))]
+    return (keep + lax.ppermute(send, "tok", across).astype(F32)).astype(BF16)
+
+
+def sum_team(array):
     devices = lax.axis_size("tok")
-    parity = lax.axis_index("tok") % 2
+    teams = [list(range(odd, devices, 2)) for odd in range(2)]
+    members = devices // 2
+    parts = swap(array.reshape(members, array.shape[0] // members, array.shape[1]), teams)
+    return jnp.sum(parts.astype(F32), 0).astype(BF16)
+
+
+def gather_shares(share):
+    devices = lax.axis_size("tok")
+    members = devices // 2
     across = [(index, index ^ 1) for index in range(devices)]
     teams = [list(range(odd, devices, 2)) for odd in range(2)]
-    total, channels = array.shape
-    share = total // devices
-    halves = array.reshape(2, total // 2, channels)
-    theirs = lax.ppermute(lax.dynamic_index_in_dim(halves, 1 - parity, 0, False), "tok", across)
-    mine = lax.dynamic_index_in_dim(halves, parity, 0, False)
-    mine = (mine.astype(F32) + theirs.astype(F32)).astype(BF16)
-    parts = swap(mine.reshape(devices // 2, share, channels), teams)
-    summed = jnp.sum(parts.astype(F32), 0).astype(BF16)
-    copies = jnp.broadcast_to(summed[None], (devices // 2, share, channels))
-    mine = swap(copies, teams).reshape(total // 2, channels)
+    mine = swap(jnp.broadcast_to(share[None], (members,) + share.shape), teams)
+    mine = mine.reshape(members * share.shape[0], share.shape[1])
     theirs = lax.ppermute(mine, "tok", across)
-    even = parity == 0
-    summed = jnp.concatenate([jnp.where(even, mine, theirs), jnp.where(even, theirs, mine)], 0)
-    return summed.astype(F32)
+    even = lax.axis_index("tok") % 2 == 0
+    both = jnp.concatenate([jnp.where(even, mine, theirs), jnp.where(even, theirs, mine)], 0)
+    return both.astype(F32)
 
 
 def body(
@@ -477,89 +516,124 @@
     samples, depth = query_states.shape[2:4]
     lanes = heads * layers
     sizes = [row_count]
-    if row_count % 32 == 0:
-        sizes = [row_count // 4, row_count - row_count // 4]
-    starts = [sum(sizes[:index]) for index in range(len(sizes))]
+    if row_count % 16 == 0:
+        sizes = [row_count // 2] * 2
     w_bias = jnp.transpose(weight_bias, (0, 2, 1))
 
     group = lax.axis_index("tok") // heads
     weights = sample_weight(lax.dynamic_slice_in_dim(noise_level, group * samples, samples))
     valid = key_mask[None, :]
 
-    def take_rows(array, start, rows):
-        cut = array[:, 0].reshape(layers, samples, depth, devices, row_count)
-        cut = cut[..., start : start + rows]
-        return cut.reshape(layers, samples, depth, devices * rows)
-
-    arrived = []
-    prepared = None
-    for start, rows in zip(starts, sizes):
-        bias, *made = forward_rows(
-            start, rows, pair_states, weight_in, weight_out, w_bias, prepared
+    def by_chunk(array):
+        cut = array[:, 0].reshape(layers, samples, depth, devices, len(sizes), sizes[0])
+        cut = jnp.transpose(cut, (4, 0, 1, 2, 3, 5))
+        return cut.reshape(len(sizes), layers, samples, depth, devices * sizes[0])
+
+    queries, grads = by_chunk(query_states), by_chunk(output_grad)
+
+    sum_rows = 3 * width + lanes
+    padded_rows = 8 * devices * -(-sum_rows // (8 * devices))
+    parity = (lax.axis_index("tok") % 2).astype(jnp.int32).reshape(1)
+    doubled = jnp.concatenate([jnp.ones((width,), BF16), jnp.full((width,), 2.0, BF16)])
+    scaled = (weight_in * doubled[None, :], weight_out * jnp.asarray(0.5, BF16))
+    rows = sizes[0]
+    direct = is_direct(rows, crop)
+
+    def forward(start, count, prepared, **more):
+        return forward_rows(
+            start, count, pair_states, weight_in, weight_out, w_bias, prepared, **more
         )
-        prepared = prepared or made
-        if is_direct(rows, crop):
+
+    def send_bias(bias):
+        if direct:
             bias = bias.reshape(heads, layers, rows, crop)
         else:
             bias = jnp.transpose(bias.reshape(rows, layers, heads, crop), (2, 1, 0, 3))
         if groups > 1:
             bias = jnp.tile(bias, (groups, 1, 1, 1))
-        arrived.append(swap(bias))
-
-    returned = []
-    d_queries = []
-    state = None
-    for start, rows, bias in zip(starts, sizes, arrived):
-        direct = is_direct(rows, crop)
+        return swap(bias)
+
+    def attend(start, bias, state=None, after=None):
         if not direct:
             bias = jnp.transpose(bias, (1, 0, 2, 3)).reshape(1, layers, devices * rows, crop)
-        d_query, d_key, d_value, d_bias = attend_rows(
+        *grads_made, d_bias = attend_rows(
             start == 0,
             start + rows == row_count,
             weights,
             bias,
             valid,
-            take_rows(query_states, start, rows),
+            queries[start // rows],
             key_states[:, 0],
             value_states[:, 0],
-            take_rows(output_grad, start, rows),
+            grads[start // rows],
             state,
+            after,
         )
-        state = (d_key, d_value)
-        d_queries.append(d_query.reshape(layers, samples, depth, devices, rows))
         if not direct:
             d_bias = jnp.transpose(d_bias.reshape(layers, devices, rows, crop), (1, 0, 2, 3))
-        returned.append(swap(d_bias))
-
-    sum_rows = 3 * width + lanes
-    packed_rows = 8 * devices * -(-sum_rows // (8 * devices))
-    pair_state = None
-    for start, rows, d_bias in zip(starts, sizes, returned):
+        return grads_made, d_bias
+
+    def send_back(d_bias):
+        d_bias = swap(d_bias)
         if groups > 1:
             d_bias = d_bias.reshape(groups, heads, layers, rows, crop).astype(F32)
             d_bias = jnp.sum(d_bias, 0).astype(BF16)
-        if is_direct(rows, crop):
-            d_bias = d_bias.reshape(lanes, rows, crop)
-        else:
-            d_bias = jnp.transpose(d_bias, (2, 1, 0, 3)).reshape(rows, lanes, crop)
-        pair_state = backward_rows(
+        if direct:
+            return d_bias.reshape(lanes, rows, crop)
+        return jnp.transpose(d_bias, (2, 1, 0, 3)).reshape(rows, lanes, crop)
+
+    def backward(start, count, base, d_bias, prepared, state=None):
+        weights_used = (*prepared, *scaled)
+        return backward_rows(
             start,
-            rows,
-            packed_rows,
+            count,
+            base,
+            direct,
+            padded_rows,
             pair_states,
             d_bias,
             w_bias,
+            weights_used,
+            state,
+            parity,
+        )
+
+    bias, *prepared = forward(0, rows, None)
+    bias = send_bias(bias)
+    if len(sizes) == 1:
+        (d_query, d_key, d_value), d_bias = attend(0, bias)
+        d_queries = [d_query]
+        pair_grad, _, keep, send = backward(0, rows, 0, send_back(d_bias), prepared)
+    else:
+        half = rows // 2
+        (lines,) = forward(rows, half, prepared, chunk_rows=rows)
+        (d_query, *state), d_bias = attend(0, bias)
+        d_queries = [d_query]
+        (bias,) = forward(
+            rows + half,
+            half,
             prepared,
-            pair_state and pair_state[:2],
+            base=half,
+            chunk_rows=rows,
+            taken=lines,
+            after=d_bias,
         )
-    pair_grad, _, packed = pair_state
-
-    summed = sum_over_devices(packed)
+        d_bias = send_back(d_bias)
+        bias = send_bias(bias)
+        pair_state = backward(0, half, 0, d_bias, prepared)
+        (d_query, d_key, d_value), d_bias_later = attend(rows, bias, state, pair_state[1])
+        d_queries.append(d_query)
+        d_bias_later = send_back(d_bias_later)
+        pair_state = backward(half, half, half, d_bias, prepared, pair_state)
+        pair_grad, _, keep, send = backward(rows, rows, 0, d_bias_later, prepared, pair_state)
+
+    summed = gather_shares(sum_team(sum_pairs(keep, send)))
     grad_in = summed[: 2 * width].T
     grad_out = summed[2 * width : 3 * width]
     grad_bias = summed[3 * width : sum_rows].reshape(layers, heads, channels)
     grad_bias = jnp.transpose(grad_bias, (0, 2, 1))
 
+    d_queries = [part.reshape(layers, samples, depth, devices, rows) for part in d_queries]
     d_query = jnp.concatenate(d_queries, -1).reshape(query_states.shape)
     return (
         pair_grad,

time: 171 us -> 160 us (0.936)
  local copies, waits for them, and re-layouts: 10.8 us -> 5.41 us
  Pallas kernels: 89.8 us -> 84.9 us
  waiting for transfers between devices: 18.7 us -> 16.6 us
    slice x6 -> x2, local copies, waits for them, and re-layouts: 5.19 us -> 0.07 us  [the longest x1 0.04 us: attend(): queries[start // rows]]
    pallas_call x4 -> x6, Pallas kernels: 81.4 us -> 76.4 us  [the longest x3 51.6 us: backward_rows(): pl.pallas_call(functools.partial(backward_kernel, first, last, direct, ba...]
    all_to_all x4, waiting for transfers between devices: 17.4 us -> 14.8 us  [swap(): lax.all_to_all(array, 'tok', split_axis=0, concat_axis=0, tiled=True, axi...]
    unnamed x18 -> x28, local copies, waits for them, and re-layouts: 2.79 us -> 4.43 us
  transfers between devices with their start and end apart: 6 -> 6, of which waited for: 5 -> 5; matrix products, arithmetic and copies ran while one was open for 5% -> 2% of each run, Pallas kernels for 24% -> 26%
where the time goes in v10:
time: 160 us; the launch traced here: 159 us
  Pallas kernels  84.9 us (53%)
  blocking collectives  24.3 us (15%)
  starting transfers between devices  22.5 us (14%)
  waiting for transfers between devices  16.6 us (10%)
  local copies, waits for them, and re-layouts  5.41 us (3%)
  other arithmetic  4.08 us (3%)
    pallas_call x3, Pallas kernels, backward_rows(): pl.pallas_call(functools.partial(backward_kernel, first, last, direct, ba...  51.6 us
    pallas_call x3, Pallas kernels, forward_rows(): pl.pallas_call(functools.partial(forward_kernel, direct, first, taken is...  24.8 us
    all_to_all x2, blocking collectives, swap(): lax.all_to_all(array, 'tok', split_axis=0, concat_axis=0, tiled=True, axi...  24.3 us
    all_to_all x4, starting transfers between devices, swap(): lax.all_to_all(array, 'tok', split_axis=0, concat_axis=0, tiled=True, axi...  22.5 us
    all_to_all x4, waiting for transfers between devices, swap(): lax.all_to_all(array, 'tok', split_axis=0, concat_axis=0, tiled=True, axi...  14.8 us
    pallas_call x2, Pallas kernels, attend_rows(): pl.pallas_call(functools.partial(attend_kernel, first, last), grid=(layer...  8.57 us
    unnamed x28, local copies, waits for them, and re-layouts  4.43 us
  transfers between devices with their start and end apart: 6, of which 5 were waited for; matrix products, arithmetic and copies ran while one was open for 2% of the time, Pallas kernels for 26%

profile of v10, /device:TPU:0, one launch (start us, length us, event | category | flops | bytes accessed | tf_op | source)
XLA Modules:
  0.0 158.7 jit_solution(14400469890649190861)
XLA Ops:
  0.7 11.2 %pair_forward.3 = (bf16[32,16,512]{2,1,0:T(8,128)(2,1)}, bf16[1024,128]{1,0:T(8,128)(2,1)}, bf16[128,512]{1,0:T(8,128)(2,1)}) custom-call(bf16[32,512,128]{2,1,0:T(8,128)(2,1)} %pair_ref.11, bf16[2,16,128]{2,1,0:T(8,128)(2,1)} %bitcast.60, bf16[128,1024]{1,0:T(8,128)(2,1)} %refs_0_.1, bf16[512,128]{1,0:T(8,128)(2,1)} %refs_1_.1), custom_call_target="tpu_custom_call" | custom-call | flops 9865003008 | bytes 2621440 | tf_op jit(solution)/shard_map/pair_forward/pallas_call | solution.py:204
  11.9 7.5 %all-to-all-start = ((bf16[16,2,16,512]{3,2,1,0:T(8,128)(2,1)}), bf16[16,2,16,512]{3,2,1,0:T(8,128)(2,1)S(1)}, u32[]{:S(2)}, u32[]{:S(2)}) async-start(bf16[16,2,16,512]{3,2,1,0:T(8,128)(2,1)} %bitcast.57), calls=%async_computation | async-start | bytes 1048576 | tf_op jit(solution)/shard_map/all_to_all | solution.py:468
  19.4 0.3 copy.24
  19.9 0.3 copy.25
  20.2 0.1 copy.27.g_ref
  20.4 0.7 broadcast_multiply_fusion.w_back_ref
  21.1 12.7 %all-to-all-done.bias_ref = bf16[16,2,16,512]{3,2,1,0:T(8,128)(2,1)S(1)} async-done(((bf16[16,2,16,512]{3,2,1,0:T(8,128)(2,1)}), bf16[16,2,16,512]{3,2,1,0:T(8,128)(2,1)S(1)}, u32[]{:S(2)}, u32[]{:S(2)}) %all-to-all-start) | async-done | bytes 524320 | tf_op jit(solution)/shard_map/all_to_all | solution.py:468
  33.9 4.3 %attention_backward.2 = (bf16[2,2,48,256]{3,2,1,0:T(8,128)(2,1)S(1)}, f32[2,2,48,512]{3,2,1,0:T(8,128)S(1)}, f32[2,2,48,512]{3,2,1,0:T(8,128)S(1)}, bf16[16,2,16,512]{3,2,1,0:T(8,128)(2,1)}) custom-call(f32[2]{0:T(128)S(1)} %multiply_divide_fusion.weight_ref, bf16[16,2,16,512]{3,2,1,0:T(8,128)(2,1)S(1)} %all-to-all-done.bias_ref, s32[1,512]{1,0:T(1,128)S(1)} %bitcast.41, ...), custom_call_target="tpu_custom_call" | custom-call | flops 5033164800 | bytes 2228224 | tf_op jit(solution)/shard_map/attention_backward/pallas_call | solution.py:446
  38.2 4.1 %all-to-all-start.2 = ((bf16[16,2,16,512]{3,2,1,0:T(8,128)(2,1)}), bf16[16,2,16,512]{3,2,1,0:T(8,128)(2,1)S(1)}, u32[]{:S(2)}, u32[]{:S(2)}) async-start(bf16[16,2,16,512]{3,2,1,0:T(8,128)(2,1)} %get-tuple-element.28.refs_3_), calls=%async_computation.2 | async-start | bytes 1048576 | tf_op jit(solution)/shard_map/all_to_all | solution.py:468
  42.3 0.7 broadcast_multiply_fusion.1.w_half_ref
  43.2 6.7 %pair_forward.4.refs_2_ = f32[4,512,128]{2,1,0:T(8,128)} custom-call(bf16[32,512,128]{2,1,0:T(8,128)(2,1)} %pair_ref.11, bf16[2,16,128]{2,1,0:T(8,128)(2,1)} %bitcast.61, bf16[1024,128]{1,0:T(8,128)(2,1)} %get-tuple-element.25.refs_0_.w_in_t_ref, bf16[128,512]{1,0:T(8,128)(2,1)} %get-tuple-element.26.refs_1_.w_out_t_ref), custom_call_target="tpu_custom_call" | custom-call | flops 4932501504 | bytes 1310720 | tf_op jit(solution)/shard_map/pair_forward/pallas_call | solution.py:204
  49.9 7.0 %pair_forward.5 = bf16[32,16,512]{2,1,0:T(8,128)(2,1)} custom-call(bf16[32,512,128]{2,1,0:T(8,128)(2,1)} %pair_ref.11, bf16[2,16,128]{2,1,0:T(8,128)(2,1)} %bitcast.62, bf16[1024,128]{1,0:T(8,128)(2,1)} %get-tuple-element.25.refs_0_.w_in_t_ref, bf16[128,512]{1,0:T(8,128)(2,1)} %get-tuple-element.26.refs_1_.w_out_t_ref, f32[4,512,128]{2,1,0:T(8,128)} %pair_forward.4.refs_2_, ...), custom_call_target="tpu_custom_call" | custom-call | flops 4932501504 | bytes 1310720 | tf_op jit(solution)/shard_map/pair_forward/pallas_call | solution.py:204
  56.9 6.0 %all-to-all-start.1 = ((bf16[16,2,16,512]{3,2,1,0:T(8,128)(2,1)}), bf16[16,2,16,512]{3,2,1,0:T(8,128)(2,1)S(1)}, u32[]{:S(2)}, u32[]{:S(2)}) async-start(bf16[16,2,16,512]{3,2,1,0:T(8,128)(2,1)} %bitcast.58), calls=%async_computation.1 | async-start | bytes 1048576 | tf_op jit(solution)/shard_map/all_to_all | solution.py:468
  62.9 13.3 %pair_backward.3 = (bf16[32,512,128]{2,1,0:T(8,128)(2,1)}, f32[1664,128]{1,0:T(8,128)}) custom-call(bf16[32,512,128]{2,1,0:T(8,128)(2,1)} %pair_ref.11, bf16[32,16,512]{2,1,0:T(8,128)(2,1)} %bitcast.54, bf16[2,16,128]{2,1,0:T(8,128)(2,1)} %bitcast.63, bf16[1024,128]{1,0:T(8,128)(2,1)} %get-tuple-element.25.refs_0_.w_in_t_ref, ...), custom_call_target="tpu_custom_call" | custom-call | flops 14696841216 | bytes 2359296 | tf_op jit(solution)/shard_map/pair_backward/pallas_call | solution.py:368
  76.2 1.2 all-to-all-done.1.bias_ref
  77.4 1.2 copy-done.3
  78.5 4.3 %attention_backward.3 = (bf16[2,2,48,256]{3,2,1,0:T(8,128)(2,1)S(1)}, bf16[2,2,48,512]{3,2,1,0:T(8,128)(2,1)}, bf16[2,2,48,512]{3,2,1,0:T(8,128)(2,1)}, bf16[16,2,16,512]{3,2,1,0:T(8,128)(2,1)}) custom-call(f32[2]{0:T(128)S(1)} %multiply_divide_fusion.weight_ref, bf16[16,2,16,512]{3,2,1,0:T(8,128)(2,1)S(1)} %all-to-all-done.1.bias_ref, ...), custom_call_target="tpu_custom_call" | custom-call | flops 5033164800 | bytes 2228224 | tf_op jit(solution)/shard_map/attention_backward/pallas_call | solution.py:446
  82.8 4.8 %all-to-all-start.3 = ((bf16[16,2,16,512]{3,2,1,0:T(8,128)(2,1)}), bf16[16,2,16,512]{3,2,1,0:T(8,128)(2,1)S(1)}, u32[]{:S(2)}, u32[]{:S(2)}) async-start(bf16[16,2,16,512]{3,2,1,0:T(8,128)(2,1)} %get-tuple-element.32), calls=%async_computation.3 | async-start | bytes 1048576 | tf_op jit(solution)/shard_map/all_to_all | solution.py:468
  87.6 13.6 %pair_backward.4 = (bf16[32,512,128]{2,1,0:T(8,128)(2,1)}, f32[1664,128]{1,0:T(8,128)}) custom-call(bf16[32,512,128]{2,1,0:T(8,128)(2,1)} %pair_ref.11, bf16[32,16,512]{2,1,0:T(8,128)(2,1)} %bitcast.55, bf16[2,16,128]{2,1,0:T(8,128)(2,1)} %bitcast.64, bf16[1024,128]{1,0:T(8,128)(2,1)} %get-tuple-element.25.refs_0_.w_in_t_ref, ...), custom_call_target="tpu_custom_call", output_to_operand_aliasing={{0}: (8, {})} | custom-call | flops 14696841216 | bytes 2359296 | tf_op jit(solution)/shard_map/pair_backward/pallas_call | solution.py:368
  101.2 0.9 all-to-all-done.3
  102.1 0.8 copy-done.5
  102.9 24.7 %pair_backward.5 = (bf16[32,512,128]{2,1,0:T(8,128)(2,1)}, f32[1664,128]{1,0:T(8,128)}, f32[832,128]{1,0:T(8,128)}, bf16[832,128]{1,0:T(8,128)(2,1)}) custom-call(bf16[32,512,128]{2,1,0:T(8,128)(2,1)} %pair_ref.11, bf16[32,16,512]{2,1,0:T(8,128)(2,1)} %bitcast.56, bf16[2,16,128]{2,1,0:T(8,128)(2,1)} %bitcast.65, ...), custom_call_target="tpu_custom_call", output_to_operand_aliasing={{0}: (9, {})} | custom-call | flops 29393682432 | bytes 4718592 | tf_op jit(solution)/shard_map/pair_backward/pallas_call | solution.py:368
  127.6 1.7 %collective-permute-done = bf16[832,128]{1,0:T(8,128)(2,1)S(1)} collective-permute-done((bf16[832,128]{1,0:T(8,128)(2,1)}, bf16[832,128]{1,0:T(8,128)(2,1)S(1)}, u32[]{:S(2)}, u32[]{:S(2)}) %collective-permute-start) | collective-permute-done | bytes 213024 | tf_op jit(solution)/shard_map/ppermute | solution.py:475
  129.3 1.1 add_convert_fusion
  130.4 13.3 %all_to_all.30 = bf16[8,104,128]{2,1,0:T(8,128)(2,1)S(1)} all-to-all(bf16[8,104,128]{2,1,0:T(8,128)(2,1)S(1)} %bitcast.53), channel_id=1, replica_groups={{0,2,4,6,8,10,12,14},{1,3,5,7,9,11,13,15},{16,18,20,22,24,26,28,30},{17..., dimensions={0} | all-to-all | bytes 425984 | tf_op jit(solution)/shard_map/all_to_all | solution.py:468
  143.8 11.0 %all_to_all.31 = bf16[8,104,128]{2,1,0:T(8,128)(2,1)S(1)} all-to-all(bf16[8,104,128]{2,1,0:T(8,128)(2,1)S(1)} %broadcast_in_dim.18), channel_id=1, replica_groups={{0,2,4,6,8,10,12,14},{1,3,5,7,9,11,13,15},{16,18,20,22,24,26,28,30},{17..., dimensions={0} | all-to-all | bytes 425984 | tf_op jit(solution)/shard_map/all_to_all | solution.py:468
  154.7 0.2 copy.30
  154.9 0.2 copy.31
  155.2 0.9 copy.33
  156.3 0.7 maximum_convert_fusion.1
  157.0 0.6 maximum_convert_fusion.2
  157.7 1.0 copy.36
  (38 shorter events, 1.0 us)
Async XLA Ops:
  0.6 18.8 %copy-start.7 = (bf16[2,1,2,48,512]{4,3,2,1,0:T(8,128)(2,1)S(1)}, bf16[2,1,2,48,512]{4,3,2,1,0:T(8,128)(2,1)}, u32[]{:S(2)}) copy-start(bf16[2,1,2,48,512]{4,3,2,1,0:T(8,128)(2,1)} %param.16) | copy-start | bytes 589828
  0.6 19.2 %copy-start.8 = (bf16[2,1,2,48,512]{4,3,2,1,0:T(8,128)(2,1)S(1)}, bf16[2,1,2,48,512]{4,3,2,1,0:T(8,128)(2,1)}, u32[]{:S(2)}) copy-start(bf16[2,1,2,48,512]{4,3,2,1,0:T(8,128)(2,1)} %param.19) | copy-start | bytes 589828
  11.8 8.5 %copy-start.11 = (s32[2]{0:T(128)S(1)}, s32[2]{0:T(128)}, u32[]{:S(2)}) copy-start(s32[2]{0:T(128)} %param.15) | copy-start | bytes 28
  11.8 8.5 %copy-start.6 = (bf16[128,1024]{1,0:T(8,128)(2,1)S(1)}, bf16[128,1024]{1,0:T(8,128)(2,1)}, u32[]{:S(2)}) copy-start(bf16[128,1024]{1,0:T(8,128)(2,1)} %refs_0_.1) | copy-start | bytes 786436
  11.8 8.6 %copy-start.10 = (bf16[1024]{0:T(1024)(128)(2,1)S(1)}, bf16[1024]{0:T(1024)(128)(2,1)}, u32[]{:S(2)}) copy-start(bf16[1024]{0:T(1024)(128)(2,1)} %constant.43.clone.1) | copy-start | bytes 6148
  11.8 22.0 %copy-start = (bf16[2,1,2,48,512]{4,3,2,1,0:T(8,128)(2,1)S(1)}, bf16[2,1,2,48,512]{4,3,2,1,0:T(8,128)(2,1)}, u32[]{:S(2)}) copy-start(bf16[2,1,2,48,512]{4,3,2,1,0:T(8,128)(2,1)} %param.17) | copy-start | bytes 589828
  11.8 22.0 %copy-start.1 = (bf16[2,1,2,48,512]{4,3,2,1,0:T(8,128)(2,1)S(1)}, bf16[2,1,2,48,512]{4,3,2,1,0:T(8,128)(2,1)}, u32[]{:S(2)}) copy-start(bf16[2,1,2,48,512]{4,3,2,1,0:T(8,128)(2,1)} %param.18) | copy-start | bytes 589828
  11.8 22.0 %copy-start.2 = (s32[512]{0:T(512)S(1)}, s32[512]{0:T(512)}, u32[]{:S(2)}) copy-start(s32[512]{0:T(512)} %param.14) | copy-start | bytes 6148
  11.9 22.0 %all-to-all-start = ((bf16[16,2,16,512]{3,2,1,0:T(8,128)(2,1)}), bf16[16,2,16,512]{3,2,1,0:T(8,128)(2,1)S(1)}, u32[]{:S(2)}, u32[]{:S(2)}) async-start(bf16[16,2,16,512]{3,2,1,0:T(8,128)(2,1)} %bitcast.57), calls=%async_computation | async-start | bytes 1048576 | tf_op jit(solution)/shard_map/all_to_all | solution.py:468
  33.9 8.4 %copy-start.9 = (bf16[512,128]{1,0:T(8,128)(2,1)S(1)}, bf16[512,128]{1,0:T(8,128)(2,1)}, u32[]{:S(2)}) copy-start(bf16[512,128]{1,0:T(8,128)(2,1)} %refs_1_.1) | copy-start | bytes 393220
  38.2 18.7 %all-to-all-start.2 = ((bf16[16,2,16,512]{3,2,1,0:T(8,128)(2,1)}), bf16[16,2,16,512]{3,2,1,0:T(8,128)(2,1)S(1)}, u32[]{:S(2)}, u32[]{:S(2)}) async-start(bf16[16,2,16,512]{3,2,1,0:T(8,128)(2,1)} %get-tuple-element.28.refs_3_), calls=%async_computation.2 | async-start | bytes 1048576 | tf_op jit(solution)/shard_map/all_to_all | solution.py:468
  56.9 6.0 %copy-start.4 = (bf16[16,2,16,512]{3,2,1,0:T(8,128)(2,1)}, bf16[16,2,16,512]{3,2,1,0:T(8,128)(2,1)S(1)}, u32[]{:S(2)}) copy-start(bf16[16,2,16,512]{3,2,1,0:T(8,128)(2,1)S(1)} %all-to-all-done.2) | copy-start | bytes 1572868
  56.9 20.5 %all-to-all-start.1 = ((bf16[16,2,16,512]{3,2,1,0:T(8,128)(2,1)}), bf16[16,2,16,512]{3,2,1,0:T(8,128)(2,1)S(1)}, u32[]{:S(2)}, u32[]{:S(2)}) async-start(bf16[16,2,16,512]{3,2,1,0:T(8,128)(2,1)} %bitcast.58), calls=%async_computation.1 | async-start | bytes 1048576 | tf_op jit(solution)/shard_map/all_to_all | solution.py:468
  77.4 1.2 copy-start.3
  82.8 19.3 %all-to-all-start.3 = ((bf16[16,2,16,512]{3,2,1,0:T(8,128)(2,1)}), bf16[16,2,16,512]{3,2,1,0:T(8,128)(2,1)S(1)}, u32[]{:S(2)}, u32[]{:S(2)}) async-start(bf16[16,2,16,512]{3,2,1,0:T(8,128)(2,1)} %get-tuple-element.32), calls=%async_computation.3 | async-start | bytes 1048576 | tf_op jit(solution)/shard_map/all_to_all | solution.py:468
  102.1 0.8 copy-start.5
  127.6 1.7 %collective-permute-start = (bf16[832,128]{1,0:T(8,128)(2,1)}, bf16[832,128]{1,0:T(8,128)(2,1)S(1)}, u32[]{:S(2)}, u32[]{:S(2)}) collective-permute-start(bf16[832,128]{1,0:T(8,128)(2,1)} %get-tuple-element.42), channel_id=1, source_target_pairs={{0,1},{1,0},{2,3},{3,2},{4,5},{5,4},{6,7},{7,6},{8,9},{9,8},{10,11... | collective-permute-start | bytes 638984 | tf_op jit(solution)/shard_map/ppermute | solution.py:475
  154.7 1.5 collective-permute-start.1
